TPU v7x, 128 devices: a whole 4x4x4 slice. The times are simulated.
128 devices in a mesh: front: 8 (over y, core), row: 4 (over x), col: 4 (over z).
Axes of the slice: x: 4, y: 4, z: 4, core: 2. Of those that a mesh axis runs over, the one named last changes fastest.
Arguments:
- parent_front: float32 [8, 2, 3072, 3072], P('front', None, 'row', 'col'), may hold values from -6 to 6
- child_left: bfloat16 [3584, 256, 256], P(('front', 'row', 'col')), may hold values from -0.375 to 0.375
- child_right: bfloat16 [3584, 256, 256], P(('front', 'row', 'col')), may hold values from -6 to 6
- tile_ranks: int32 [3584], P(('front', 'row', 'col')), may hold values from 1 to 128, as said below
- destination: int32 [3584], P(('front', 'row', 'col')), may hold values from 0 to 31, as said below
- tile_place: int32 [3584], P(('front', 'row', 'col')), may hold values from 0 to 8
- row_source: int32 [3584, 256], P(('front', 'row', 'col')), may hold values from 0 to 255, each once within a row
- col_source: int32 [3584, 256], P(('front', 'row', 'col')), may hold values from 0 to 255, each once within a row
- own_left: bfloat16 [512, 256, 256], P(('front', 'row', 'col')), may hold values from -0.375 to 0.375
- own_right: bfloat16 [512, 256, 256], P(('front', 'row', 'col')), may hold values from -6 to 6
- own_place: int32 [512], P(('front', 'row', 'col')), may hold values from 0 to 8
- pivot_inverse: float32 [8, 3, 2, 256, 256], P('front'), may hold values from -0.01171875 to 0.01171875
Outputs:
- factored: float32 [8, 2, 3072, 3072], P('front', None, 'row', 'col')
Inputs may be any that keep to these rules, and one draw needn't show every extreme that they name: `tile_ranks`: every device's tiles include one of rank 128. A destination d means front d // (row axis size) and row d mod (row axis size) in the sender's own column. No device sends more than 2 tiles to one destination; in every column one destination receives exactly 2 tiles from every device of that column.
All inputs are finite; a program needn't handle non-finite values.
Results may differ from a plain program's by a relative error of at most 0.0003.
Values may be sent and summed in bfloat16 or wider, within the bound.
No kernel may reach another device: no remote copies, remote signals or barrier semaphores. Data moves between devices by JAX's collectives and lax.ppermute only.
A program may use at most 192 MiB of HBM per device.

v0:
```python
import math

import jax
import jax.numpy as jnp
from jax import lax
from jax.sharding import PartitionSpec as P

TILE = 256
RANK = 128
CAP = 2
TS = 3
PANELS = 3


def from_root(block, axis, owner):
    block = jnp.where(lax.axis_index(axis) == owner, block, jnp.zeros_like(block))
    return lax.psum(block, axis)


def complex_mult(left, right):
    highest = lax.Precision.HIGHEST
    real_part = jnp.dot(left[0], right[0], precision=highest) - jnp.dot(
        left[1], right[1], precision=highest
    )
    imag_part = jnp.dot(left[0], right[1], precision=highest) + jnp.dot(
        left[1], right[0], precision=highest
    )
    return jnp.stack([real_part, imag_part])


def pick_rows(block, chosen):
    return block[chosen]


def extend_add(front_tiles, factor_left, factor_right, places):
    item_count = factor_left.shape[0]
    block_size = math.gcd(item_count, 8)
    targets = jnp.arange(front_tiles.shape[0]).astype(jnp.float32)

    def add_block(block_index, running):
        first_slot = block_index * block_size
        left_block = lax.dynamic_slice_in_dim(factor_left, first_slot, block_size, 0)
        right_block = lax.dynamic_slice_in_dim(factor_right, first_slot, block_size, 0)
        place_block = lax.dynamic_slice_in_dim(places, first_slot, block_size, 0)
        real_side = jnp.concatenate([right_block[..., :RANK], -right_block[..., RANK:]], -1)
        imag_side = jnp.concatenate([right_block[..., RANK:], right_block[..., :RANK]], -1)
        both_sides = jnp.stack([real_side, imag_side], 1)
        update = jnp.einsum(
            "skq,sclq->sckl", left_block, both_sides, preferred_element_type=jnp.float32
        )
        onehot = (place_block.astype(jnp.float32)[:, None] == targets[None, :]).astype(jnp.float32)
        return running + jnp.einsum(
            "st,sckl->tckl", onehot, update, precision=lax.Precision.HIGHEST
        )

    return lax.fori_loop(0, item_count // block_size, add_block, front_tiles)


def body(
    parent_front,
    child_left,
    child_right,
    tile_ranks,
    destination,
    tile_place,
    row_source,
    col_source,
    own_left,
    own_right,
    own_place,
    pivot_inverse,
):
    width_index = jnp.arange(2 * RANK) % RANK
    keep = (width_index[None, :] < tile_ranks[:, None]).astype(jnp.bfloat16)
    masked = child_left * keep[:, None, :]
    left_ready = jax.vmap(pick_rows)(masked, row_source)
    right_ready = jax.vmap(pick_rows)(child_right, col_source)
    tile_count = destination.shape[0]
    fronts_here = lax.axis_size("front")
    rows_here = lax.axis_size("row")
    slot_count = fronts_here * rows_here * CAP
    positions = jnp.arange(tile_count)
    earlier = jnp.sum(
        (destination[:, None] == destination[None, :]) & (positions[None, :] < positions[:, None]),
        1,
    )
    slot_of = destination * CAP + earlier
    matches = slot_of[None, :] == jnp.arange(slot_count)[:, None]
    filled = jnp.any(matches, 1)
    source_index = jnp.sum(jnp.where(matches, positions[None, :], 0), 1)
    zero_value = jnp.zeros((), jnp.bfloat16)
    left_slots = jnp.where(filled[:, None, None], left_ready[source_index], zero_value)
    right_slots = jnp.where(filled[:, None, None], right_ready[source_index], zero_value)
    place_slots = jnp.where(filled, tile_place[source_index], -1).astype(jnp.bfloat16)
    block_here = parent_front[0]
    front_tiles = (
        block_here.reshape(2, TS, TILE, TS, TILE)
        .transpose(1, 3, 0, 2, 4)
        .reshape(TS * TS, 2, TILE, TILE)
    )
    front_tiles = extend_add(front_tiles, own_left, own_right, own_place)
    arrived = (
        lax.all_to_all(left_slots, ("front", "row"), split_axis=0, concat_axis=0, tiled=True),
        lax.all_to_all(right_slots, ("front", "row"), split_axis=0, concat_axis=0, tiled=True),
        lax.all_to_all(place_slots, ("front", "row"), split_axis=0, concat_axis=0, tiled=True),
    )
    front_tiles = extend_add(front_tiles, arrived[0], arrived[1], arrived[2])
    current = (
        front_tiles.reshape(TS, TS, 2, TILE, TILE)
        .transpose(2, 0, 3, 1, 4)
        .reshape(2, TS * TILE, TS * TILE)
    )
    rows_local = current.shape[1]
    cols_local = current.shape[2]
    global_rows = lax.axis_index("row") * rows_local + jnp.arange(rows_local)
    global_cols = lax.axis_index("col") * cols_local + jnp.arange(cols_local)
    first_column = lax.axis_index("col") == 0
    for panel in range(PANELS):
        first_col = panel * TILE
        end_col = first_col + TILE
        inverse = pivot_inverse[0, panel]

        def compute_factor(matrix):
            return complex_mult(matrix[:, :, first_col:end_col], inverse)

        def empty_factor(matrix):
            return jnp.zeros((2, matrix.shape[1], TILE), jnp.float32)

        factor = lax.cond(first_column, compute_factor, empty_factor, current)
        factor = from_root(factor, "col", 0)
        pivot_block = from_root(current[:, first_col:end_col, :], "row", 0)
        under_rows = global_rows >= end_col
        right_cols = global_cols >= end_col
        product = complex_mult(factor, pivot_block)
        trailing = (under_rows[:, None] & right_cols[None, :])[None]
        current = jnp.where(trailing, current - product, current)
        replace_rows = (under_rows & first_column)[None, :, None]
        new_columns = jnp.where(replace_rows, factor, current[:, :, first_col:end_col])
        current = current.at[:, :, first_col:end_col].set(new_columns)
    return current[None]


def solution(mesh):
    return jax.shard_map(
        body,
        mesh=mesh,
        in_specs=(
            P("front", None, "row", "col"),
            P(("front", "row", "col"), None, None),
            P(("front", "row", "col"), None, None),
            P(("front", "row", "col")),
            P(("front", "row", "col")),
            P(("front", "row", "col")),
            P(("front", "row", "col"), None),
            P(("front", "row", "col"), None),
            P(("front", "row", "col"), None, None),
            P(("front", "row", "col"), None, None),
            P(("front", "row", "col")),
            P("front", None, None, None, None),
        ),
        out_specs=P("front", None, "row", "col"),
        check_vma=False,
    )
```

profile of v0, /device:TPU:34, one launch (start us, length us, event | category | flops | bytes accessed | tf_op | source)
XLA Modules:
  0.0 1085.2 jit_solution(12751610533734463071)
XLA Ops:
  10.5 7.6 all-to-all-start
  23.8 125.2 %gather_fusion.4 = bf16[7168,256]{1,0:T(8,128)(2,1)} fusion(bf16[28,256,256]{2,1,0:T(8,128)(2,1)} %broadcast_multiply_fusion, s32[7168]{0:T(1024)S(1)} %reshape.343), kind=kCustom, calls=%fused_computation.4 | custom fusion | bytes 7397376 | tf_op jit(solution)/shard_map/vmap()/gather | solution.py:32
  156.5 125.4 %gather_fusion.3 = bf16[7168,256]{1,0:T(8,128)(2,1)} fusion(bf16[28,256,256]{2,1,0:T(8,128)(2,1)} %param.28, s32[7168]{0:T(1024)S(1)} %reshape.337), kind=kCustom, calls=%fused_computation.3 | custom fusion | bytes 7397376 | tf_op jit(solution)/shard_map/vmap()/gather | solution.py:32
  289.4 11.5 %broadcast_select_fusion = (bf16[64,256,256]{2,1,0:T(8,128)(2,1)}, bf16[64,256,256]{2,1,0:T(8,128)(2,1)}) fusion(bf16[64,256,256]{2,1,0:T(8,128)(2,1)} %gather_fusion.2, pred[64]{0:T(512)(128)(4,1)S(1)} %fusion.95, bf16[64,256,256]{2,1,0:T(8,128)(2,1)} %gather_fusion.1), kind=kLoop, calls=%fused_computation.95 | loop fusion | flops 8388608 | bytes 33554496 | tf_op jit(solution)/shard_map/jit(_where)/select_n | solution.py:92
  300.9 100.8 %all_to_all.19 = bf16[64,256,256]{2,1,0:T(8,128)(2,1)} all-to-all(bf16[64,256,256]{2,1,0:T(8,128)(2,1)} %get-tuple-element.238), channel_id=1, replica_groups=mesh['front'=8,'row'=4,'col'=4] {'front','row'}, dimensions={0} | all-to-all | bytes 16777216 | tf_op jit(solution)/shard_map/all_to_all | solution.py:104
  413.3 8.1 reshape_squeeze.3
  427.2 10.4 copy_add_fusion
  437.8 68.4 %all-to-all-done.2 = bf16[64,256,256]{2,1,0:T(8,128)(2,1)} async-done(((bf16[64,256,256]{2,1,0:T(8,128)(2,1)}), bf16[64,256,256]{2,1,0:T(8,128)(2,1)}, u32[]{:S(2)}, u32[]{:S(2)}) %all-to-all-start.2) | async-done | bytes 8388640 | tf_op jit(solution)/shard_map/all_to_all | solution.py:103
  506.1 177.7 %while.22 = (s32[]{:T(128)}, f32[9,2,256,256]{3,0,2,1:T(8,128)}, bf16[64]{0:T(256)(128)(2,1)S(1)}, bf16[64,256,256]{2,1,0:T(8,128)(2,1)}, bf16[64,256,256]{2,1,0...) while((s32[]{:T(128)}, f32[9,2,256,256]{3,0,2,1:T(8,128)}, ...), condition=%wide.region_4.5_spmd.clone, body=%wide.region_3.4_spmd.clone.sunk | while | flops 657326144 | bytes 35651912 | solution.py:56
  517.4 10.9 %convolution_add_fusion.5 = f32[9,2,256,256]{3,0,2,1:T(8,128)} fusion(f32[9,2,256,256]{3,0,2,1:T(8,128)} %get-tuple-element.295, f32[8,2,256,256]{3,0,2,1:T(8,128)} %copy.43, f32[9]{0:T(128)S(1)} %iota_convert_fusion.3, f32[8]{0:T(128)S(1)} %dynamic-slice_convert_fusion.2), kind=kOutput, calls=%fused_computation.75.clone.1 | convolution fusion | flops 114425928 | bytes 13631556 | tf_op jit(solution)/shard_map/while/body/eval_jaxpr/st,sckl->tckl/dot_general | solution.py:52
  539.6 10.9 %convolution_add_fusion.5 = f32[9,2,256,256]{3,0,2,1:T(8,128)} fusion(f32[9,2,256,256]{3,0,2,1:T(8,128)} %get-tuple-element.295, f32[8,2,256,256]{3,0,2,1:T(8,128)} %copy.43, f32[9]{0:T(128)S(1)} %iota_convert_fusion.3, f32[8]{0:T(128)S(1)} %dynamic-slice_convert_fusion.2), kind=kOutput, calls=%fused_computation.75.clone.1 | convolution fusion | flops 114425928 | bytes 13631556 | tf_op jit(solution)/shard_map/while/body/eval_jaxpr/st,sckl->tckl/dot_general | solution.py:52
  561.8 10.9 %convolution_add_fusion.5 = f32[9,2,256,256]{3,0,2,1:T(8,128)} fusion(f32[9,2,256,256]{3,0,2,1:T(8,128)} %get-tuple-element.295, f32[8,2,256,256]{3,0,2,1:T(8,128)} %copy.43, f32[9]{0:T(128)S(1)} %iota_convert_fusion.3, f32[8]{0:T(128)S(1)} %dynamic-slice_convert_fusion.2), kind=kOutput, calls=%fused_computation.75.clone.1 | convolution fusion | flops 114425928 | bytes 13631556 | tf_op jit(solution)/shard_map/while/body/eval_jaxpr/st,sckl->tckl/dot_general | solution.py:52
  584.0 10.9 %convolution_add_fusion.5 = f32[9,2,256,256]{3,0,2,1:T(8,128)} fusion(f32[9,2,256,256]{3,0,2,1:T(8,128)} %get-tuple-element.295, f32[8,2,256,256]{3,0,2,1:T(8,128)} %copy.43, f32[9]{0:T(128)S(1)} %iota_convert_fusion.3, f32[8]{0:T(128)S(1)} %dynamic-slice_convert_fusion.2), kind=kOutput, calls=%fused_computation.75.clone.1 | convolution fusion | flops 114425928 | bytes 13631556 | tf_op jit(solution)/shard_map/while/body/eval_jaxpr/st,sckl->tckl/dot_general | solution.py:52
  606.2 10.9 %convolution_add_fusion.5 = f32[9,2,256,256]{3,0,2,1:T(8,128)} fusion(f32[9,2,256,256]{3,0,2,1:T(8,128)} %get-tuple-element.295, f32[8,2,256,256]{3,0,2,1:T(8,128)} %copy.43, f32[9]{0:T(128)S(1)} %iota_convert_fusion.3, f32[8]{0:T(128)S(1)} %dynamic-slice_convert_fusion.2), kind=kOutput, calls=%fused_computation.75.clone.1 | convolution fusion | flops 114425928 | bytes 13631556 | tf_op jit(solution)/shard_map/while/body/eval_jaxpr/st,sckl->tckl/dot_general | solution.py:52
  628.4 10.9 %convolution_add_fusion.5 = f32[9,2,256,256]{3,0,2,1:T(8,128)} fusion(f32[9,2,256,256]{3,0,2,1:T(8,128)} %get-tuple-element.295, f32[8,2,256,256]{3,0,2,1:T(8,128)} %copy.43, f32[9]{0:T(128)S(1)} %iota_convert_fusion.3, f32[8]{0:T(128)S(1)} %dynamic-slice_convert_fusion.2), kind=kOutput, calls=%fused_computation.75.clone.1 | convolution fusion | flops 114425928 | bytes 13631556 | tf_op jit(solution)/shard_map/while/body/eval_jaxpr/st,sckl->tckl/dot_general | solution.py:52
  650.6 10.9 %convolution_add_fusion.5 = f32[9,2,256,256]{3,0,2,1:T(8,128)} fusion(f32[9,2,256,256]{3,0,2,1:T(8,128)} %get-tuple-element.295, f32[8,2,256,256]{3,0,2,1:T(8,128)} %copy.43, f32[9]{0:T(128)S(1)} %iota_convert_fusion.3, f32[8]{0:T(128)S(1)} %dynamic-slice_convert_fusion.2), kind=kOutput, calls=%fused_computation.75.clone.1 | convolution fusion | flops 114425928 | bytes 13631556 | tf_op jit(solution)/shard_map/while/body/eval_jaxpr/st,sckl->tckl/dot_general | solution.py:52
  672.8 10.9 %convolution_add_fusion.5 = f32[9,2,256,256]{3,0,2,1:T(8,128)} fusion(f32[9,2,256,256]{3,0,2,1:T(8,128)} %get-tuple-element.295, f32[8,2,256,256]{3,0,2,1:T(8,128)} %copy.43, f32[9]{0:T(128)S(1)} %iota_convert_fusion.3, f32[8]{0:T(128)S(1)} %dynamic-slice_convert_fusion.2), kind=kOutput, calls=%fused_computation.75.clone.1 | convolution fusion | flops 114425928 | bytes 13631556 | tf_op jit(solution)/shard_map/while/body/eval_jaxpr/st,sckl->tckl/dot_general | solution.py:52
  695.8 8.5 reshape.312
  709.4 53.8 %all-reduce.7.cloned.1.call-done = f32[2,768,256]{2,1,0:T(8,128)} async-done(((f32[2,768,256]{2,1,0:T(8,128)}), f32[2,768,256]{2,1,0:T(8,128)}) %all-reduce.7.cloned.1.call-update) | async-done | bytes 1572880 | tf_op jit(solution)/shard_map/psum | solution.py:17
  763.1 52.8 %all-reduce.9.cloned.1.call-done = f32[2,256,768]{2,1,0:T(8,128)} async-done(((f32[2,256,768]{2,1,0:T(8,128)}), f32[2,256,768]{2,1,0:T(8,128)}) %all-reduce.9.cloned.1.call-update) | async-done | bytes 1572880 | tf_op jit(solution)/shard_map/psum | solution.py:17
  834.5 52.1 %all-reduce.11.cloned.1.call-done = f32[2,768,256]{2,1,0:T(8,128)} async-done(((f32[2,768,256]{2,1,0:T(8,128)}), f32[2,768,256]{2,1,0:T(8,128)}) %all-reduce.11.cloned.1.call-update) | async-done | bytes 1572880 | tf_op jit(solution)/shard_map/psum | solution.py:17
  886.6 52.7 %all-reduce.13.cloned.1.call-done = f32[2,256,768]{2,1,0:T(8,128)} async-done(((f32[2,256,768]{2,1,0:T(8,128)}), f32[2,256,768]{2,1,0:T(8,128)}) %all-reduce.13.cloned.1.call-update) | async-done | bytes 1572880 | tf_op jit(solution)/shard_map/psum | solution.py:17
  957.8 52.1 %all-reduce.15.cloned.1.call-done = f32[2,768,256]{2,1,0:T(8,128)} async-done(((f32[2,768,256]{2,1,0:T(8,128)}), f32[2,768,256]{2,1,0:T(8,128)}) %all-reduce.15.cloned.1.call-update) | async-done | bytes 1572880 | tf_op jit(solution)/shard_map/psum | solution.py:17
  1009.8 52.7 %all-reduce.17.cloned.1.call-done = f32[2,256,768]{2,1,0:T(8,128)} async-done(((f32[2,256,768]{2,1,0:T(8,128)}), f32[2,256,768]{2,1,0:T(8,128)}) %all-reduce.17.cloned.1.call-update) | async-done | bytes 1572880 | tf_op jit(solution)/shard_map/psum | solution.py:17
  (175 shorter events, 201.9 us)
Async XLA Ops:
  6.5 402.9 %copy-start = (bf16[4,256,256]{2,1,0:T(8,128)(2,1)S(1)}, bf16[4,256,256]{2,1,0:T(8,128)(2,1)}, u32[]{:S(2)}) copy-start(bf16[4,256,256]{2,1,0:T(8,128)(2,1)} %param.34) | copy-start | bytes 1572868
  10.5 290.4 %all-to-all-start = ((bf16[32,2,1]{1,2,0:T(2,128)(2,1)}), bf16[32,2,1]{1,2,0:T(2,128)(2,1)S(1)}, u32[]{:S(2)}, u32[]{:S(2)}) async-start(bf16[32,2,1]{1,2,0:T(2,128)(2,1)} %convert_element_type.66), calls=%async_computation | async-start | bytes 32768 | tf_op jit(solution)/shard_map/all_to_all | solution.py:105
  149.0 7.5 copy-start.12
  401.6 7.6 copy-start.11
  401.6 104.5 %all-to-all-start.2 = ((bf16[64,256,256]{2,1,0:T(8,128)(2,1)}), bf16[64,256,256]{2,1,0:T(8,128)(2,1)}, u32[]{:S(2)}, u32[]{:S(2)}) async-start(bf16[64,256,256]{2,1,0:T(8,128)(2,1)} %get-tuple-element.237), calls=%async_computation.2 | async-start | bytes 16777216 | tf_op jit(solution)/shard_map/all_to_all | solution.py:103
  409.0 354.2 %all-reduce.7.cloned.1.call-start = ((), (), s32[]{:S(2)}) async-start(), calls=%async_computation.3 | async-start | bytes 3145728 | tf_op jit(solution)/shard_map/psum | solution.py:17
  421.4 5.8 copy-start.13
  695.8 8.5 copy-start.7
  705.7 110.2 %all-reduce.9.cloned.1.call-start = ((), (), s32[]{:S(2)}) async-start(), calls=%async_computation.4 | async-start | bytes 3145728 | tf_op jit(solution)/shard_map/psum | solution.py:17
  708.5 178.0 %all-reduce.11.cloned.1.call-start = ((), (), s32[]{:S(2)}) async-start(), calls=%async_computation.5 | async-start | bytes 3145728 | tf_op jit(solution)/shard_map/psum | solution.py:17
  763.1 56.5 %copy-start.4 = (f32[2,768,256]{2,1,0:T(8,128)S(1)}, f32[2,768,256]{2,1,0:T(8,128)}, u32[]{:S(2)}) copy-start(f32[2,768,256]{2,1,0:T(8,128)} %all-reduce.7.cloned.1.call-done) | copy-start | bytes 4718596
  819.7 6.8 slice-start.4
  821.9 4.6 slice-start.5
  831.3 107.9 %all-reduce.13.cloned.1.call-start = ((), (), s32[]{:S(2)}) async-start(), calls=%async_computation.6 | async-start | bytes 3145728 | tf_op jit(solution)/shard_map/psum | solution.py:17
  834.1 175.8 %all-reduce.15.cloned.1.call-start = ((), (), s32[]{:S(2)}) async-start(), calls=%async_computation.7 | async-start | bytes 3145728 | tf_op jit(solution)/shard_map/psum | solution.py:17
  886.5 56.4 %copy-start.6 = (f32[2,768,256]{2,1,0:T(8,128)S(1)}, f32[2,768,256]{2,1,0:T(8,128)}, u32[]{:S(2)}) copy-start(f32[2,768,256]{2,1,0:T(8,128)} %all-reduce.11.cloned.1.call-done) | copy-start | bytes 4718596
  942.9 6.8 slice-start.2
  945.1 4.6 slice-start.3
  954.6 107.9 %all-reduce.17.cloned.1.call-start = ((), (), s32[]{:S(2)}) async-start(), calls=%async_computation.8 | async-start | bytes 3145728 | tf_op jit(solution)/shard_map/psum | solution.py:17
  1009.8 56.4 %copy-start.5 = (f32[2,768,256]{2,1,0:T(8,128)S(1)}, f32[2,768,256]{2,1,0:T(8,128)}, u32[]{:S(2)}) copy-start(f32[2,768,256]{2,1,0:T(8,128)} %all-reduce.15.cloned.1.call-done) | copy-start | bytes 4718596
  1062.5 3.7 copy-start.10
  1066.2 6.8 slice-start
  1068.4 4.6 slice-start.1
  1073.7 4.4 copy-start.1
  (4 other events, 11.8 us)
Sparse Core Ops, SparseCore 0:
  705.9 57.2 all-reduce.6
  765.5 50.4 all-reduce.8
  831.4 55.1 all-reduce.10
  888.8 50.4 all-reduce.12
  954.7 55.0 all-reduce.14
  1012.0 50.4 all-reduce.16
where the time goes:
time: 1100 us; the launch traced here: 1090 us
  waiting for transfers between devices  385 us (35%)
  local copies, waits for them, and re-layouts  353 us (32%)
  matrix products  162 us (15%)
  blocking collectives  101 us (9%)
  other arithmetic  53.2 us (5%)
  starting transfers between devices  15.8 us (1%)
  between operations  14.3 us (1%)
    psum x6, waiting for transfers between devices, from_root(): return lax.psum(block, axis)  316 us
    gather x4, local copies, waits for them, and re-layouts, pick_rows(): return block[chosen]  251 us
    all_to_all x1, blocking collectives, body(): lax.all_to_all(right_slots, ('front', 'row'), split_axis=0, concat_axis=0...  101 us
    dot_general x9, matrix products, add_block(): jnp.einsum('st,sckl->tckl', onehot, update, precision=lax.Precision.HIGHEST)  97.5 us
    all_to_all x1, waiting for transfers between devices, body(): lax.all_to_all(left_slots, ('front', 'row'), split_axis=0, concat_axis=0,...  68.4 us
    transpose x9, local copies, waits for them, and re-layouts, add_block(): jnp.einsum('skq,sclq->sckl', left_block, both_sides, preferred_element_ty...  46.5 us
    dot_general x9, matrix products, add_block(): jnp.einsum('skq,sclq->sckl', left_block, both_sides, preferred_element_ty...  33.7 us
  transfers between devices with their start and end apart: 8, of which 7 were waited for; matrix products, arithmetic and copies ran while one was open for 30% of the time, Pallas kernels for 0%

commit v1 on v0

v1 whole, which is shorter than its diff:
```python
import functools
import math

import jax
import jax.numpy as jnp
from jax import lax
from jax.experimental import pallas as pl
from jax.experimental.pallas import tpu as pltpu
from jax.sharding import PartitionSpec as P

TILE = 256
RANK = 128
TS = 3
SIDE = TS * TILE
SENT = 28
GROUP = 32
RING = 4
CODE_ROWS = 16
LOG_STEP = math.log(2.0) / 32.0
VMEM_BYTES = 48 * 1024 * 1024
BF16 = jnp.bfloat16
F32 = jnp.float32


def encode(values):
    peak = jnp.maximum(jnp.max(jnp.abs(values), axis=0, keepdims=True), 1e-30)
    code = jnp.ceil(jnp.log(peak * (1.0 / 32700.0)) * (1.0 / LOG_STEP))
    whole = jnp.round(values * jnp.exp(code * -LOG_STEP))
    whole = jnp.clip(whole, -32767.0, 32767.0).astype(jnp.int32)
    code_rows = jnp.broadcast_to(code.astype(jnp.int32), (CODE_ROWS, values.shape[1]))
    return whole.astype(jnp.int16), code_rows.astype(jnp.int16)


def store_piece(ref, piece, values):
    rows = values.shape[0]
    whole, code_rows = encode(values)
    ref[piece, :rows, :] = whole
    ref[piece, rows:, :] = code_rows


def decode(piece_rows, code_rows):
    code = code_rows[:1].astype(jnp.int32).astype(F32)
    return piece_rows.astype(jnp.int32).astype(F32) * jnp.exp(code * LOG_STEP)


def cut(x):
    high = x.astype(BF16)
    return high, (x - high.astype(F32)).astype(BF16)


def dot(a, b):
    return lax.dot_general(a, b, (((1,), (0,)), ((), ())), preferred_element_type=F32)


def dot_cut(a, b):
    return dot(a[0], b[0]) + (dot(a[0], b[1]) + dot(a[1], b[0]))


def complex_dot(a, b):
    a = [cut(x) for x in a]
    b = [cut(x) for x in b]
    return (
        dot_cut(a[0], b[0]) - dot_cut(a[1], b[1]),
        dot_cut(a[0], b[1]) + dot_cut(a[1], b[0]),
    )


def minus(a, b):
    return a[0] - b[0], a[1] - b[1]


def pack_kernel(source, filled, ranks, left, right, rows, cols, out):
    slot = pl.program_id(0)

    @pl.when(filled[slot] == 1)
    def _():
        rank = ranks[source[slot]]
        index = lax.broadcasted_iota(jnp.int32, (TILE, TILE), 0)

        def picked(chosen, block):
            onehot = jnp.where(index == chosen, 1.0, 0.0).astype(BF16)
            return lax.dot_general(
                onehot, block, (((0,), (0,)), ((), ())), preferred_element_type=F32
            )

        width = lax.broadcasted_iota(jnp.int32, (TILE, 2 * RANK), 1)
        width = jnp.where(width >= RANK, width - RANK, width)
        moved = picked(rows[0], left[0])
        out[0, :TILE, :] = jnp.where(width < rank, moved, 0.0).astype(BF16)
        out[0, TILE:, :] = picked(cols[0], right[0]).astype(BF16)


def pack(source, filled, ranks, left, right, rows, cols):
    tile = pl.BlockSpec((1, TILE, 2 * RANK), lambda s, src, fil, rnk: (src[s], 0, 0))
    line = pl.BlockSpec((1, 1, TILE), lambda s, src, fil, rnk: (src[s], 0, 0))
    return pl.pallas_call(
        pack_kernel,
        grid_spec=pltpu.PrefetchScalarGridSpec(
            num_scalar_prefetch=3,
            grid=(GROUP,),
            in_specs=[tile, tile, line, line],
            out_specs=pl.BlockSpec(
                (1, 2 * TILE, 2 * RANK), lambda s, src, fil, rnk: (s, 0, 0)
            ),
        ),
        out_shape=jax.ShapeDtypeStruct((GROUP, 2 * TILE, 2 * RANK), BF16),
        compiler_params=pltpu.CompilerParams(vmem_limit_bytes=VMEM_BYTES),
        cost_estimate=pl.CostEstimate(
            flops=4 * SENT * TILE**3, bytes_accessed=16 * 2**20, transcendentals=0
        ),
    )(source, filled, ranks, left, right, rows, cols)


def add_tile(out, place, left, right):
    real_side = jnp.concatenate([right[:, :RANK], -right[:, RANK:]], 1)
    imag_side = jnp.concatenate([right[:, RANK:], right[:, :RANK]], 1)
    a = place // TS
    rows = pl.ds(pl.multiple_of(a * TILE, TILE), TILE)
    cols = pl.ds(pl.multiple_of((place - a * TS) * TILE, TILE), TILE)
    contract = (((1,), (1,)), ((), ()))
    out[0, rows, cols] += lax.dot_general(left, real_side, contract, preferred_element_type=F32)
    out[1, rows, cols] += lax.dot_general(left, imag_side, contract, preferred_element_type=F32)


def first_kernel(block_of, places, own_places, before, own_left, own_right, slots, out):
    step = pl.program_id(0)

    @pl.when(step == 0)
    def _():
        out[...] = before[...]

        def own_step(j, carry):
            add_tile(out, own_places[j], own_left[j], own_right[j])
            return carry

        lax.fori_loop(0, own_left.shape[0], own_step, 0)

    @pl.when(places[step] >= 0)
    def _():
        add_tile(out, places[step], slots[0, :TILE, :], slots[0, TILE:, :])


def second_kernel(block_of, places, role, before, slots, inverse, out, upper, lower):
    step = pl.program_id(0)

    @pl.when(step == 0)
    def _():
        out[...] = before[...]

    @pl.when(places[step] >= 0)
    def _():
        add_tile(out, places[step], slots[0, :TILE, :], slots[0, TILE:, :])

    @pl.when((step == GROUP - 1) & (role[0] == 0) & (role[1] == 0))
    def _():
        def at(i, j):
            rows, cols = slice(i * TILE, (i + 1) * TILE), slice(j * TILE, (j + 1) * TILE)
            return out[0, rows, cols], out[1, rows, cols]

        def put(i, j, value):
            rows, cols = slice(i * TILE, (i + 1) * TILE), slice(j * TILE, (j + 1) * TILE)
            out[0, rows, cols] = value[0]
            out[1, rows, cols] = value[1]

        for p in range(TS - 1):
            pivot = inverse[p, 0], inverse[p, 1]
            for i in range(p + 1, TS):
                factor = complex_dot(at(i, p), pivot)
                put(i, p, factor)
                for j in range(p + 1, TS):
                    put(i, j, minus(at(i, j), complex_dot(factor, at(p, j))))

        quarter = TILE // RING
        for piece in range(RING):
            part = slice(piece * quarter, (piece + 1) * quarter)
            for ref, tiles in ((upper, ((0, 1), (0, 2), (1, 2))), (lower, ((1, 0), (2, 0), (2, 1)))):
                wide = jnp.concatenate([x[part] for ij in tiles for x in at(*ij)], 1)
                store_piece(ref, piece, wide)


def whole(shape):
    return pl.BlockSpec(shape, lambda *_: (0,) * len(shape))


def slot_spec():
    return pl.BlockSpec((1, 2 * TILE, 2 * RANK), lambda s, blk, *_: (blk[s], 0, 0))


ADD_COST = pl.CostEstimate(
    flops=4 * GROUP * TILE**3, bytes_accessed=20 * 2**20, transcendentals=0
)


def add_first(block_of, places, own_places, before, own_left, own_right, slots):
    return pl.pallas_call(
        first_kernel,
        grid_spec=pltpu.PrefetchScalarGridSpec(
            num_scalar_prefetch=3,
            grid=(GROUP,),
            in_specs=[
                whole(before.shape),
                whole(own_left.shape),
                whole(own_right.shape),
                slot_spec(),
            ],
            out_specs=whole(before.shape),
        ),
        out_shape=jax.ShapeDtypeStruct(before.shape, F32),
        compiler_params=pltpu.CompilerParams(vmem_limit_bytes=VMEM_BYTES),
        cost_estimate=ADD_COST,
    )(block_of, places, own_places, before, own_left, own_right, slots)


def small_shape():
    return (RING, TILE // RING + CODE_ROWS, 2 * TS * TILE)


def add_second(block_of, places, role, before, slots, inverse):
    return pl.pallas_call(
        second_kernel,
        grid_spec=pltpu.PrefetchScalarGridSpec(
            num_scalar_prefetch=3,
            grid=(GROUP,),
            in_specs=[whole(before.shape), slot_spec(), whole(inverse.shape)],
            out_specs=[whole(before.shape), whole(small_shape()), whole(small_shape())],
        ),
        out_shape=[
            jax.ShapeDtypeStruct(before.shape, F32),
            jax.ShapeDtypeStruct(small_shape(), jnp.int16),
            jax.ShapeDtypeStruct(small_shape(), jnp.int16),
        ],
        compiler_params=pltpu.CompilerParams(vmem_limit_bytes=VMEM_BYTES),
        cost_estimate=ADD_COST,
    )(block_of, places, role, before, slots, inverse)


def gather_pieces(refs, place, rows, put):
    own, below, above, far_top, far_bottom = refs
    half = far_top.shape[0]

    def at(shift):
        return (place + shift) & (RING - 1)

    put(at(0) * rows, decode(own[:rows, :], own[rows:, :]))
    put(at(RING - 1) * rows, decode(below[:rows, :], below[rows:, :]))
    put(at(1) * rows, decode(above[:rows, :], above[rows:, :]))
    codes = far_bottom[rows - half :, :]
    put(at(2) * rows, decode(far_top[...], codes))
    put(at(2) * rows + half, decode(far_bottom[: rows - half, :], codes))


def panel_kernel(role, block, inverse, *refs):
    uppers, lowers = refs[:5], refs[5:10]
    out, left_coded, right_coded, held, wide = refs[10:]
    quarter = TILE // RING

    def fill(pieces, place):
        def put(start, values):
            wide[pl.ds(pl.multiple_of(start, 8), values.shape[0]), :] = values

        gather_pieces(pieces, place, quarter, put)

    def small(t):
        first = 2 * t * TILE
        return wide[:, first : first + TILE], wide[:, first + TILE : first + 2 * TILE]

    def pivot(p):
        return inverse[p, 0], inverse[p, 1]

    @pl.when((role[0] > 0) & (role[1] == 0))
    def _():
        pltpu.sync_copy(block, held)
        fill(uppers, role[0])

        def chunk(i, carry):
            rows = pl.ds(pl.multiple_of(i * TILE, TILE), TILE)

            def at(j):
                cols = slice(j * TILE, (j + 1) * TILE)
                return held[0, rows, cols], held[1, rows, cols]

            f0 = complex_dot(at(0), pivot(0))
            f1 = complex_dot(minus(at(1), complex_dot(f0, small(0))), pivot(1))
            a2 = minus(at(2), complex_dot(f0, small(1)))
            a2 = minus(a2, complex_dot(f1, small(2)))
            for j, f in enumerate((f0, f1, complex_dot(a2, pivot(2)))):
                cols = slice(j * TILE, (j + 1) * TILE)
                held[0, rows, cols] = f[0]
                held[1, rows, cols] = f[1]
            return carry

        lax.fori_loop(0, TS, chunk, 0)
        pltpu.sync_copy(held, out)
        part = SIDE // RING

        def code_piece(piece, carry):
            rows = pl.ds(pl.multiple_of(piece * part, 8), part)
            store_piece(
                left_coded, piece, jnp.concatenate([held[0, rows, :], held[1, rows, :]], 1)
            )
            return carry

        lax.fori_loop(0, RING, code_piece, 0)

    @pl.when((role[0] == 0) & (role[1] > 0))
    def _():
        pltpu.sync_copy(block, held)
        fill(lowers, role[1])

        def chunk(j, carry):
            cols = pl.ds(pl.multiple_of(j * TILE, TILE), TILE)

            def at(i):
                rows = slice(i * TILE, (i + 1) * TILE)
                return held[0, rows, cols], held[1, rows, cols]

            p0 = at(0)
            p1 = minus(at(1), complex_dot(small(0), p0))
            p2 = minus(at(2), complex_dot(small(1), p0))
            p2 = minus(p2, complex_dot(small(2), p1))
            for i, p in ((1, p1), (2, p2)):
                rows = slice(i * TILE, (i + 1) * TILE)
                held[0, rows, cols] = p[0]
                held[1, rows, cols] = p[1]
            return carry

        lax.fori_loop(0, TS, chunk, 0)
        pltpu.sync_copy(held, out)
        part = 2 * SIDE // RING
        for piece in range(RING):
            half, start = divmod(piece * part, SIDE)
            store_piece(right_coded, piece, held[half, start : start + part, :])


def left_shape():
    return (RING, SIDE // RING + CODE_ROWS, 2 * SIDE)


def right_shape():
    return (RING, 2 * SIDE // RING + CODE_ROWS, SIDE)


def panel(role, block, inverse, uppers, lowers):
    anywhere = pl.BlockSpec(memory_space=pl.ANY)
    held = pl.BlockSpec(memory_space=pltpu.VMEM)
    return pl.pallas_call(
        panel_kernel,
        in_specs=[pl.BlockSpec(memory_space=pltpu.SMEM), anywhere] + [held] * 11,
        out_specs=[anywhere, held, held],
        out_shape=[
            jax.ShapeDtypeStruct(block.shape, F32),
            jax.ShapeDtypeStruct(left_shape(), jnp.int16),
            jax.ShapeDtypeStruct(right_shape(), jnp.int16),
        ],
        scratch_shapes=[
            pltpu.VMEM(block.shape, F32),
            pltpu.VMEM((TILE, 2 * TS * TILE), F32),
        ],
        input_output_aliases={1: 0},
        compiler_params=pltpu.CompilerParams(vmem_limit_bytes=VMEM_BYTES),
    )(role, block, inverse, *uppers, *lowers)


def trail_kernel(role, block, *refs):
    lefts, rights = refs[:5], refs[5:10]
    out, held, left_high, left_low, right_high, right_low, sem = refs[10:]

    @pl.when((role[0] > 0) & (role[1] > 0))
    def _():
        fetch = pltpu.make_async_copy(block, held, sem)
        fetch.start()

        def into(high, low):
            def put(start, values):
                rows = pl.ds(pl.multiple_of(start, 16), values.shape[0])
                h, l = cut(values)
                high[rows, :] = h
                low[rows, :] = l

            return put

        gather_pieces(lefts, role[1], SIDE // RING, into(left_high, left_low))
        gather_pieces(rights, role[0], 2 * SIDE // RING, into(right_high, right_low))
        fetch.wait()

        def chunk(i, carry):
            rows = pl.ds(pl.multiple_of(i * TILE, TILE), TILE)
            high, low = left_high[rows, :], left_low[rows, :]

            def real_of(x):
                return jnp.concatenate([x[:, :SIDE], -x[:, SIDE:]], 1)

            def imag_of(x):
                return jnp.concatenate([x[:, SIDE:], x[:, :SIDE]], 1)

            for half, form in ((0, real_of), (1, imag_of)):
                h, l = form(high), form(low)
                for j in range(TS):
                    cols = slice(j * TILE, (j + 1) * TILE)
                    b = right_high[:, cols], right_low[:, cols]
                    held[half, rows, cols] -= dot_cut((h, l), b)
            return carry

        lax.fori_loop(0, TS, chunk, 0)
        pltpu.sync_copy(held, out)


def trail(role, block, lefts, rights):
    anywhere = pl.BlockSpec(memory_space=pl.ANY)
    held = pl.BlockSpec(memory_space=pltpu.VMEM)
    return pl.pallas_call(
        trail_kernel,
        in_specs=[pl.BlockSpec(memory_space=pltpu.SMEM), anywhere] + [held] * 10,
        out_specs=anywhere,
        out_shape=jax.ShapeDtypeStruct(block.shape, F32),
        scratch_shapes=[
            pltpu.VMEM(block.shape, F32),
            pltpu.VMEM((SIDE, 2 * SIDE), BF16),
            pltpu.VMEM((SIDE, 2 * SIDE), BF16),
            pltpu.VMEM((2 * SIDE, SIDE), BF16),
            pltpu.VMEM((2 * SIDE, SIDE), BF16),
            pltpu.SemaphoreType.DMA,
        ],
        input_output_aliases={1: 0},
        compiler_params=pltpu.CompilerParams(vmem_limit_bytes=VMEM_BYTES),
    )(role, block, *lefts, *rights)


def spread(pieces, axis):
    got = [lax.ppermute(pieces[d], axis, [(0, d)]) for d in (1, 3, 2)]
    here = lax.axis_index(axis)
    return jnp.where(
        here == 0,
        pieces[0],
        jnp.where(here == 1, got[0], jnp.where(here == 3, got[1], got[2])),
    )


def ring(own, axis, rows):
    up = [(i, (i + 1) % RING) for i in range(RING)]
    down = [(i, (i - 1) % RING) for i in range(RING)]
    half = rows // 2 // 16 * 16
    below = lax.ppermute(own, axis, up)
    above = lax.ppermute(own, axis, down)
    far_top = lax.ppermute(below[:half], axis, up)
    far_bottom = lax.ppermute(above[half:], axis, down)
    return own, below, above, far_top, far_bottom


def body(
    parent_front,
    child_left,
    child_right,
    tile_ranks,
    destination,
    tile_place,
    row_source,
    col_source,
    own_left,
    own_right,
    own_place,
    pivot_inverse,
):
    joined = ("front", "row")
    me = lax.axis_index(joined)
    role = jnp.stack([lax.axis_index("row"), lax.axis_index("col")]).astype(jnp.int32)
    none = 16 * SENT
    numbered = 16 * jnp.arange(SENT, dtype=jnp.int32) + tile_place

    told = lax.all_gather(destination * 16 + tile_place, joined)
    told_place = told & 15
    told_number = 16 * jnp.arange(SENT, dtype=jnp.int32)[None, :] + told_place
    to_me = jnp.where((told >> 4) == me, told_number, none)
    first_in = jnp.min(to_me, 1)
    second_in = jnp.min(jnp.where(to_me > first_in[:, None], to_me, none), 1)

    to_each = jnp.where(
        destination[None, :] == jnp.arange(GROUP, dtype=jnp.int32)[:, None],
        numbered[None, :],
        none,
    )
    first_out = jnp.min(to_each, 1)
    second_out = jnp.min(jnp.where(to_each > first_out[:, None], to_each, none), 1)

    rows = row_source[:, None, :]
    cols = col_source[:, None, :]
    slots = []
    for number in (first_out, second_out):
        filled = (number < none).astype(jnp.int32)
        slots.append(
            pack((number >> 4) * filled, filled, tile_ranks, child_left, child_right, rows, cols)
        )
    first_slots = lax.all_to_all(slots[0], joined, split_axis=0, concat_axis=0, tiled=True)
    second_slots = lax.all_to_all(slots[1], joined, split_axis=0, concat_axis=0, tiled=True)

    def places_of(number):
        filled = number < none
        block_of = jnp.where(filled, jnp.arange(GROUP, dtype=jnp.int32), 0)
        return block_of, jnp.where(filled, number & 15, -1)

    inverse = pivot_inverse[0]
    block = add_first(
        *places_of(first_in), own_place, parent_front[0], own_left, own_right, first_slots
    )
    block, upper, lower = add_second(
        *places_of(second_in), role, block, second_slots, inverse
    )
    uppers = ring(spread(upper, "row"), "row", TILE // RING)
    lowers = ring(spread(lower, "col"), "col", TILE // RING)
    block, left, right = panel(role, block, inverse, uppers, lowers)
    lefts = ring(spread(left, "col"), "col", SIDE // RING)
    rights = ring(spread(right, "row"), "row", 2 * SIDE // RING)
    return trail(role, block, lefts, rights)[None]


def solution(mesh):
    joined = ("front", "row", "col")
    tiles = P(joined, None, None)
    return jax.shard_map(
        body,
        mesh=mesh,
        in_specs=(
            P("front", None, "row", "col"),
            tiles,
            tiles,
            P(joined),
            P(joined),
            P(joined),
            P(joined, None),
            P(joined, None),
            tiles,
            tiles,
            P(joined),
            P("front", None, None, None, None),
        ),
        out_specs=P("front", None, "row", "col"),
        check_vma=False,
    )
```

time: 1100 us -> 426 us (0.39)
  local copies, waits for them, and re-layouts: 353 us -> 11.9 us
  waiting for transfers between devices: 385 us -> 126 us
  matrix products: 162 us -> 0 us
  Pallas kernels: 0 us -> 92.2 us
  starting transfers between devices: 15.8 us -> 76.2 us
  other arithmetic: 53.2 us -> 4.14 us
  between operations: 14.3 us -> 1.3 us
    psum x6 -> x0, waiting for transfers between devices: 316 us -> none  [from_root(): return lax.psum(block, axis)]
    gather x7 -> x0, local copies, waits for them, and re-layouts: 267 us -> none  [the longest x4 251 us: pick_rows(): return block[chosen]]
    dot_general x30 -> x0, matrix products: 162 us -> none  [the longest x9 97.5 us: add_block(): jnp.einsum('st,sckl->tckl', onehot, update, precision=lax.Precision.HIGHEST)]
    unnamed x0 -> x1, blocking collectives: none -> 108 us
    all_to_all x1 -> x0, blocking collectives: 101 us -> none  [body(): lax.all_to_all(right_slots, ('front', 'row'), split_axis=0, concat_axis=0...]
    pallas_call x0 -> x6, Pallas kernels: none -> 92.2 us  [the longest x2 38.2 us: pack(): pl.pallas_call(pack_kernel, grid_spec=pltpu.PrefetchScalarGridSpec(num_sc...]
    ppermute x0 -> x28, starting transfers between devices: none -> 59.8 us  [the longest x4 33.9 us: ring(): above = lax.ppermute(own, axis, down)]
    transpose x11 -> x0, local copies, waits for them, and re-layouts: 58.1 us -> none  [the longest x9 46.5 us: add_block(): jnp.einsum('skq,sclq->sckl', left_block, both_sides, preferred_element_ty...]
  transfers between devices with their start and end apart: 8 -> 30, of which waited for: 7 -> 9; matrix products, arithmetic and copies ran while one was open for 30% -> 1% of each run, Pallas kernels for 0% -> 9%
where the time goes in v1:
time: 426 us; the launch traced here: 420 us
  waiting for transfers between devices  126 us (30%)
  blocking collectives  108 us (25%)
  Pallas kernels  92.2 us (22%)
  starting transfers between devices  76.2 us (18%)
  local copies, waits for them, and re-layouts  11.9 us (3%)
    unnamed x1, blocking collectives  108 us
    all_to_all x1, waiting for transfers between devices, body(): lax.all_to_all(slots[0], joined, split_axis=0, concat_axis=0, tiled=True)  78.9 us
    pallas_call x2, Pallas kernels, pack(): pl.pallas_call(pack_kernel, grid_spec=pltpu.PrefetchScalarGridSpec(num_sc...  38.2 us
    ppermute x4, starting transfers between devices, ring(): above = lax.ppermute(own, axis, down)  33.9 us
    ppermute x12, waiting for transfers between devices, spread(): got = [lax.ppermute(pieces[d], axis, [(0, d)]) for d in (1, 3, 2)]  26.9 us
    pallas_call x1, Pallas kernels, add_first(): pl.pallas_call(first_kernel, grid_spec=pltpu.PrefetchScalarGridSpec(num_s...  20 us
    pallas_call x1, Pallas kernels, trail(): pl.pallas_call(trail_kernel, in_specs=[pl.BlockSpec(memory_space=pltpu.SM...  18.1 us
    pallas_call x1, Pallas kernels, add_second(): pl.pallas_call(second_kernel, grid_spec=pltpu.PrefetchScalarGridSpec(num_...  13.7 us
  transfers between devices with their start and end apart: 30, of which 9 were waited for; matrix products, arithmetic and copies ran while one was open for 1% of the time, Pallas kernels for 9%

profile of v1, /device:TPU:34, one launch (start us, length us, event | category | flops | bytes accessed | tf_op | source)
XLA Modules:
  0.0 420.1 jit_solution(3697503329988031308)
XLA Ops:
  7.7 22.1 %shard_map.118 = bf16[32,512,256]{2,1,0:T(8,128)(2,1)} custom-call(s32[32]{0:T(128)S(1)} %compare_select_fusion.3.source, s32[32]{0:T(128)S(1)} %compare_convert_fusion.1.filled, s32[28]{0:T(128)S(1)} %copy-done.6, bf16[28,256,256]{2,1,0:T(8,128)(2,1)S(1)} %copy-done.1, bf16[28,256,256]{2,1,0:T(8,128)(2,1)} %right.3, ...), custom_call_target="tpu_custom_call" | custom-call | flops 1879048192 | bytes 16777216 | tf_op jit(solution)/shard_map/pallas_call | solution.py:96
  29.8 7.6 %all-to-all-start = ((bf16[32,512,256]{2,1,0:T(8,128)(2,1)}), bf16[32,512,256]{2,1,0:T(8,128)(2,1)}, u32[]{:S(2)}, u32[]{:S(2)}) async-start(bf16[32,512,256]{2,1,0:T(8,128)(2,1)} %shard_map.118), calls=%async_computation | async-start | bytes 16777216 | tf_op jit(solution)/shard_map/all_to_all | solution.py:493
  39.7 16.1 %shard_map.120 = bf16[32,512,256]{2,1,0:T(8,128)(2,1)} custom-call(s32[32]{0:T(128)S(1)} %compare_select_fusion.2.source, s32[32]{0:T(128)S(1)} %compare_convert_fusion.filled, s32[28]{0:T(128)S(1)} %copy-done.7, bf16[28,256,256]{2,1,0:T(8,128)(2,1)S(1)} %copy-done.2, bf16[28,256,256]{2,1,0:T(8,128)(2,1)} %right.3, s32[28,1,256]{2,1,0:T(1,128)S(1)} %broadcast_in_dim.44.rows, ...), custom_call_target="tpu_custom_call" | custom-call | flops 1879048192 | bytes 16777216 | tf_op jit(solution)/shard_map/pallas_call | solution.py:96
  55.8 78.9 %all-to-all-done.slots = bf16[32,512,256]{2,1,0:T(8,128)(2,1)} async-done(((bf16[32,512,256]{2,1,0:T(8,128)(2,1)}), bf16[32,512,256]{2,1,0:T(8,128)(2,1)}, u32[]{:S(2)}, u32[]{:S(2)}) %all-to-all-start) | async-done | bytes 8388640 | tf_op jit(solution)/shard_map/all_to_all | solution.py:493
  134.6 8.8 %all-to-all-start.1 = ((bf16[32,512,256]{2,1,0:T(8,128)(2,1)}), bf16[32,512,256]{2,1,0:T(8,128)(2,1)}, u32[]{:S(2)}, u32[]{:S(2)}) async-start(bf16[32,512,256]{2,1,0:T(8,128)(2,1)} %shard_map.120), calls=%async_computation.1 | async-start | bytes 16777216 | tf_op jit(solution)/shard_map/all_to_all | solution.py:494
  143.5 108.5 %all-reduce = s32[896]{0:T(1024)S(1)} all-reduce(s32[896]{0:T(1024)S(1)} %get-tuple-element.30), channel_id=2, replica_groups=mesh['front'=8,'row'=4,'col'=4] {'front','row'}, use_global_device_ids=true, to_apply=%add | all-reduce | flops 896 | bytes 7168
  252.7 20.0 %shard_map.119.before = f32[2,768,768]{2,1,0:T(8,128)S(1)} custom-call(s32[32]{0:T(128)S(1)} %get-tuple-element.32.block_of, s32[32]{0:T(128)S(1)} %get-tuple-element.31.places, s32[4]{0:T(128)S(1)} %copy-done.8, f32[2,768,768]{2,1,0:T(8,128)} %bitcast.40, bf16[4,256,256]{2,1,0:T(8,128)(2,1)S(1)} %copy-done.4, bf16[4,256,256]{2,1,0:T(8,128)(2,1)S(1)} %copy-done.5, ...), custom_call_target="tpu_custom_call" | custom-call | flops 2147483648 | bytes 20971520 | tf_op jit(solution)/shard_map/pallas_call | solution.py:195
  272.7 2.2 copy-done
  274.9 13.7 %shard_map.121 = (f32[2,768,768]{2,1,0:T(8,128)}, s16[4,80,1536]{2,1,0:T(8,128)(2,1)S(1)}, s16[4,80,1536]{2,1,0:T(8,128)(2,1)S(1)}) custom-call(s32[32]{0:T(128)S(1)} %get-tuple-element.34.block_of, s32[32]{0:T(128)S(1)} %get-tuple-element.33.places, s32[2]{0:T(128)S(1)} %pad_add_fusion.role, f32[2,768,768]{2,1,0:T(8,128)} %copy-done, ...), custom_call_target="tpu_custom_call" | custom-call | flops 2147483648 | bytes 20971520 | tf_op jit(solution)/shard_map/pallas_call | solution.py:219
  293.4 4.1 collective-permute-done.7
  298.3 5.4 %collective-permute-start.11 = (s16[80,1536]{1,0:T(8,128)(2,1)S(1)}, s16[80,1536]{1,0:T(8,128)(2,1)S(1)}, u32[]{:S(2)}, u32[]{:S(2)}) collective-permute-start(s16[80,1536]{1,0:T(8,128)(2,1)S(1)} %bitcast_select_fusion.2.refs_5_), channel_id=1, source_target_pairs={{0,3},{1,0},{2,1},{3,2},{4,7},{5,4},{6,5},{7,6},{8,11},{9,8},{10,9... | collective-permute-start | bytes 737288 | tf_op jit(solution)/shard_map/ppermute | solution.py:444
  303.9 12.9 %collective-permute-start.4 = (s16[80,1536]{1,0:T(8,128)(2,1)S(1)}, s16[80,1536]{1,0:T(8,128)(2,1)S(1)}, u32[]{:S(2)}, u32[]{:S(2)}) collective-permute-start(s16[80,1536]{1,0:T(8,128)(2,1)S(1)} %bitcast_select_fusion.3.refs_0_), channel_id=1, source_target_pairs={{0,12},{4,0},{8,4},{12,8},{1,13},{5,1},{9,5},{13,9},{2,14},{6,2},{... | collective-permute-start | bytes 737288 | tf_op jit(solution)/shard_map/ppermute | solution.py:444
  316.7 2.3 collective-permute-start.3
  319.1 3.8 collective-permute-start.13
  327.0 3.7 collective-permute-done.12.refs_8_
  330.8 2.2 shard_map.122
  339.4 22.8 %collective-permute-done.14 = s16[208,1536]{1,0:T(8,128)(2,1)S(1)} collective-permute-done((s16[208,1536]{1,0:T(8,128)(2,1)S(1)}, s16[208,1536]{1,0:T(8,128)(2,1)S(1)}, u32[]{:S(2)}, u32[]{:S(2)}) %collective-permute-start.14) | collective-permute-done | bytes 639008 | tf_op jit(solution)/shard_map/ppermute | solution.py:430
  364.4 7.7 %collective-permute-start.18 = (s16[208,1536]{1,0:T(8,128)(2,1)S(1)}, s16[208,1536]{1,0:T(8,128)(2,1)S(1)}, u32[]{:S(2)}, u32[]{:S(2)}) collective-permute-start(s16[208,1536]{1,0:T(8,128)(2,1)S(1)} %bitcast_select_fusion.refs_0_), channel_id=1, source_target_pairs={{0,3},{1,0},{2,1},{3,2},{4,7},{5,4},{6,5},{7,6},{8,11},{9,8},{10,9... | collective-permute-start | bytes 1916936 | tf_op jit(solution)/shard_map/ppermute | solution.py:444
  372.4 7.9 %collective-permute-start.25 = (s16[400,768]{1,0:T(8,128)(2,1)S(1)}, s16[400,768]{1,0:T(8,128)(2,1)S(1)}, u32[]{:S(2)}, u32[]{:S(2)}) collective-permute-start(s16[400,768]{1,0:T(8,128)(2,1)S(1)} %bitcast_select_fusion.1.refs_5_), channel_id=1, source_target_pairs={{0,12},{4,0},{8,4},{12,8},{1,13},{5,1},{9,5},{13,9},{2,14},{6,2},{... | collective-permute-start | bytes 1843208 | tf_op jit(solution)/shard_map/ppermute | solution.py:444
  384.5 5.9 %collective-permute-done.25.refs_7_ = s16[400,768]{1,0:T(8,128)(2,1)S(1)} collective-permute-done((s16[400,768]{1,0:T(8,128)(2,1)S(1)}, s16[400,768]{1,0:T(8,128)(2,1)S(1)}, u32[]{:S(2)}, u32[]{:S(2)}) %collective-permute-start.25) | collective-permute-done | bytes 614432 | tf_op jit(solution)/shard_map/ppermute | solution.py:444
  392.4 2.5 collective-permute-start.26
  395.1 4.1 collective-permute-done.26.refs_8_
  399.2 2.6 collective-permute-done.19.refs_3_
  401.8 18.1 %shard_map.123 = f32[2,768,768]{2,1,0:T(8,128)} custom-call(s32[2]{0:T(128)S(1)} %pad_add_fusion.role, f32[2,768,768]{2,1,0:T(8,128)} %get-tuple-element.14.block, s16[208,1536]{1,0:T(8,128)(2,1)S(1)} %bitcast_select_fusion.refs_0_, s16[208,1536]{1,0:T(8,128)(2,1)S(1)} %collective-permute-done.17.refs_1_, ...), custom_call_target="tpu_custom_call", output_to_operand_aliasing={{}: (1, {})} | custom-call | tf_op jit(solution)/shard_map/pallas_call | solution.py:411
  (100 shorter events, 34.9 us)
Async XLA Ops:
  29.8 104.8 %all-to-all-start = ((bf16[32,512,256]{2,1,0:T(8,128)(2,1)}), bf16[32,512,256]{2,1,0:T(8,128)(2,1)}, u32[]{:S(2)}, u32[]{:S(2)}) async-start(bf16[32,512,256]{2,1,0:T(8,128)(2,1)} %shard_map.118), calls=%async_computation | async-start | bytes 16777216 | tf_op jit(solution)/shard_map/all_to_all | solution.py:493
  134.6 140.2 %all-to-all-start.1 = ((bf16[32,512,256]{2,1,0:T(8,128)(2,1)}), bf16[32,512,256]{2,1,0:T(8,128)(2,1)}, u32[]{:S(2)}, u32[]{:S(2)}) async-start(bf16[32,512,256]{2,1,0:T(8,128)(2,1)} %shard_map.120), calls=%async_computation.1 | async-start | bytes 16777216 | tf_op jit(solution)/shard_map/all_to_all | solution.py:494
  288.6 8.8 %collective-permute-start.7 = (s16[80,1536]{1,0:T(8,128)(2,1)S(1)}, s16[80,1536]{1,0:T(8,128)(2,1)S(1)}, u32[]{:S(2)}, u32[]{:S(2)}) collective-permute-start(s16[80,1536]{1,0:T(8,128)(2,1)S(1)} %get-tuple-element.25), channel_id=1, source_target_pairs={{0,1},{4,5},{8,9},{12,13},{16,17},{20,21},{24,25},{28,29},{32,33},... | collective-permute-start | bytes 737288 | tf_op jit(solution)/shard_map/ppermute | solution.py:430
  289.9 8.2 %collective-permute-start.8 = (s16[80,1536]{1,0:T(8,128)(2,1)S(1)}, s16[80,1536]{1,0:T(8,128)(2,1)S(1)}, u32[]{:S(2)}, u32[]{:S(2)}) collective-permute-start(s16[80,1536]{1,0:T(8,128)(2,1)S(1)} %get-tuple-element.24), channel_id=1, source_target_pairs={{0,3},{4,7},{8,11},{12,15},{16,19},{20,23},{24,27},{28,31},{32,35}... | collective-permute-start | bytes 737288 | tf_op jit(solution)/shard_map/ppermute | solution.py:430
  291.4 12.3 %collective-permute-start = (s16[80,1536]{1,0:T(8,128)(2,1)S(1)}, s16[80,1536]{1,0:T(8,128)(2,1)S(1)}, u32[]{:S(2)}, u32[]{:S(2)}) collective-permute-start(s16[80,1536]{1,0:T(8,128)(2,1)S(1)} %get-tuple-element.28), channel_id=1, source_target_pairs={{0,4},{1,5},{2,6},{3,7},{16,20},{17,21},{18,22},{19,23},{32,36},{3... | collective-permute-start | bytes 737288 | tf_op jit(solution)/shard_map/ppermute | solution.py:430
  292.7 11.0 %collective-permute-start.1 = (s16[80,1536]{1,0:T(8,128)(2,1)S(1)}, s16[80,1536]{1,0:T(8,128)(2,1)S(1)}, u32[]{:S(2)}, u32[]{:S(2)}) collective-permute-start(s16[80,1536]{1,0:T(8,128)(2,1)S(1)} %get-tuple-element.27), channel_id=1, source_target_pairs={{0,12},{1,13},{2,14},{3,15},{16,28},{17,29},{18,30},{19,31},{32,44... | collective-permute-start | bytes 737288 | tf_op jit(solution)/shard_map/ppermute | solution.py:430
  298.3 20.8 %collective-permute-start.11 = (s16[80,1536]{1,0:T(8,128)(2,1)S(1)}, s16[80,1536]{1,0:T(8,128)(2,1)S(1)}, u32[]{:S(2)}, u32[]{:S(2)}) collective-permute-start(s16[80,1536]{1,0:T(8,128)(2,1)S(1)} %bitcast_select_fusion.2.refs_5_), channel_id=1, source_target_pairs={{0,3},{1,0},{2,1},{3,2},{4,7},{5,4},{6,5},{7,6},{8,11},{9,8},{10,9... | collective-permute-start | bytes 737288 | tf_op jit(solution)/shard_map/ppermute | solution.py:444
  303.9 19.0 %collective-permute-start.4 = (s16[80,1536]{1,0:T(8,128)(2,1)S(1)}, s16[80,1536]{1,0:T(8,128)(2,1)S(1)}, u32[]{:S(2)}, u32[]{:S(2)}) collective-permute-start(s16[80,1536]{1,0:T(8,128)(2,1)S(1)} %bitcast_select_fusion.3.refs_0_), channel_id=1, source_target_pairs={{0,12},{4,0},{8,4},{12,8},{1,13},{5,1},{9,5},{13,9},{2,14},{6,2},{... | collective-permute-start | bytes 737288 | tf_op jit(solution)/shard_map/ppermute | solution.py:444
  316.7 8.1 %collective-permute-start.10 = (s16[80,1536]{1,0:T(8,128)(2,1)S(1)}, s16[80,1536]{1,0:T(8,128)(2,1)S(1)}, u32[]{:S(2)}, u32[]{:S(2)}) collective-permute-start(s16[80,1536]{1,0:T(8,128)(2,1)S(1)} %bitcast_select_fusion.2.refs_5_), channel_id=1, source_target_pairs={{0,1},{1,2},{2,3},{3,0},{4,5},{5,6},{6,7},{7,4},{8,9},{9,10},{10,1... | collective-permute-start | bytes 737288 | tf_op jit(solution)/shard_map/ppermute | solution.py:443
  316.7 8.2 %collective-permute-start.3 = (s16[80,1536]{1,0:T(8,128)(2,1)S(1)}, s16[80,1536]{1,0:T(8,128)(2,1)S(1)}, u32[]{:S(2)}, u32[]{:S(2)}) collective-permute-start(s16[80,1536]{1,0:T(8,128)(2,1)S(1)} %bitcast_select_fusion.3.refs_0_), channel_id=1, source_target_pairs={{0,4},{4,8},{8,12},{12,0},{1,5},{5,9},{9,13},{13,1},{2,6},{6,10},{... | collective-permute-start | bytes 737288 | tf_op jit(solution)/shard_map/ppermute | solution.py:443
  319.1 11.7 %collective-permute-start.13 = (s16[48,1536]{1,0:T(8,128)(2,1)S(1)}, s16[48,1536]{1,0:T(8,128)(2,1)S(1)}, u32[]{:S(2)}, u32[]{:S(2)}) collective-permute-start(s16[48,1536]{1,0:T(8,128)(2,1)S(1)} %slice.99), channel_id=1, source_target_pairs={{0,3},{1,0},{2,1},{3,2},{4,7},{5,4},{6,5},{7,6},{8,11},{9,8},{10,9... | collective-permute-start | bytes 442376 | tf_op jit(solution)/shard_map/ppermute | solution.py:446
  322.9 7.9 %collective-permute-start.6 = (s16[48,1536]{1,0:T(8,128)(2,1)S(1)}, s16[48,1536]{1,0:T(8,128)(2,1)S(1)}, u32[]{:S(2)}, u32[]{:S(2)}) collective-permute-start(s16[48,1536]{1,0:T(8,128)(2,1)S(1)} %slice.97), channel_id=1, source_target_pairs={{0,12},{4,0},{8,4},{12,8},{1,13},{5,1},{9,5},{13,9},{2,14},{6,2},{... | collective-permute-start | bytes 442376 | tf_op jit(solution)/shard_map/ppermute | solution.py:446
  334.6 27.7 %collective-permute-start.14 = (s16[208,1536]{1,0:T(8,128)(2,1)S(1)}, s16[208,1536]{1,0:T(8,128)(2,1)S(1)}, u32[]{:S(2)}, u32[]{:S(2)}) collective-permute-start(s16[208,1536]{1,0:T(8,128)(2,1)S(1)} %get-tuple-element.19), channel_id=1, source_target_pairs={{0,1},{4,5},{8,9},{12,13},{16,17},{20,21},{24,25},{28,29},{32,33},... | collective-permute-start | bytes 1916936 | tf_op jit(solution)/shard_map/ppermute | solution.py:430
  335.9 27.1 %collective-permute-start.15 = (s16[208,1536]{1,0:T(8,128)(2,1)S(1)}, s16[208,1536]{1,0:T(8,128)(2,1)S(1)}, u32[]{:S(2)}, u32[]{:S(2)}) collective-permute-start(s16[208,1536]{1,0:T(8,128)(2,1)S(1)} %get-tuple-element.18), channel_id=1, source_target_pairs={{0,3},{4,7},{8,11},{12,15},{16,19},{20,23},{24,27},{28,31},{32,35}... | collective-permute-start | bytes 1916936 | tf_op jit(solution)/shard_map/ppermute | solution.py:430
  336.6 26.4 %collective-permute-start.16 = (s16[208,1536]{1,0:T(8,128)(2,1)S(1)}, s16[208,1536]{1,0:T(8,128)(2,1)S(1)}, u32[]{:S(2)}, u32[]{:S(2)}) collective-permute-start(s16[208,1536]{1,0:T(8,128)(2,1)S(1)} %get-tuple-element.17), channel_id=1, source_target_pairs={{0,2},{4,6},{8,10},{12,14},{16,18},{20,22},{24,26},{28,30},{32,34}... | collective-permute-start | bytes 1916936 | tf_op jit(solution)/shard_map/ppermute | solution.py:430
  337.4 34.6 %collective-permute-start.21 = (s16[400,768]{1,0:T(8,128)(2,1)S(1)}, s16[400,768]{1,0:T(8,128)(2,1)S(1)}, u32[]{:S(2)}, u32[]{:S(2)}) collective-permute-start(s16[400,768]{1,0:T(8,128)(2,1)S(1)} %get-tuple-element.22), channel_id=1, source_target_pairs={{0,4},{1,5},{2,6},{3,7},{16,20},{17,21},{18,22},{19,23},{32,36},{3... | collective-permute-start | bytes 1843208 | tf_op jit(solution)/shard_map/ppermute | solution.py:430
  338.7 33.3 %collective-permute-start.22 = (s16[400,768]{1,0:T(8,128)(2,1)S(1)}, s16[400,768]{1,0:T(8,128)(2,1)S(1)}, u32[]{:S(2)}, u32[]{:S(2)}) collective-permute-start(s16[400,768]{1,0:T(8,128)(2,1)S(1)} %get-tuple-element.21), channel_id=1, source_target_pairs={{0,12},{1,13},{2,14},{3,15},{16,28},{17,29},{18,30},{19,31},{32,44... | collective-permute-start | bytes 1843208 | tf_op jit(solution)/shard_map/ppermute | solution.py:430
  362.3 9.8 %collective-permute-start.23 = (s16[400,768]{1,0:T(8,128)(2,1)S(1)}, s16[400,768]{1,0:T(8,128)(2,1)S(1)}, u32[]{:S(2)}, u32[]{:S(2)}) collective-permute-start(s16[400,768]{1,0:T(8,128)(2,1)S(1)} %get-tuple-element.20), channel_id=1, source_target_pairs={{0,8},{1,9},{2,10},{3,11},{16,24},{17,25},{18,26},{19,27},{32,40},... | collective-permute-start | bytes 1843208 | tf_op jit(solution)/shard_map/ppermute | solution.py:430
  364.4 18.0 %collective-permute-start.18 = (s16[208,1536]{1,0:T(8,128)(2,1)S(1)}, s16[208,1536]{1,0:T(8,128)(2,1)S(1)}, u32[]{:S(2)}, u32[]{:S(2)}) collective-permute-start(s16[208,1536]{1,0:T(8,128)(2,1)S(1)} %bitcast_select_fusion.refs_0_), channel_id=1, source_target_pairs={{0,3},{1,0},{2,1},{3,2},{4,7},{5,4},{6,5},{7,6},{8,11},{9,8},{10,9... | collective-permute-start | bytes 1916936 | tf_op jit(solution)/shard_map/ppermute | solution.py:444
  372.4 18.0 %collective-permute-start.25 = (s16[400,768]{1,0:T(8,128)(2,1)S(1)}, s16[400,768]{1,0:T(8,128)(2,1)S(1)}, u32[]{:S(2)}, u32[]{:S(2)}) collective-permute-start(s16[400,768]{1,0:T(8,128)(2,1)S(1)} %bitcast_select_fusion.1.refs_5_), channel_id=1, source_target_pairs={{0,12},{4,0},{8,4},{12,8},{1,13},{5,1},{9,5},{13,9},{2,14},{6,2},{... | collective-permute-start | bytes 1843208 | tf_op jit(solution)/shard_map/ppermute | solution.py:444
  380.3 14.7 %collective-permute-start.17 = (s16[208,1536]{1,0:T(8,128)(2,1)S(1)}, s16[208,1536]{1,0:T(8,128)(2,1)S(1)}, u32[]{:S(2)}, u32[]{:S(2)}) collective-permute-start(s16[208,1536]{1,0:T(8,128)(2,1)S(1)} %bitcast_select_fusion.refs_0_), channel_id=1, source_target_pairs={{0,1},{1,2},{2,3},{3,0},{4,5},{5,6},{6,7},{7,4},{8,9},{9,10},{10,1... | collective-permute-start | bytes 1916936 | tf_op jit(solution)/shard_map/ppermute | solution.py:443
  380.3 12.1 %collective-permute-start.24 = (s16[400,768]{1,0:T(8,128)(2,1)S(1)}, s16[400,768]{1,0:T(8,128)(2,1)S(1)}, u32[]{:S(2)}, u32[]{:S(2)}) collective-permute-start(s16[400,768]{1,0:T(8,128)(2,1)S(1)} %bitcast_select_fusion.1.refs_5_), channel_id=1, source_target_pairs={{0,4},{4,8},{8,12},{12,0},{1,5},{5,9},{9,13},{13,1},{2,6},{6,10},{... | collective-permute-start | bytes 1843208 | tf_op jit(solution)/shard_map/ppermute | solution.py:443
  382.5 19.4 %collective-permute-start.20 = (s16[112,1536]{1,0:T(8,128)(2,1)S(1)}, s16[112,1536]{1,0:T(8,128)(2,1)S(1)}, u32[]{:S(2)}, u32[]{:S(2)}) collective-permute-start(s16[112,1536]{1,0:T(8,128)(2,1)S(1)} %slice.101), channel_id=1, source_target_pairs={{0,3},{1,0},{2,1},{3,2},{4,7},{5,4},{6,5},{7,6},{8,11},{9,8},{10,9... | collective-permute-start | bytes 1032200 | tf_op jit(solution)/shard_map/ppermute | solution.py:446
  390.4 8.8 %collective-permute-start.27 = (s16[208,768]{1,0:T(8,128)(2,1)S(1)}, s16[208,768]{1,0:T(8,128)(2,1)S(1)}, u32[]{:S(2)}, u32[]{:S(2)}) collective-permute-start(s16[208,768]{1,0:T(8,128)(2,1)S(1)} %slice.103), channel_id=1, source_target_pairs={{0,12},{4,0},{8,4},{12,8},{1,13},{5,1},{9,5},{13,9},{2,14},{6,2},{... | collective-permute-start | bytes 958472 | tf_op jit(solution)/shard_map/ppermute | solution.py:446
  (16 other events, 674.2 us)

commit v2 on v0

v2 whole, which is shorter than its diff:
```python
import functools
import math

import jax
import jax.numpy as jnp
from jax import lax
from jax.experimental import pallas as pl
from jax.experimental.pallas import tpu as pltpu
from jax.sharding import PartitionSpec as P

TILE = 256
RANK = 128
TS = 3
SIDE = TS * TILE
SENT = 28
GROUP = 32
RING = 4
CODE_ROWS = 16
STEP = 4
NOTE_ROWS = 16
LOG_STEP = math.log(2.0) / 32.0
VMEM_BYTES = 48 * 1024 * 1024
BF16 = jnp.bfloat16
F32 = jnp.float32


def encode(values):
    peak = jnp.maximum(jnp.max(jnp.abs(values), axis=0, keepdims=True), 1e-30)
    code = jnp.ceil(jnp.log(peak * (1.0 / 32700.0)) * (1.0 / LOG_STEP))
    whole = jnp.round(values * jnp.exp(code * -LOG_STEP))
    whole = jnp.clip(whole, -32767.0, 32767.0).astype(jnp.int32)
    code_rows = jnp.broadcast_to(code.astype(jnp.int32), (CODE_ROWS, values.shape[1]))
    return whole.astype(jnp.int16), code_rows.astype(jnp.int16)


def store_piece(ref, piece, values):
    rows = values.shape[0]
    whole, code_rows = encode(values)
    ref[piece, :rows, :] = whole
    ref[piece, rows:, :] = code_rows


def decode(piece_rows, code_rows):
    code = code_rows[:1].astype(jnp.int32).astype(F32)
    return piece_rows.astype(jnp.int32).astype(F32) * jnp.exp(code * LOG_STEP)


def cut(x):
    high = x.astype(BF16)
    return high, (x - high.astype(F32)).astype(BF16)


def dot(a, b):
    return lax.dot_general(a, b, (((1,), (0,)), ((), ())), preferred_element_type=F32)


def dot_cut(a, b):
    return dot(a[0], b[0]) + (dot(a[0], b[1]) + dot(a[1], b[0]))


def cuts(pair):
    return [cut(x) for x in pair]


def complex_dot(a, b):
    return (
        dot_cut(a[0], b[0]) - dot_cut(a[1], b[1]),
        dot_cut(a[0], b[1]) + dot_cut(a[1], b[0]),
    )


def minus(a, b):
    return a[0] - b[0], a[1] - b[1]


def pack_kernel(told, source, filled, ranks, *notes_and_refs):
    notes, refs = notes_and_refs[:told], notes_and_refs[told:]
    lefts, rights, rows, cols = (refs[STEP * i : STEP * (i + 1)] for i in range(4))
    out = refs[4 * STEP]
    first = pl.program_id(0) * STEP
    index = lax.broadcasted_iota(jnp.int32, (TILE, TILE), 0)
    width = lax.broadcasted_iota(jnp.int32, (TILE, 2 * RANK), 1)
    width = jnp.where(width >= RANK, width - RANK, width)
    turned = (((0,), (0,)), ((), ()))

    def onehot(chosen):
        return jnp.where(index == chosen, 1.0, 0.0).astype(BF16)

    for j in range(STEP):
        if told:
            at = lax.broadcasted_iota(jnp.int32, (NOTE_ROWS, TILE), 0)
            lines = jnp.where(at == 0, notes[0][first + j], notes[1][first + j])
            out[j, TILE + 2 * RANK :, :] = lines.astype(F32).astype(BF16)

        @pl.when(filled[first + j] == 1)
        def _(j=j):
            rank = ranks[source[first + j]]
            moved = lax.dot_general(
                onehot(rows[j][0]), lefts[j][0], turned, preferred_element_type=F32
            )
            out[j, :TILE, :] = jnp.where(width < rank, moved, 0.0).astype(BF16)
            out[j, TILE : TILE + 2 * RANK, :] = lax.dot_general(
                rights[j][0], onehot(cols[j][0]), turned, preferred_element_type=F32
            ).astype(BF16)


def pack(source, filled, ranks, notes, left, right, rows, cols):
    depth = TILE + 2 * RANK + (NOTE_ROWS if notes else 0)

    def spec(shape, j):
        return pl.BlockSpec((1,) + shape, lambda s, src, *_: (src[s * STEP + j], 0, 0))

    tiles = [spec((TILE, 2 * RANK), j) for j in range(STEP)]
    lines = [spec((1, TILE), j) for j in range(STEP)]
    return pl.pallas_call(
        functools.partial(pack_kernel, len(notes)),
        grid_spec=pltpu.PrefetchScalarGridSpec(
            num_scalar_prefetch=3 + len(notes),
            grid=(GROUP // STEP,),
            in_specs=tiles + tiles + lines + lines,
            out_specs=pl.BlockSpec((STEP, depth, TILE), lambda s, *_: (s, 0, 0)),
        ),
        out_shape=jax.ShapeDtypeStruct((GROUP, depth, TILE), BF16),
        compiler_params=pltpu.CompilerParams(vmem_limit_bytes=VMEM_BYTES),
        cost_estimate=pl.CostEstimate(
            flops=4 * SENT * TILE**3, bytes_accessed=16 * 2**20, transcendentals=0
        ),
    )(source, filled, ranks, *notes, *[left] * STEP, *[right] * STEP, *[rows] * STEP, *[cols] * STEP)


def add_at(out, place, real, imag):
    a = place // TS
    rows = pl.ds(pl.multiple_of(a * TILE, TILE), TILE)
    cols = pl.ds(pl.multiple_of((place - a * TS) * TILE, TILE), TILE)
    out[0, rows, cols] += real
    out[1, rows, cols] += imag


def add_own(out, place, left, right):
    real_side = jnp.concatenate([right[:, :RANK], -right[:, RANK:]], 1)
    imag_side = jnp.concatenate([right[:, RANK:], right[:, :RANK]], 1)
    contract = (((1,), (1,)), ((), ()))
    add_at(
        out,
        place,
        lax.dot_general(left, real_side, contract, preferred_element_type=F32),
        lax.dot_general(left, imag_side, contract, preferred_element_type=F32),
    )


def add_slots(out, places, slots):
    first = pl.program_id(0) * STEP
    for j in range(STEP):

        @pl.when(places[first + j] >= 0)
        def _(j=j):
            left = slots[j, :TILE, :]
            top = slots[j, TILE : TILE + RANK, :]
            bottom = slots[j, TILE + RANK : TILE + 2 * RANK, :]
            add_at(
                out,
                places[first + j],
                dot(left, jnp.concatenate([top, -bottom], 0)),
                dot(left, jnp.concatenate([bottom, top], 0)),
            )


def first_kernel(places, own_places, before, own_left, own_right, slots, out):
    @pl.when(pl.program_id(0) == 0)
    def _():
        pltpu.sync_copy(before, out)

        def own_step(j, carry):
            add_own(out, own_places[j], own_left[j], own_right[j])
            return carry

        lax.fori_loop(0, own_left.shape[0], own_step, 0)

    add_slots(out, places, slots)


def tile_at(i, j):
    return slice(i * TILE, (i + 1) * TILE), slice(j * TILE, (j + 1) * TILE)


def get(ref, rows, cols):
    return ref[0, rows, cols], ref[1, rows, cols]


def put(ref, rows, cols, value):
    ref[0, rows, cols] = value[0]
    ref[1, rows, cols] = value[1]


def second_kernel(places, role, before, slots, inverse, out, along_row, along_col):
    step = pl.program_id(0)

    @pl.when(step == 0)
    def _():
        pltpu.sync_copy(before, out)

    add_slots(out, places, slots)
    last = step == GROUP // STEP - 1
    long, short = SIDE // RING, 2 * TILE // RING

    @pl.when(last & (role[0] == 0) & (role[1] == 0))
    def _():
        pivots = [cuts((inverse[p, 0], inverse[p, 1])) for p in range(TS)]
        for p in range(TS - 1):
            uppers = {j: cuts(get(out, *tile_at(p, j))) for j in range(p + 1, TS)}
            for i in range(p + 1, TS):
                factor = complex_dot(cuts(get(out, *tile_at(i, p))), pivots[p])
                put(out, *tile_at(i, p), factor)
                factor = cuts(factor)
                for j in range(p + 1, TS):
                    at = tile_at(i, j)
                    put(out, *at, minus(get(out, *at), complex_dot(factor, uppers[j])))
        lower = [get(out, *tile_at(i, j)) for i, j in ((1, 0), (2, 0), (2, 1))]
        lower = jnp.concatenate([jnp.concatenate(x, 1) for x in lower], 0)
        upper = [
            complex_dot(cuts(get(out, *tile_at(i, j))), pivots[j])
            for i, j in ((0, 1), (0, 2), (1, 2))
        ]
        upper = [jnp.concatenate([x[half] for x in upper], 1) for half in (0, 1)]
        for piece in range(RING):
            store_piece(along_row, piece, lower[piece * long : (piece + 1) * long])
            half, start = divmod(piece * short, TILE)
            store_piece(along_col, piece, upper[half][start : start + short])

    @pl.when(last & (role[0] > 0) & (role[1] == 0))
    def _():
        for p in range(TS):
            pivot = cuts((inverse[p, 0], inverse[p, 1]))
            for i in range(TS):
                at = tile_at(i, p)
                put(out, *at, complex_dot(cuts(get(out, *at)), pivot))
        for piece in range(RING):
            rows = slice(piece * long, (piece + 1) * long)
            store_piece(along_row, piece, jnp.concatenate(get(out, rows, slice(0, TILE)), 1))

    @pl.when(last & (role[0] == 0) & (role[1] > 0))
    def _():
        for piece in range(RING):
            half, start = divmod(piece * short, TILE)
            store_piece(along_col, piece, out[half, start : start + short, :])


def whole(shape):
    return pl.BlockSpec(shape, lambda *_: (0,) * len(shape))


def slot_spec(slots):
    return pl.BlockSpec((STEP,) + slots.shape[1:], lambda s, *_: (s, 0, 0))


ANYWHERE = pl.BlockSpec(memory_space=pl.ANY)
HELD = pl.BlockSpec(memory_space=pltpu.VMEM)
ADD_COST = pl.CostEstimate(
    flops=4 * GROUP * TILE**3, bytes_accessed=20 * 2**20, transcendentals=0
)


def add_first(places, own_places, before, own_left, own_right, slots):
    return pl.pallas_call(
        first_kernel,
        grid_spec=pltpu.PrefetchScalarGridSpec(
            num_scalar_prefetch=2,
            grid=(GROUP // STEP,),
            in_specs=[ANYWHERE, whole(own_left.shape), whole(own_right.shape), slot_spec(slots)],
            out_specs=whole(before.shape),
        ),
        out_shape=jax.ShapeDtypeStruct(before.shape, F32),
        compiler_params=pltpu.CompilerParams(vmem_limit_bytes=VMEM_BYTES),
        cost_estimate=ADD_COST,
    )(places, own_places, before, own_left, own_right, slots)


def row_shape(panels):
    return (RING, SIDE // RING + CODE_ROWS, 2 * TILE * panels)


def col_shape(panels):
    return (RING, 2 * TILE * panels // RING + CODE_ROWS, SIDE)


def coded(shape):
    return jax.ShapeDtypeStruct(shape, jnp.int16)


def add_second(places, role, before, slots, inverse):
    return pl.pallas_call(
        second_kernel,
        grid_spec=pltpu.PrefetchScalarGridSpec(
            num_scalar_prefetch=2,
            grid=(GROUP // STEP,),
            in_specs=[ANYWHERE, slot_spec(slots), whole(inverse.shape)],
            out_specs=[whole(before.shape), whole(row_shape(1)), whole(col_shape(1))],
        ),
        out_shape=[
            jax.ShapeDtypeStruct(before.shape, F32),
            coded(row_shape(1)),
            coded(col_shape(1)),
        ],
        compiler_params=pltpu.CompilerParams(vmem_limit_bytes=VMEM_BYTES),
        cost_estimate=ADD_COST,
    )(places, role, before, slots, inverse)


def unpack(refs, place, high, low):
    rows = refs[0].shape[0] - CODE_ROWS
    for ref, shift in zip(refs, (0, 2, RING - 1, 1)):
        at = ((place + shift) & (RING - 1)) * rows
        h, l = cut(decode(ref[:rows, :], ref[rows:, :]))
        high[pl.ds(pl.multiple_of(at, 16), rows), :] = h
        low[pl.ds(pl.multiple_of(at, 16), rows), :] = l


def trailing(held, rows, left, right):
    panels = left[0].shape[1] // (2 * TILE)

    def turned(x, imag):
        parts = []
        for p in range(panels):
            a = x[rows, 2 * p * TILE : (2 * p + 1) * TILE]
            b = x[rows, (2 * p + 1) * TILE : (2 * p + 2) * TILE]
            parts += [b, a] if imag else [a, -b]
        return jnp.concatenate(parts, 1)

    for half in (0, 1):
        a = [turned(x, half == 1) for x in left]
        for j in range(TS):
            cols = slice(j * TILE, (j + 1) * TILE)
            held[half, rows, cols] -= dot_cut(a, [x[:, cols] for x in right])


def piece_scratch(panels):
    return [pltpu.VMEM((SIDE, 2 * TILE * panels), BF16)] * 2 + [
        pltpu.VMEM((2 * TILE * panels, SIDE), BF16)
    ] * 2


def panel_kernel(role, block, *refs):
    from_row, from_col = refs[:RING], refs[RING : 2 * RING]
    out, along_row, along_col, held, row_high, row_low, col_high, col_low, sem = refs[2 * RING :]

    @pl.when((role[0] > 0) | (role[1] > 0))
    def _():
        fetch = pltpu.make_async_copy(block, held, sem)
        fetch.start()

        @pl.when(role[1] > 0)
        def _():
            unpack(from_row, role[1], row_high, row_low)

        @pl.when(role[0] > 0)
        def _():
            unpack(from_col, role[0], col_high, col_low)

        fetch.wait()

    @pl.when((role[0] > 0) & (role[1] == 0))
    def _():
        def tile(t):
            cols = slice(t * TILE, (t + 1) * TILE)
            return [(col_high[rows, cols], col_low[rows, cols]) for rows in (slice(0, TILE), slice(TILE, 2 * TILE))]

        def chunk(i, carry):
            rows = pl.ds(pl.multiple_of(i * TILE, TILE), TILE)
            cols = [slice(j * TILE, (j + 1) * TILE) for j in range(TS)]
            f0 = cuts(get(held, rows, cols[0]))
            f1 = minus(get(held, rows, cols[1]), complex_dot(f0, tile(0)))
            put(held, rows, cols[1], f1)
            f2 = minus(get(held, rows, cols[2]), complex_dot(f0, tile(1)))
            put(held, rows, cols[2], minus(f2, complex_dot(cuts(f1), tile(2))))
            return carry

        lax.fori_loop(0, TS, chunk, 0)
        store = pltpu.make_async_copy(held, out, sem)
        store.start()
        part = SIDE // RING

        def code_piece(piece, carry):
            rows = pl.ds(pl.multiple_of(piece * part, 8), part)
            wide = [x for j in range(1, TS) for x in get(held, rows, slice(j * TILE, (j + 1) * TILE))]
            store_piece(along_row, piece, jnp.concatenate(wide, 1))
            return carry

        lax.fori_loop(0, RING, code_piece, 0)
        store.wait()

    @pl.when((role[0] == 0) & (role[1] > 0))
    def _():
        def tile(t):
            rows = slice(t * TILE, (t + 1) * TILE)
            return [(row_high[rows, cols], row_low[rows, cols]) for cols in (slice(0, TILE), slice(TILE, 2 * TILE))]

        def chunk(j, carry):
            cols = pl.ds(pl.multiple_of(j * TILE, TILE), TILE)
            rows = [slice(i * TILE, (i + 1) * TILE) for i in range(TS)]
            p0 = cuts(get(held, rows[0], cols))
            p1 = minus(get(held, rows[1], cols), complex_dot(tile(0), p0))
            put(held, rows[1], cols, p1)
            p2 = minus(get(held, rows[2], cols), complex_dot(tile(1), p0))
            put(held, rows[2], cols, minus(p2, complex_dot(tile(2), cuts(p1))))
            return carry

        lax.fori_loop(0, TS, chunk, 0)
        store = pltpu.make_async_copy(held, out, sem)
        store.start()
        for piece in range(RING):
            at, half = divmod(piece, 2)
            store_piece(along_col, piece, held[half, (at + 1) * TILE : (at + 2) * TILE, :])
        store.wait()

    @pl.when((role[0] > 0) & (role[1] > 0))
    def _():
        def chunk(i, carry):
            rows = pl.ds(pl.multiple_of(i * TILE, TILE), TILE)
            trailing(held, rows, (row_high, row_low), (col_high, col_low))
            return carry

        lax.fori_loop(0, TS, chunk, 0)
        pltpu.sync_copy(held, out)


def panel(role, block, from_row, from_col):
    return pl.pallas_call(
        panel_kernel,
        in_specs=[pl.BlockSpec(memory_space=pltpu.SMEM), ANYWHERE] + [HELD] * (2 * RING),
        out_specs=[ANYWHERE, HELD, HELD],
        out_shape=[
            jax.ShapeDtypeStruct(block.shape, F32),
            coded(row_shape(2)),
            coded(col_shape(2)),
        ],
        scratch_shapes=[pltpu.VMEM(block.shape, F32)]
        + piece_scratch(1)
        + [pltpu.SemaphoreType.DMA],
        input_output_aliases={1: 0},
        compiler_params=pltpu.CompilerParams(vmem_limit_bytes=VMEM_BYTES),
    )(role, block, *from_row, *from_col)


def trail_kernel(role, block, *refs):
    from_row, from_col = refs[:RING], refs[RING : 2 * RING]
    out, held, row_high, row_low, col_high, col_low, sem, sems = refs[2 * RING :]

    @pl.when((role[0] > 0) & (role[1] > 0))
    def _():
        fetch = pltpu.make_async_copy(block, held, sem)
        fetch.start()
        unpack(from_row, role[1], row_high, row_low)
        unpack(from_col, role[0], col_high, col_low)
        fetch.wait()

        def store(i):
            rows = pl.ds(pl.multiple_of(i * TILE, TILE), TILE)
            return pltpu.make_async_copy(held.at[:, rows, :], out.at[:, rows, :], sems.at[i])

        def chunk(i, carry):
            rows = pl.ds(pl.multiple_of(i * TILE, TILE), TILE)
            trailing(held, rows, (row_high, row_low), (col_high, col_low))
            store(i).start()
            return carry

        lax.fori_loop(0, TS, chunk, 0)
        for i in range(TS):
            store(i).wait()


def trail(role, block, from_row, from_col):
    return pl.pallas_call(
        trail_kernel,
        in_specs=[pl.BlockSpec(memory_space=pltpu.SMEM), ANYWHERE] + [HELD] * (2 * RING),
        out_specs=ANYWHERE,
        out_shape=jax.ShapeDtypeStruct(block.shape, F32),
        scratch_shapes=[pltpu.VMEM(block.shape, F32)]
        + piece_scratch(2)
        + [pltpu.SemaphoreType.DMA, pltpu.SemaphoreType.DMA((TS,))],
        input_output_aliases={1: 0},
        compiler_params=pltpu.CompilerParams(vmem_limit_bytes=VMEM_BYTES),
    )(role, block, *from_row, *from_col)


def spread(pieces, axis):
    got = [lax.ppermute(pieces[d], axis, [(0, d)]) for d in (2, 1, 3)]
    here = lax.axis_index(axis)
    return jnp.where(
        here == 0,
        pieces[0],
        jnp.where(here == 2, got[0], jnp.where(here == 1, got[1], got[2])),
    )


def exchange(own, axis):
    others = []
    for shift in (2, 1, 3):
        pairs = [(i, (i + shift) % RING) for i in range(RING)]
        others.append(lax.ppermute(own, axis, [p for p in pairs if p[1] != 0]))
    return [own] + others


def body(
    parent_front,
    child_left,
    child_right,
    tile_ranks,
    destination,
    tile_place,
    row_source,
    col_source,
    own_left,
    own_right,
    own_place,
    pivot_inverse,
):
    joined = ("front", "row")
    role = jnp.stack([lax.axis_index("row"), lax.axis_index("col")]).astype(jnp.int32)
    none = 16 * SENT
    numbers = 16 * jnp.arange(SENT, dtype=jnp.int32) + tile_place
    to_each = jnp.where(
        destination[None, :] == jnp.arange(GROUP, dtype=jnp.int32)[:, None],
        numbers[None, :],
        none,
    )
    first_out = jnp.min(to_each, 1)
    second_out = jnp.min(jnp.where(to_each > first_out[:, None], to_each, none), 1)

    rows = row_source[:, None, :]
    cols = col_source[:, None, :]

    def place_of(number):
        return jnp.where(number < none, number & 15, -1)

    def sent(number, notes):
        filled = (number < none).astype(jnp.int32)
        slots = pack(
            (number >> 4) * filled, filled, tile_ranks, notes, child_left, child_right, rows, cols
        )
        return lax.all_to_all(slots, joined, split_axis=0, concat_axis=0, tiled=True)

    second_slots = sent(second_out, [place_of(second_out), place_of(first_out)])
    first_slots = sent(first_out, [])
    places = second_slots[:, TILE + 2 * RANK : TILE + 2 * RANK + 2, 0].astype(jnp.int32)

    block = add_first(places[:, 0], own_place, parent_front[0], own_left, own_right, second_slots)
    block, row_pieces, col_pieces = add_second(
        places[:, 1], role, block, first_slots, pivot_inverse[0]
    )
    from_row, from_col = spread(row_pieces, "col"), spread(col_pieces, "row")
    from_row, from_col = exchange(from_row, "col"), exchange(from_col, "row")
    block, row_pieces, col_pieces = panel(role, block, from_row, from_col)
    from_row, from_col = spread(row_pieces, "col"), spread(col_pieces, "row")
    from_row, from_col = exchange(from_row, "col"), exchange(from_col, "row")
    return trail(role, block, from_row, from_col)[None]


def solution(mesh):
    joined = ("front", "row", "col")
    tiles = P(joined, None, None)
    return jax.shard_map(
        body,
        mesh=mesh,
        in_specs=(
            P("front", None, "row", "col"),
            tiles,
            tiles,
            P(joined),
            P(joined),
            P(joined),
            P(joined, None),
            P(joined, None),
            tiles,
            tiles,
            P(joined),
            P("front", None, None, None, None),
        ),
        out_specs=P("front", None, "row", "col"),
        check_vma=False,
    )
```

time: 1100 us -> 363 us (0.33)
  local copies, waits for them, and re-layouts: 353 us -> 8.81 us
  matrix products: 162 us -> 0 us
  waiting for transfers between devices: 385 us -> 223 us
  blocking collectives: 101 us -> 0 us
  Pallas kernels: 0 us -> 65.4 us
  other arithmetic: 53.2 us -> 3.96 us
  starting transfers between devices: 15.8 us -> 57.1 us
  between operations: 14.3 us -> 0.63 us
    psum x6 -> x0, waiting for transfers between devices: 316 us -> none  [from_root(): return lax.psum(block, axis)]
    gather x7 -> x0, local copies, waits for them, and re-layouts: 267 us -> none  [the longest x4 251 us: pick_rows(): return block[chosen]]
    dot_general x30 -> x0, matrix products: 162 us -> none  [the longest x9 97.5 us: add_block(): jnp.einsum('st,sckl->tckl', onehot, update, precision=lax.Precision.HIGHEST)]
    all_to_all x2, waiting for transfers between devices: 68.4 us -> 171 us  [sent(): lax.all_to_all(slots, joined, split_axis=0, concat_axis=0, tiled=True)]
    all_to_all x1 -> x0, blocking collectives: 101 us -> none  [body(): lax.all_to_all(right_slots, ('front', 'row'), split_axis=0, concat_axis=0...]
    pallas_call x0 -> x6, Pallas kernels: none -> 65.4 us  [the longest x2 19.5 us: pack(): pl.pallas_call(functools.partial(pack_kernel, len(notes)), grid_spec=pltp...]
    transpose x11 -> x0, local copies, waits for them, and re-layouts: 58.1 us -> none  [the longest x9 46.5 us: add_block(): jnp.einsum('skq,sclq->sckl', left_block, both_sides, preferred_element_ty...]
    ppermute x0 -> x24, waiting for transfers between devices: none -> 51.7 us  [the longest x12 30.5 us: spread(): got = [lax.ppermute(pieces[d], axis, [(0, d)]) for d in (2, 1, 3)]]
  transfers between devices with their start and end apart: 8 -> 26, of which waited for: 7 -> 11; matrix products, arithmetic and copies ran while one was open for 30% -> 1% of each run, Pallas kernels for 0% -> 6%
where the time goes in v2:
time: 363 us; the launch traced here: 359 us
  waiting for transfers between devices  223 us (61%)
  Pallas kernels  65.4 us (18%)
  starting transfers between devices  57.1 us (16%)
  local copies, waits for them, and re-layouts  8.81 us (2%)
  other arithmetic  3.96 us (1%)
    all_to_all x2, waiting for transfers between devices, sent(): lax.all_to_all(slots, joined, split_axis=0, concat_axis=0, tiled=True)  171 us
    ppermute x12, waiting for transfers between devices, spread(): got = [lax.ppermute(pieces[d], axis, [(0, d)]) for d in (2, 1, 3)]  30.5 us
    ppermute x12, starting transfers between devices, exchange(): others.append(lax.ppermute(own, axis, [p for p in pairs if p[1] != 0]))  29.9 us
    ppermute x12, waiting for transfers between devices, exchange(): others.append(lax.ppermute(own, axis, [p for p in pairs if p[1] != 0]))  21.3 us
    pallas_call x2, Pallas kernels, pack(): pl.pallas_call(functools.partial(pack_kernel, len(notes)), grid_spec=pltp...  19.5 us
    all_to_all x2, starting transfers between devices, sent(): lax.all_to_all(slots, joined, split_axis=0, concat_axis=0, tiled=True)  16.6 us
    pallas_call x1, Pallas kernels, add_second(): pl.pallas_call(second_kernel, grid_spec=pltpu.PrefetchScalarGridSpec(num_...  14 us
    pallas_call x1, Pallas kernels, trail(): pl.pallas_call(trail_kernel, in_specs=[pl.BlockSpec(memory_space=pltpu.SM...  12.8 us
  transfers between devices with their start and end apart: 26, of which 11 were waited for; matrix products, arithmetic and copies ran while one was open for 1% of the time, Pallas kernels for 6%

profile of v2, /device:TPU:34, one launch (start us, length us, event | category | flops | bytes accessed | tf_op | source)
XLA Modules:
  0.0 359.2 jit_solution(16731643807142102616)
XLA Ops:
  3.9 2.0 copy-done
  6.6 8.4 %shard_map.118 = bf16[32,528,256]{2,1,0:T(8,128)(2,1)} custom-call(s32[32]{0:T(128)S(1)} %get-tuple-element.34.source, s32[32]{0:T(128)S(1)} %fusion.1.filled, s32[28]{0:T(128)S(1)} %copy-done.6, s32[32]{0:T(128)S(1)} %get-tuple-element.33.notes_and_refs_0_, s32[32]{0:T(128)S(1)} %get-tuple-element.32.notes_and_refs_1_, bf16[28,256,256]{2,1,0:T(8,128)(2,1)S(1)} %copy-done, ...), custom_call_target="tpu_custom_call" | custom-call | flops 1879048192 | bytes 16777216 | tf_op jit(solution)/shard_map/pallas_call | solution.py:115
  15.0 7.6 %all-to-all-start = ((bf16[32,528,256]{2,1,0:T(8,128)(2,1)}), bf16[32,528,256]{2,1,0:T(8,128)(2,1)}, u32[]{:S(2)}, u32[]{:S(2)}) async-start(bf16[32,528,256]{2,1,0:T(8,128)(2,1)} %shard_map.118), calls=%async_computation | async-start | bytes 17301504 | tf_op jit(solution)/shard_map/all_to_all | solution.py:540
  22.7 2.0 copy-done.1
  24.7 11.1 %shard_map.120 = bf16[32,512,256]{2,1,0:T(8,128)(2,1)} custom-call(s32[32]{0:T(128)S(1)} %get-tuple-element.31.source, s32[32]{0:T(128)S(1)} %fusion.2.filled, s32[28]{0:T(128)S(1)} %copy-done.7, bf16[28,256,256]{2,1,0:T(8,128)(2,1)S(1)} %copy-done.1, bf16[28,256,256]{2,1,0:T(8,128)(2,1)S(1)} %copy-done.1, bf16[28,256,256]{2,1,0:T(8,128)(2,1)S(1)} %copy-done.1, ...), custom_call_target="tpu_custom_call" | custom-call | flops 1879048192 | bytes 16777216 | tf_op jit(solution)/shard_map/pallas_call | solution.py:115
  35.8 87.7 %all-to-all-done.slots = bf16[32,528,256]{2,1,0:T(8,128)(2,1)} async-done(((bf16[32,528,256]{2,1,0:T(8,128)(2,1)}), bf16[32,528,256]{2,1,0:T(8,128)(2,1)}, u32[]{:S(2)}, u32[]{:S(2)}) %all-to-all-start) | async-done | bytes 8650784 | tf_op jit(solution)/shard_map/all_to_all | solution.py:540
  123.5 9.0 %all-to-all-start.1 = ((bf16[32,512,256]{2,1,0:T(8,128)(2,1)}), bf16[32,512,256]{2,1,0:T(8,128)(2,1)}, u32[]{:S(2)}, u32[]{:S(2)}) async-start(bf16[32,512,256]{2,1,0:T(8,128)(2,1)} %shard_map.120), calls=%async_computation.1 | async-start | bytes 16777216 | tf_op jit(solution)/shard_map/all_to_all | solution.py:540
  133.6 9.8 %shard_map.119.before = f32[2,768,768]{2,1,0:T(8,128)S(1)} custom-call(s32[32]{0:T(128)S(1)} %get-tuple-element.29.places, s32[4]{0:T(128)S(1)} %copy-done.8, f32[2,768,768]{2,1,0:T(8,128)} %bitcast.43, bf16[4,256,256]{2,1,0:T(8,128)(2,1)S(1)} %copy-done.4, bf16[4,256,256]{2,1,0:T(8,128)(2,1)S(1)} %copy-done.5, bf16[32,528,256]{2,1,0:T(8,128)(2,1)} %all-to-all-done.slots), custom_call_target="tpu_custom_call" | custom-call | flops 2147483648 | bytes 20971520 | tf_op jit(solution)/shard_map/pallas_call | solution.py:264
  143.4 2.1 copy-done.2
  145.5 83.8 %all-to-all-done.1.slots = bf16[32,512,256]{2,1,0:T(8,128)(2,1)} async-done(((bf16[32,512,256]{2,1,0:T(8,128)(2,1)}), bf16[32,512,256]{2,1,0:T(8,128)(2,1)}, u32[]{:S(2)}, u32[]{:S(2)}) %all-to-all-start.1) | async-done | bytes 8388640 | tf_op jit(solution)/shard_map/all_to_all | solution.py:540
  229.3 14.0 %shard_map.121 = (f32[2,768,768]{2,1,0:T(8,128)}, s16[4,208,512]{2,1,0:T(8,128)(2,1)S(1)}, s16[4,144,768]{2,1,0:T(8,128)(2,1)S(1)}) custom-call(s32[32]{0:T(128)S(1)} %get-tuple-element.30.places, s32[2]{0:T(128)S(1)} %pad_add_fusion.role, f32[2,768,768]{2,1,0:T(8,128)} %copy-done.2, bf16[32,512,256]{2,1,0:T(8,128)(2,1)} %all-to-all-done.1.slots, ...), custom_call_target="tpu_custom_call" | custom-call | flops 2147483648 | bytes 20971520 | tf_op jit(solution)/shard_map/pallas_call | solution.py:291
  248.8 12.1 %collective-permute-done.1 = s16[208,512]{1,0:T(8,128)(2,1)S(1)} collective-permute-done((s16[208,512]{1,0:T(8,128)(2,1)S(1)}, s16[208,512]{1,0:T(8,128)(2,1)S(1)}, u32[]{:S(2)}, u32[]{:S(2)}) %collective-permute-start.1) | collective-permute-done | bytes 213024 | tf_op jit(solution)/shard_map/ppermute | solution.py:486
  261.0 2.0 collective-permute-start.3
  266.4 4.9 %collective-permute-start.9 = (s16[144,768]{1,0:T(8,128)(2,1)S(1)}, s16[144,768]{1,0:T(8,128)(2,1)S(1)}, u32[]{:S(2)}, u32[]{:S(2)}) collective-permute-start(s16[144,768]{1,0:T(8,128)(2,1)S(1)} %bitcast_select_fusion.2.refs_4_), channel_id=1, source_target_pairs={{0,8},{4,12},{12,4},{1,9},{5,13},{13,5},{2,10},{6,14},{14,6},{3,11... | collective-permute-start | bytes 663560 | tf_op jit(solution)/shard_map/ppermute | solution.py:499
  271.3 5.8 %collective-permute-start.4 = (s16[208,512]{1,0:T(8,128)(2,1)S(1)}, s16[208,512]{1,0:T(8,128)(2,1)S(1)}, u32[]{:S(2)}, u32[]{:S(2)}) collective-permute-start(s16[208,512]{1,0:T(8,128)(2,1)S(1)} %bitcast_select_fusion.3.refs_0_), channel_id=1, source_target_pairs={{0,1},{1,2},{2,3},{4,5},{5,6},{6,7},{8,9},{9,10},{10,11},{12,13},{... | collective-permute-start | bytes 638984 | tf_op jit(solution)/shard_map/ppermute | solution.py:499
  278.4 5.2 %collective-permute-done.4.refs_2_ = s16[208,512]{1,0:T(8,128)(2,1)S(1)} collective-permute-done((s16[208,512]{1,0:T(8,128)(2,1)S(1)}, s16[208,512]{1,0:T(8,128)(2,1)S(1)}, u32[]{:S(2)}, u32[]{:S(2)}) %collective-permute-start.4) | collective-permute-done | bytes 213024 | tf_op jit(solution)/shard_map/ppermute | solution.py:499
  283.6 2.5 collective-permute-done.5.refs_3_
  286.1 9.2 %shard_map.122 = (f32[2,768,768]{2,1,0:T(8,128)}, s16[4,208,1024]{2,1,0:T(8,128)(2,1)S(1)}, s16[4,272,768]{2,1,0:T(8,128)(2,1)S(1)}) custom-call(s32[2]{0:T(128)S(1)} %pad_add_fusion.role, f32[2,768,768]{2,1,0:T(8,128)} %get-tuple-element.11.block, s16[208,512]{1,0:T(8,128)(2,1)S(1)} %bitcast_select_fusion.3.refs_0_, ...), custom_call_target="tpu_custom_call", output_to_operand_aliasing={{0}: (1, {})} | custom-call | tf_op jit(solution)/shard_map/pallas_call | solution.py:427
  301.0 15.2 %collective-permute-done.19 = s16[272,768]{1,0:T(8,128)(2,1)S(1)} collective-permute-done((s16[272,768]{1,0:T(8,128)(2,1)S(1)}, s16[272,768]{1,0:T(8,128)(2,1)S(1)}, u32[]{:S(2)}, u32[]{:S(2)}) %collective-permute-start.19) | collective-permute-done | bytes 417824 | tf_op jit(solution)/shard_map/ppermute | solution.py:486
  318.4 3.2 collective-permute-done.13
  327.0 4.4 %collective-permute-start.22 = (s16[272,768]{1,0:T(8,128)(2,1)S(1)}, s16[272,768]{1,0:T(8,128)(2,1)S(1)}, u32[]{:S(2)}, u32[]{:S(2)}) collective-permute-start(s16[272,768]{1,0:T(8,128)(2,1)S(1)} %bitcast_select_fusion.1.refs_4_), channel_id=1, source_target_pairs={{0,4},{4,8},{8,12},{1,5},{5,9},{9,13},{2,6},{6,10},{10,14},{3,7},{... | collective-permute-start | bytes 1253384 | tf_op jit(solution)/shard_map/ppermute | solution.py:499
  333.2 7.7 %collective-permute-done.22.refs_6_ = s16[272,768]{1,0:T(8,128)(2,1)S(1)} collective-permute-done((s16[272,768]{1,0:T(8,128)(2,1)S(1)}, s16[272,768]{1,0:T(8,128)(2,1)S(1)}, u32[]{:S(2)}, u32[]{:S(2)}) %collective-permute-start.22) | collective-permute-done | bytes 417824 | tf_op jit(solution)/shard_map/ppermute | solution.py:499
  340.9 4.1 %collective-permute-done.23.refs_7_ = s16[272,768]{1,0:T(8,128)(2,1)S(1)} collective-permute-done((s16[272,768]{1,0:T(8,128)(2,1)S(1)}, s16[272,768]{1,0:T(8,128)(2,1)S(1)}, u32[]{:S(2)}, u32[]{:S(2)}) %collective-permute-start.23) | collective-permute-done | bytes 417824 | tf_op jit(solution)/shard_map/ppermute | solution.py:499
  346.2 12.8 %shard_map.123 = f32[2,768,768]{2,1,0:T(8,128)} custom-call(s32[2]{0:T(128)S(1)} %pad_add_fusion.role, f32[2,768,768]{2,1,0:T(8,128)} %get-tuple-element.14.block, s16[208,1024]{1,0:T(8,128)(2,1)S(1)} %bitcast_select_fusion.refs_0_, s16[208,1024]{1,0:T(8,128)(2,1)S(1)} %collective-permute-done.15.refs_1_, ...), custom_call_target="tpu_custom_call", output_to_operand_aliasing={{}: (1, {})} | custom-call | tf_op jit(solution)/shard_map/pallas_call | solution.py:472
  (73 shorter events, 31.7 us)
Async XLA Ops:
  15.0 108.4 %all-to-all-start = ((bf16[32,528,256]{2,1,0:T(8,128)(2,1)}), bf16[32,528,256]{2,1,0:T(8,128)(2,1)}, u32[]{:S(2)}, u32[]{:S(2)}) async-start(bf16[32,528,256]{2,1,0:T(8,128)(2,1)} %shard_map.118), calls=%async_computation | async-start | bytes 17301504 | tf_op jit(solution)/shard_map/all_to_all | solution.py:540
  123.5 105.8 %all-to-all-start.1 = ((bf16[32,512,256]{2,1,0:T(8,128)(2,1)}), bf16[32,512,256]{2,1,0:T(8,128)(2,1)}, u32[]{:S(2)}, u32[]{:S(2)}) async-start(bf16[32,512,256]{2,1,0:T(8,128)(2,1)} %shard_map.120), calls=%async_computation.1 | async-start | bytes 16777216 | tf_op jit(solution)/shard_map/all_to_all | solution.py:540
  244.1 16.8 %collective-permute-start.1 = (s16[208,512]{1,0:T(8,128)(2,1)S(1)}, s16[208,512]{1,0:T(8,128)(2,1)S(1)}, u32[]{:S(2)}, u32[]{:S(2)}) collective-permute-start(s16[208,512]{1,0:T(8,128)(2,1)S(1)} %get-tuple-element.27), channel_id=1, source_target_pairs={{0,1},{4,5},{8,9},{12,13},{16,17},{20,21},{24,25},{28,29},{32,33},... | collective-permute-start | bytes 638984 | tf_op jit(solution)/shard_map/ppermute | solution.py:486
  245.4 15.5 %collective-permute-start.2 = (s16[208,512]{1,0:T(8,128)(2,1)S(1)}, s16[208,512]{1,0:T(8,128)(2,1)S(1)}, u32[]{:S(2)}, u32[]{:S(2)}) collective-permute-start(s16[208,512]{1,0:T(8,128)(2,1)S(1)} %get-tuple-element.26), channel_id=1, source_target_pairs={{0,3},{4,7},{8,11},{12,15},{16,19},{20,23},{24,27},{28,31},{32,35}... | collective-permute-start | bytes 638984 | tf_op jit(solution)/shard_map/ppermute | solution.py:486
  246.1 16.9 %collective-permute-start.6 = (s16[144,768]{1,0:T(8,128)(2,1)S(1)}, s16[144,768]{1,0:T(8,128)(2,1)S(1)}, u32[]{:S(2)}, u32[]{:S(2)}) collective-permute-start(s16[144,768]{1,0:T(8,128)(2,1)S(1)} %get-tuple-element.25), channel_id=1, source_target_pairs={{0,8},{1,9},{2,10},{3,11},{16,24},{17,25},{18,26},{19,27},{32,40},... | collective-permute-start | bytes 663560 | tf_op jit(solution)/shard_map/ppermute | solution.py:486
  246.8 16.2 %collective-permute-start.7 = (s16[144,768]{1,0:T(8,128)(2,1)S(1)}, s16[144,768]{1,0:T(8,128)(2,1)S(1)}, u32[]{:S(2)}, u32[]{:S(2)}) collective-permute-start(s16[144,768]{1,0:T(8,128)(2,1)S(1)} %get-tuple-element.24), channel_id=1, source_target_pairs={{0,4},{1,5},{2,6},{3,7},{16,20},{17,21},{18,22},{19,23},{32,36},{3... | collective-permute-start | bytes 663560 | tf_op jit(solution)/shard_map/ppermute | solution.py:486
  248.1 14.9 %collective-permute-start.8 = (s16[144,768]{1,0:T(8,128)(2,1)S(1)}, s16[144,768]{1,0:T(8,128)(2,1)S(1)}, u32[]{:S(2)}, u32[]{:S(2)}) collective-permute-start(s16[144,768]{1,0:T(8,128)(2,1)S(1)} %get-tuple-element.23), channel_id=1, source_target_pairs={{0,12},{1,13},{2,14},{3,15},{16,28},{17,29},{18,30},{19,31},{32,44... | collective-permute-start | bytes 663560 | tf_op jit(solution)/shard_map/ppermute | solution.py:486
  261.0 16.1 %collective-permute-start.3 = (s16[208,512]{1,0:T(8,128)(2,1)S(1)}, s16[208,512]{1,0:T(8,128)(2,1)S(1)}, u32[]{:S(2)}, u32[]{:S(2)}) collective-permute-start(s16[208,512]{1,0:T(8,128)(2,1)S(1)} %bitcast_select_fusion.3.refs_0_), channel_id=1, source_target_pairs={{0,2},{1,3},{3,1},{4,6},{5,7},{7,5},{8,10},{9,11},{11,9},{12,14},{... | collective-permute-start | bytes 638984 | tf_op jit(solution)/shard_map/ppermute | solution.py:499
  263.2 22.9 %collective-permute-start.10 = (s16[144,768]{1,0:T(8,128)(2,1)S(1)}, s16[144,768]{1,0:T(8,128)(2,1)S(1)}, u32[]{:S(2)}, u32[]{:S(2)}) collective-permute-start(s16[144,768]{1,0:T(8,128)(2,1)S(1)} %bitcast_select_fusion.2.refs_4_), channel_id=1, source_target_pairs={{0,4},{4,8},{8,12},{1,5},{5,9},{9,13},{2,6},{6,10},{10,14},{3,7},{... | collective-permute-start | bytes 663560 | tf_op jit(solution)/shard_map/ppermute | solution.py:499
  265.1 21.0 %collective-permute-start.11 = (s16[144,768]{1,0:T(8,128)(2,1)S(1)}, s16[144,768]{1,0:T(8,128)(2,1)S(1)}, u32[]{:S(2)}, u32[]{:S(2)}) collective-permute-start(s16[144,768]{1,0:T(8,128)(2,1)S(1)} %bitcast_select_fusion.2.refs_4_), channel_id=1, source_target_pairs={{0,12},{8,4},{12,8},{1,13},{9,5},{13,9},{2,14},{10,6},{14,10},{3,1... | collective-permute-start | bytes 663560 | tf_op jit(solution)/shard_map/ppermute | solution.py:499
  266.4 19.7 %collective-permute-start.9 = (s16[144,768]{1,0:T(8,128)(2,1)S(1)}, s16[144,768]{1,0:T(8,128)(2,1)S(1)}, u32[]{:S(2)}, u32[]{:S(2)}) collective-permute-start(s16[144,768]{1,0:T(8,128)(2,1)S(1)} %bitcast_select_fusion.2.refs_4_), channel_id=1, source_target_pairs={{0,8},{4,12},{12,4},{1,9},{5,13},{13,5},{2,10},{6,14},{14,6},{3,11... | collective-permute-start | bytes 663560 | tf_op jit(solution)/shard_map/ppermute | solution.py:499
  271.3 12.3 %collective-permute-start.4 = (s16[208,512]{1,0:T(8,128)(2,1)S(1)}, s16[208,512]{1,0:T(8,128)(2,1)S(1)}, u32[]{:S(2)}, u32[]{:S(2)}) collective-permute-start(s16[208,512]{1,0:T(8,128)(2,1)S(1)} %bitcast_select_fusion.3.refs_0_), channel_id=1, source_target_pairs={{0,1},{1,2},{2,3},{4,5},{5,6},{6,7},{8,9},{9,10},{10,11},{12,13},{... | collective-permute-start | bytes 638984 | tf_op jit(solution)/shard_map/ppermute | solution.py:499
  277.1 9.0 %collective-permute-start.5 = (s16[208,512]{1,0:T(8,128)(2,1)S(1)}, s16[208,512]{1,0:T(8,128)(2,1)S(1)}, u32[]{:S(2)}, u32[]{:S(2)}) collective-permute-start(s16[208,512]{1,0:T(8,128)(2,1)S(1)} %bitcast_select_fusion.3.refs_0_), channel_id=1, source_target_pairs={{0,3},{2,1},{3,2},{4,7},{6,5},{7,6},{8,11},{10,9},{11,10},{12,15},... | collective-permute-start | bytes 638984 | tf_op jit(solution)/shard_map/ppermute | solution.py:499
  296.2 20.0 %collective-permute-start.19 = (s16[272,768]{1,0:T(8,128)(2,1)S(1)}, s16[272,768]{1,0:T(8,128)(2,1)S(1)}, u32[]{:S(2)}, u32[]{:S(2)}) collective-permute-start(s16[272,768]{1,0:T(8,128)(2,1)S(1)} %get-tuple-element.21), channel_id=1, source_target_pairs={{0,4},{1,5},{2,6},{3,7},{16,20},{17,21},{18,22},{19,23},{32,36},{3... | collective-permute-start | bytes 1253384 | tf_op jit(solution)/shard_map/ppermute | solution.py:486
  297.5 18.7 %collective-permute-start.20 = (s16[272,768]{1,0:T(8,128)(2,1)S(1)}, s16[272,768]{1,0:T(8,128)(2,1)S(1)}, u32[]{:S(2)}, u32[]{:S(2)}) collective-permute-start(s16[272,768]{1,0:T(8,128)(2,1)S(1)} %get-tuple-element.20), channel_id=1, source_target_pairs={{0,12},{1,13},{2,14},{3,15},{16,28},{17,29},{18,30},{19,31},{32,44... | collective-permute-start | bytes 1253384 | tf_op jit(solution)/shard_map/ppermute | solution.py:486
  298.2 20.1 %collective-permute-start.12 = (s16[208,1024]{1,0:T(8,128)(2,1)S(1)}, s16[208,1024]{1,0:T(8,128)(2,1)S(1)}, u32[]{:S(2)}, u32[]{:S(2)}) collective-permute-start(s16[208,1024]{1,0:T(8,128)(2,1)S(1)} %get-tuple-element.19), channel_id=1, source_target_pairs={{0,2},{4,6},{8,10},{12,14},{16,18},{20,22},{24,26},{28,30},{32,34}... | collective-permute-start | bytes 1277960 | tf_op jit(solution)/shard_map/ppermute | solution.py:486
  298.9 22.6 %collective-permute-start.13 = (s16[208,1024]{1,0:T(8,128)(2,1)S(1)}, s16[208,1024]{1,0:T(8,128)(2,1)S(1)}, u32[]{:S(2)}, u32[]{:S(2)}) collective-permute-start(s16[208,1024]{1,0:T(8,128)(2,1)S(1)} %get-tuple-element.18), channel_id=1, source_target_pairs={{0,1},{4,5},{8,9},{12,13},{16,17},{20,21},{24,25},{28,29},{32,33},... | collective-permute-start | bytes 1277960 | tf_op jit(solution)/shard_map/ppermute | solution.py:486
  300.3 21.3 %collective-permute-start.14 = (s16[208,1024]{1,0:T(8,128)(2,1)S(1)}, s16[208,1024]{1,0:T(8,128)(2,1)S(1)}, u32[]{:S(2)}, u32[]{:S(2)}) collective-permute-start(s16[208,1024]{1,0:T(8,128)(2,1)S(1)} %get-tuple-element.17), channel_id=1, source_target_pairs={{0,3},{4,7},{8,11},{12,15},{16,19},{20,23},{24,27},{28,31},{32,35}... | collective-permute-start | bytes 1277960 | tf_op jit(solution)/shard_map/ppermute | solution.py:486
  316.4 15.5 %collective-permute-start.21 = (s16[272,768]{1,0:T(8,128)(2,1)S(1)}, s16[272,768]{1,0:T(8,128)(2,1)S(1)}, u32[]{:S(2)}, u32[]{:S(2)}) collective-permute-start(s16[272,768]{1,0:T(8,128)(2,1)S(1)} %bitcast_select_fusion.1.refs_4_), channel_id=1, source_target_pairs={{0,8},{4,12},{12,4},{1,9},{5,13},{13,5},{2,10},{6,14},{14,6},{3,11... | collective-permute-start | bytes 1253384 | tf_op jit(solution)/shard_map/ppermute | solution.py:499
  321.8 23.2 %collective-permute-start.15 = (s16[208,1024]{1,0:T(8,128)(2,1)S(1)}, s16[208,1024]{1,0:T(8,128)(2,1)S(1)}, u32[]{:S(2)}, u32[]{:S(2)}) collective-permute-start(s16[208,1024]{1,0:T(8,128)(2,1)S(1)} %bitcast_select_fusion.refs_0_), channel_id=1, source_target_pairs={{0,2},{1,3},{3,1},{4,6},{5,7},{7,5},{8,10},{9,11},{11,9},{12,14},{... | collective-permute-start | bytes 1277960 | tf_op jit(solution)/shard_map/ppermute | solution.py:499
  323.7 21.3 %collective-permute-start.16 = (s16[208,1024]{1,0:T(8,128)(2,1)S(1)}, s16[208,1024]{1,0:T(8,128)(2,1)S(1)}, u32[]{:S(2)}, u32[]{:S(2)}) collective-permute-start(s16[208,1024]{1,0:T(8,128)(2,1)S(1)} %bitcast_select_fusion.refs_0_), channel_id=1, source_target_pairs={{0,1},{1,2},{2,3},{4,5},{5,6},{6,7},{8,9},{9,10},{10,11},{12,13},{... | collective-permute-start | bytes 1277960 | tf_op jit(solution)/shard_map/ppermute | solution.py:499
  325.7 20.5 %collective-permute-start.17 = (s16[208,1024]{1,0:T(8,128)(2,1)S(1)}, s16[208,1024]{1,0:T(8,128)(2,1)S(1)}, u32[]{:S(2)}, u32[]{:S(2)}) collective-permute-start(s16[208,1024]{1,0:T(8,128)(2,1)S(1)} %bitcast_select_fusion.refs_0_), channel_id=1, source_target_pairs={{0,3},{2,1},{3,2},{4,7},{6,5},{7,6},{8,11},{10,9},{11,10},{12,15},... | collective-permute-start | bytes 1277960 | tf_op jit(solution)/shard_map/ppermute | solution.py:499
  327.0 13.9 %collective-permute-start.22 = (s16[272,768]{1,0:T(8,128)(2,1)S(1)}, s16[272,768]{1,0:T(8,128)(2,1)S(1)}, u32[]{:S(2)}, u32[]{:S(2)}) collective-permute-start(s16[272,768]{1,0:T(8,128)(2,1)S(1)} %bitcast_select_fusion.1.refs_4_), channel_id=1, source_target_pairs={{0,4},{4,8},{8,12},{1,5},{5,9},{9,13},{2,6},{6,10},{10,14},{3,7},{... | collective-permute-start | bytes 1253384 | tf_op jit(solution)/shard_map/ppermute | solution.py:499
  331.9 13.2 %collective-permute-start.23 = (s16[272,768]{1,0:T(8,128)(2,1)S(1)}, s16[272,768]{1,0:T(8,128)(2,1)S(1)}, u32[]{:S(2)}, u32[]{:S(2)}) collective-permute-start(s16[272,768]{1,0:T(8,128)(2,1)S(1)} %bitcast_select_fusion.1.refs_4_), channel_id=1, source_target_pairs={{0,12},{8,4},{12,8},{1,13},{9,5},{13,9},{2,14},{10,6},{14,10},{3,1... | collective-permute-start | bytes 1253384 | tf_op jit(solution)/shard_map/ppermute | solution.py:499
  (11 other events, 413.0 us)

commit v3 on v2

v3 whole, which is shorter than its diff:
```python
import functools
import math

import jax
import jax.numpy as jnp
from jax import lax
from jax.experimental import pallas as pl
from jax.experimental.pallas import tpu as pltpu
from jax.sharding import PartitionSpec as P

TILE = 256
RANK = 128
TS = 3
SIDE = TS * TILE
SENT = 28
GROUP = 32
RING = 4
CODE_ROWS = 16
NOTE_ROWS = 16
LOG_STEP = math.log(2.0) / 32.0
VMEM_BYTES = 32 * 1024 * 1024
MORE_VMEM_BYTES = 45 * 1024 * 1024
ALL_VMEM_BYTES = 60 * 1024 * 1024
DEPTH = 4
BF16 = jnp.bfloat16
F32 = jnp.float32
IN_HBM = pl.BlockSpec(memory_space=pltpu.HBM)
HELD = pl.BlockSpec(memory_space=pltpu.VMEM)
SCALAR = pl.BlockSpec(memory_space=pltpu.SMEM)


def encode(values):
    peak = jnp.maximum(jnp.max(jnp.abs(values), axis=0, keepdims=True), 1e-30)
    code = jnp.ceil(jnp.log(peak * (1.0 / 32700.0)) * (1.0 / LOG_STEP))
    whole = jnp.round(values * jnp.exp(code * -LOG_STEP))
    whole = jnp.clip(whole, -32767.0, 32767.0).astype(jnp.int32)
    code_rows = jnp.broadcast_to(code.astype(jnp.int32), (CODE_ROWS, values.shape[1]))
    return whole.astype(jnp.int16), code_rows.astype(jnp.int16)


def store_piece(ref, values):
    rows = values.shape[0]
    whole, code_rows = encode(values)
    ref[:rows, :] = whole
    ref[rows:, :] = code_rows


def decode(piece_rows, code_rows):
    code = code_rows[:1].astype(jnp.int32).astype(F32)
    return piece_rows.astype(jnp.int32).astype(F32) * jnp.exp(code * LOG_STEP)


def cut(x):
    high = x.astype(BF16)
    return high, (x - high.astype(F32)).astype(BF16)


def dot(a, b):
    return lax.dot_general(a, b, (((1,), (0,)), ((), ())), preferred_element_type=F32)


def dot_cut(a, b):
    return dot(a[0], b[0]) + (dot(a[0], b[1]) + dot(a[1], b[0]))


def cuts(pair):
    return [cut(x) for x in pair]


def complex_dot(a, b):
    return (
        dot_cut(a[0], b[0]) - dot_cut(a[1], b[1]),
        dot_cut(a[0], b[1]) + dot_cut(a[1], b[0]),
    )


def minus(a, b):
    return a[0] - b[0], a[1] - b[1]


def pack_kernel(
    second, destination, place, ranks, left, right, rows, cols, out, *scratch
):
    number, order, lefts, rights, packed, notes, sem_in, sem_out, sem_notes = scratch

    def clear(d, carry):
        number[0, d] = -1
        number[1, d] = -1
        return carry

    lax.fori_loop(0, GROUP, clear, 0)

    def sort(k, count):
        d = destination[k]
        later = (number[0, d] >= 0).astype(jnp.int32)
        number[later, d] = k
        mine = later == second

        @pl.when(mine)
        def _():
            order[count] = k

        return count + mine.astype(jnp.int32)

    count = lax.fori_loop(0, SENT, sort, 0)

    def fetch(p, slot):
        k = order[p]
        return (
            pltpu.make_async_copy(left.at[k], lefts.at[slot], sem_in.at[slot, 0]),
            pltpu.make_async_copy(right.at[k], rights.at[slot], sem_in.at[slot, 1]),
        )

    def store(d, slot):
        target = out.at[d, pl.ds(0, TILE + 2 * RANK)]
        return pltpu.make_async_copy(packed.at[slot], target, sem_out.at[slot])

    for slot in range(DEPTH):

        @pl.when(slot < count)
        def _(slot=slot):
            for copy in fetch(slot, slot):
                copy.start()

    if second:
        line = lax.broadcasted_iota(jnp.int32, (NOTE_ROWS, TILE), 0)

        def note(d, carry):
            def code(which):
                k = number[which, d]
                return jnp.where(k >= 0, place[jnp.maximum(k, 0)], -1)

            lines = jnp.where(line == 0, code(1), code(0))
            notes[d] = lines.astype(F32).astype(BF16)
            return carry

        lax.fori_loop(0, GROUP, note, 0)
        tell = pltpu.make_async_copy(
            notes, out.at[:, pl.ds(TILE + 2 * RANK, NOTE_ROWS)], sem_notes
        )
        tell.start()

    index = lax.broadcasted_iota(jnp.int32, (TILE, TILE), 0)
    width = lax.broadcasted_iota(jnp.int32, (TILE, 2 * RANK), 1)
    width = jnp.where(width >= RANK, width - RANK, width)
    turned = (((0,), (0,)), ((), ()))

    def onehot(chosen):
        return jnp.where(index == chosen, 1.0, 0.0).astype(BF16)

    def work(p, carry):
        slot = p & (DEPTH - 1)
        k = order[p]
        for copy in fetch(p, slot):
            copy.wait()

        @pl.when(p >= DEPTH)
        def _():
            store(0, slot).wait()

        moved = lax.dot_general(
            onehot(rows[pl.ds(k, 1), :]), lefts[slot], turned, preferred_element_type=F32
        )
        packed[slot, :TILE, :] = jnp.where(width < ranks[k], moved, 0.0).astype(BF16)
        packed[slot, TILE:, :] = lax.dot_general(
            rights[slot], onehot(cols[pl.ds(k, 1), :]), turned, preferred_element_type=F32
        ).astype(BF16)
        store(destination[k], slot).start()

        @pl.when(p + DEPTH < count)
        def _():
            for copy in fetch(p + DEPTH, slot):
                copy.start()

        return carry

    lax.fori_loop(0, count, work, 0)
    for slot in range(DEPTH):

        @pl.when(slot < count)
        def _(slot=slot):
            store(0, slot).wait()

    if second:
        tell.wait()


def pack(second, destination, place, ranks, left, right, rows, cols):
    depth = TILE + 2 * RANK + (NOTE_ROWS if second else 0)
    tiles = pltpu.VMEM((DEPTH, TILE, 2 * RANK), BF16)
    return pl.pallas_call(
        functools.partial(pack_kernel, second),
        in_specs=[SCALAR] * 3 + [IN_HBM] * 2 + [HELD] * 2,
        out_specs=IN_HBM,
        out_shape=jax.ShapeDtypeStruct((GROUP, depth, TILE), BF16),
        scratch_shapes=[
            pltpu.SMEM((2, GROUP), jnp.int32),
            pltpu.SMEM((SENT,), jnp.int32),
            tiles,
            tiles,
            pltpu.VMEM((DEPTH, TILE + 2 * RANK, TILE), BF16),
            pltpu.VMEM((GROUP, NOTE_ROWS, TILE), BF16),
            pltpu.SemaphoreType.DMA((DEPTH, 2)),
            pltpu.SemaphoreType.DMA((DEPTH,)),
            pltpu.SemaphoreType.DMA,
        ],
        compiler_params=pltpu.CompilerParams(vmem_limit_bytes=ALL_VMEM_BYTES),
        cost_estimate=pl.CostEstimate(
            flops=4 * SENT * TILE**3, bytes_accessed=16 * 2**20, transcendentals=0
        ),
    )(destination, place, ranks, left, right, rows, cols)


def add_at(out, place, real, imag):
    a = place // TS
    rows = pl.ds(pl.multiple_of(a * TILE, TILE), TILE)
    cols = pl.ds(pl.multiple_of((place - a * TS) * TILE, TILE), TILE)
    out[0, rows, cols] += real
    out[1, rows, cols] += imag


def add_own(out, place, left, right):
    real_side = jnp.concatenate([right[:, :RANK], -right[:, RANK:]], 1)
    imag_side = jnp.concatenate([right[:, RANK:], right[:, :RANK]], 1)
    contract = (((1,), (1,)), ((), ()))
    add_at(
        out,
        place,
        lax.dot_general(left, real_side, contract, preferred_element_type=F32),
        lax.dot_general(left, imag_side, contract, preferred_element_type=F32),
    )


def add_slots(out, places, slots, scratch, prepare):
    order, arrived, sems = scratch

    def sort(slot, count):
        mine = places[slot] >= 0

        @pl.when(mine)
        def _():
            order[count] = slot

        return count + mine.astype(jnp.int32)

    count = lax.fori_loop(0, GROUP, sort, 0)

    def fetch(p, held):
        source = slots.at[order[p], pl.ds(0, TILE + 2 * RANK)]
        return pltpu.make_async_copy(source, arrived.at[held], sems.at[held])

    for p in range(DEPTH):

        @pl.when(p < count)
        def _(p=p):
            fetch(p, p).start()

    prepare()

    def work(p, carry):
        held = p & (DEPTH - 1)
        fetch(p, held).wait()
        left = arrived[held, :TILE, :]
        top = arrived[held, TILE : TILE + RANK, :]
        bottom = arrived[held, TILE + RANK :, :]
        add_at(
            out,
            places[order[p]],
            dot(left, jnp.concatenate([top, -bottom], 0)),
            dot(left, jnp.concatenate([bottom, top], 0)),
        )

        @pl.when(p + DEPTH < count)
        def _():
            fetch(p + DEPTH, held).start()

        return carry

    lax.fori_loop(0, count, work, 0)


def add_scratch():
    return [
        pltpu.SMEM((GROUP,), jnp.int32),
        pltpu.VMEM((DEPTH, TILE + 2 * RANK, TILE), BF16),
        pltpu.SemaphoreType.DMA((DEPTH,)),
    ]


def first_kernel(places, own_places, before, own_left, own_right, slots, out, *scratch):
    def prepare():
        pltpu.sync_copy(before, out)

        def own_step(j, carry):
            add_own(out, own_places[j], own_left[j], own_right[j])
            return carry

        lax.fori_loop(0, own_left.shape[0], own_step, 0)

    add_slots(out, places, slots, scratch, prepare)


def tile_at(i, j):
    return slice(i * TILE, (i + 1) * TILE), slice(j * TILE, (j + 1) * TILE)


def get(ref, rows, cols):
    return ref[0, rows, cols], ref[1, rows, cols]


def put(ref, rows, cols, value):
    ref[0, rows, cols] = value[0]
    ref[1, rows, cols] = value[1]


def second_kernel(places, role, before, slots, inverse, out, *refs):
    along_row, along_col = refs[:RING], refs[RING : 2 * RING]

    def prepare():
        out[...] = before[...]

    add_slots(out, places, slots, refs[2 * RING :], prepare)
    long, short = SIDE // RING, 2 * TILE // RING

    @pl.when((role[0] == 0) & (role[1] == 0))
    def _():
        pivots = [cuts((inverse[p, 0], inverse[p, 1])) for p in range(TS)]
        for p in range(TS - 1):
            uppers = {j: cuts(get(out, *tile_at(p, j))) for j in range(p + 1, TS)}
            for i in range(p + 1, TS):
                factor = complex_dot(cuts(get(out, *tile_at(i, p))), pivots[p])
                put(out, *tile_at(i, p), factor)
                factor = cuts(factor)
                for j in range(p + 1, TS):
                    at = tile_at(i, j)
                    put(out, *at, minus(get(out, *at), complex_dot(factor, uppers[j])))
        lower = [get(out, *tile_at(i, j)) for i, j in ((1, 0), (2, 0), (2, 1))]
        lower = jnp.concatenate([jnp.concatenate(x, 1) for x in lower], 0)
        upper = [
            complex_dot(cuts(get(out, *tile_at(i, j))), pivots[j])
            for i, j in ((0, 1), (0, 2), (1, 2))
        ]
        upper = [jnp.concatenate([x[half] for x in upper], 1) for half in (0, 1)]
        for piece in range(RING):
            store_piece(along_row[piece], lower[piece * long : (piece + 1) * long])
            half, start = divmod(piece * short, TILE)
            store_piece(along_col[piece], upper[half][start : start + short])

    @pl.when((role[0] > 0) & (role[1] == 0))
    def _():
        for p in range(TS):
            pivot = cuts((inverse[p, 0], inverse[p, 1]))
            for i in range(TS):
                at = tile_at(i, p)
                put(out, *at, complex_dot(cuts(get(out, *at)), pivot))
        for piece in range(RING):
            rows = slice(piece * long, (piece + 1) * long)
            store_piece(along_row[piece], jnp.concatenate(get(out, rows, slice(0, TILE)), 1))

    @pl.when((role[0] == 0) & (role[1] > 0))
    def _():
        for piece in range(RING):
            half, start = divmod(piece * short, TILE)
            store_piece(along_col[piece], out[half, start : start + short, :])


ADD_COST = pl.CostEstimate(
    flops=4 * GROUP * TILE**3, bytes_accessed=20 * 2**20, transcendentals=0
)


def add_first(places, own_places, before, own_left, own_right, slots):
    return pl.pallas_call(
        first_kernel,
        in_specs=[SCALAR, SCALAR, IN_HBM, HELD, HELD, IN_HBM],
        out_specs=HELD,
        out_shape=jax.ShapeDtypeStruct(before.shape, F32),
        scratch_shapes=add_scratch(),
        compiler_params=pltpu.CompilerParams(vmem_limit_bytes=MORE_VMEM_BYTES),
        cost_estimate=ADD_COST,
    )(places, own_places, before, own_left, own_right, slots)


def row_shape(panels):
    return (SIDE // RING + CODE_ROWS, 2 * TILE * panels)


def col_shape(panels):
    return (2 * TILE * panels // RING + CODE_ROWS, SIDE)


def coded(shape):
    return jax.ShapeDtypeStruct(shape, jnp.int16)


def pieces_of(panels):
    return [coded(row_shape(panels))] * RING + [coded(col_shape(panels))] * RING


def add_second(places, role, before, slots, inverse):
    return pl.pallas_call(
        second_kernel,
        in_specs=[SCALAR, SCALAR, HELD, IN_HBM, HELD],
        out_specs=[HELD] * (1 + 2 * RING),
        out_shape=[jax.ShapeDtypeStruct(before.shape, F32)] + pieces_of(1),
        scratch_shapes=add_scratch(),
        compiler_params=pltpu.CompilerParams(vmem_limit_bytes=MORE_VMEM_BYTES),
        cost_estimate=ADD_COST,
    )(places, role, before, slots, inverse)


def unpack(refs, place, high, low):
    rows = refs[0].shape[0] - CODE_ROWS
    for ref, shift in zip(refs, (0, 2, RING - 1, 1)):
        at = ((place + shift) & (RING - 1)) * rows
        h, l = cut(decode(ref[:rows, :], ref[rows:, :]))
        high[pl.ds(pl.multiple_of(at, 16), rows), :] = h
        low[pl.ds(pl.multiple_of(at, 16), rows), :] = l


def trailing(block, out, rows, left, right):
    panels = left[0].shape[1] // (2 * TILE)

    def turned(x, imag):
        parts = []
        for p in range(panels):
            a = x[rows, 2 * p * TILE : (2 * p + 1) * TILE]
            b = x[rows, (2 * p + 1) * TILE : (2 * p + 2) * TILE]
            parts += [b, a] if imag else [a, -b]
        return jnp.concatenate(parts, 1)

    for half in (0, 1):
        a = [turned(x, half == 1) for x in left]
        for j in range(TS):
            cols = slice(j * TILE, (j + 1) * TILE)
            product = dot_cut(a, [x[:, cols] for x in right])
            out[half, rows, cols] = block[half, rows, cols] - product


def piece_scratch(panels):
    return [pltpu.VMEM((SIDE, 2 * TILE * panels), BF16)] * 2 + [
        pltpu.VMEM((2 * TILE * panels, SIDE), BF16)
    ] * 2


def panel_kernel(role, block, *refs):
    from_row, from_col = refs[:RING], refs[RING : 2 * RING]
    out, along_row, along_col = (
        refs[2 * RING],
        refs[2 * RING + 1 : 3 * RING + 1],
        refs[3 * RING + 1 : 4 * RING + 1],
    )
    row_high, row_low, col_high, col_low = refs[4 * RING + 1 :]
    parts = [slice(t * TILE, (t + 1) * TILE) for t in range(TS)]

    @pl.when(role[1] > 0)
    def _():
        unpack(from_row, role[1], row_high, row_low)

    @pl.when(role[0] > 0)
    def _():
        unpack(from_col, role[0], col_high, col_low)

    @pl.when((role[0] == 0) & (role[1] == 0))
    def _():
        out[...] = block[...]

    @pl.when((role[0] > 0) & (role[1] == 0))
    def _():
        def tile(t):
            return [(col_high[rows, parts[t]], col_low[rows, parts[t]]) for rows in parts[:2]]

        def chunk(i, carry):
            rows = pl.ds(pl.multiple_of(i * TILE, TILE), TILE)
            f0 = get(block, rows, parts[0])
            put(out, rows, parts[0], f0)
            f0 = cuts(f0)
            f1 = minus(get(block, rows, parts[1]), complex_dot(f0, tile(0)))
            put(out, rows, parts[1], f1)
            f2 = minus(get(block, rows, parts[2]), complex_dot(f0, tile(1)))
            put(out, rows, parts[2], minus(f2, complex_dot(cuts(f1), tile(2))))
            return carry

        lax.fori_loop(0, TS, chunk, 0)
        part = SIDE // RING
        for piece in range(RING):
            rows = slice(piece * part, (piece + 1) * part)
            wide = [x for cols in parts[1:] for x in get(out, rows, cols)]
            store_piece(along_row[piece], jnp.concatenate(wide, 1))

    @pl.when((role[0] == 0) & (role[1] > 0))
    def _():
        def tile(t):
            return [(row_high[parts[t], cols], row_low[parts[t], cols]) for cols in parts[:2]]

        def chunk(j, carry):
            cols = pl.ds(pl.multiple_of(j * TILE, TILE), TILE)
            p0 = get(block, parts[0], cols)
            put(out, parts[0], cols, p0)
            p0 = cuts(p0)
            p1 = minus(get(block, parts[1], cols), complex_dot(tile(0), p0))
            put(out, parts[1], cols, p1)
            p2 = minus(get(block, parts[2], cols), complex_dot(tile(1), p0))
            put(out, parts[2], cols, minus(p2, complex_dot(tile(2), cuts(p1))))
            return carry

        lax.fori_loop(0, TS, chunk, 0)
        for piece in range(RING):
            at, half = divmod(piece, 2)
            store_piece(along_col[piece], out[half, parts[at + 1], :])

    @pl.when((role[0] > 0) & (role[1] > 0))
    def _():
        def chunk(i, carry):
            rows = pl.ds(pl.multiple_of(i * TILE, TILE), TILE)
            trailing(block, out, rows, (row_high, row_low), (col_high, col_low))
            return carry

        lax.fori_loop(0, TS, chunk, 0)


def panel(role, block, from_row, from_col):
    return pl.pallas_call(
        panel_kernel,
        in_specs=[SCALAR] + [HELD] * (1 + 2 * RING),
        out_specs=[HELD] * (1 + 2 * RING),
        out_shape=[jax.ShapeDtypeStruct(block.shape, F32)] + pieces_of(2),
        scratch_shapes=piece_scratch(1),
        compiler_params=pltpu.CompilerParams(vmem_limit_bytes=VMEM_BYTES),
    )(role, block, *from_row, *from_col)


def trail_kernel(role, block, *refs):
    from_row, from_col = refs[:RING], refs[RING : 2 * RING]
    out, held, row_high, row_low, col_high, col_low, sem, sems = refs[2 * RING :]
    inner = (role[0] > 0) & (role[1] > 0)

    @pl.when(jnp.logical_not(inner))
    def _():
        store = pltpu.make_async_copy(block, out, sem)
        store.start()
        store.wait()

    @pl.when(inner)
    def _():
        unpack(from_row, role[1], row_high, row_low)
        unpack(from_col, role[0], col_high, col_low)

        def store(i):
            rows = pl.ds(pl.multiple_of(i * TILE, TILE), TILE)
            return pltpu.make_async_copy(held.at[:, rows, :], out.at[:, rows, :], sems.at[i])

        def chunk(i, carry):
            rows = pl.ds(pl.multiple_of(i * TILE, TILE), TILE)
            trailing(block, held, rows, (row_high, row_low), (col_high, col_low))
            store(i).start()
            return carry

        lax.fori_loop(0, TS, chunk, 0)
        for i in range(TS):
            store(i).wait()


def trail(role, block, from_row, from_col):
    return pl.pallas_call(
        trail_kernel,
        in_specs=[SCALAR] + [HELD] * (1 + 2 * RING),
        out_specs=IN_HBM,
        out_shape=jax.ShapeDtypeStruct(block.shape, F32),
        scratch_shapes=[pltpu.VMEM(block.shape, F32)]
        + piece_scratch(2)
        + [pltpu.SemaphoreType.DMA, pltpu.SemaphoreType.DMA((TS,))],
        compiler_params=pltpu.CompilerParams(vmem_limit_bytes=VMEM_BYTES),
    )(role, block, *from_row, *from_col)


def spread(pieces, axis):
    got = [lax.ppermute(pieces[d], axis, [(0, d)]) for d in (2, 1, 3)]
    here = lax.axis_index(axis)
    return jnp.where(
        here == 0,
        pieces[0],
        jnp.where(here == 2, got[0], jnp.where(here == 1, got[1], got[2])),
    )


def exchange(own, axis):
    others = []
    for shift in (2, 1, 3):
        pairs = [(i, (i + shift) % RING) for i in range(RING)]
        others.append(lax.ppermute(own, axis, [p for p in pairs if p[1] != 0]))
    return [own] + others


def body(
    parent_front,
    child_left,
    child_right,
    tile_ranks,
    destination,
    tile_place,
    row_source,
    col_source,
    own_left,
    own_right,
    own_place,
    pivot_inverse,
):
    joined = ("front", "row")
    role = jnp.stack([lax.axis_index("row"), lax.axis_index("col")]).astype(jnp.int32)

    def sent(second):
        slots = pack(
            second,
            destination,
            tile_place,
            tile_ranks,
            child_left,
            child_right,
            row_source,
            col_source,
        )
        return lax.all_to_all(slots, joined, split_axis=0, concat_axis=0, tiled=True)

    second_slots = sent(1)
    first_slots = sent(0)
    places = second_slots[:, TILE + 2 * RANK : TILE + 2 * RANK + 2, 0].astype(jnp.int32)

    block = add_first(places[:, 0], own_place, parent_front[0], own_left, own_right, second_slots)
    block, *pieces = add_second(places[:, 1], role, block, first_slots, pivot_inverse[0])
    from_row, from_col = spread(pieces[:RING], "col"), spread(pieces[RING:], "row")
    from_row, from_col = exchange(from_row, "col"), exchange(from_col, "row")
    block, *pieces = panel(role, block, from_row, from_col)
    from_row, from_col = spread(pieces[:RING], "col"), spread(pieces[RING:], "row")
    from_row, from_col = exchange(from_row, "col"), exchange(from_col, "row")
    return trail(role, block, from_row, from_col)[None]


def solution(mesh):
    joined = ("front", "row", "col")
    tiles = P(joined, None, None)
    return jax.shard_map(
        body,
        mesh=mesh,
        in_specs=(
            P("front", None, "row", "col"),
            tiles,
            tiles,
            P(joined),
            P(joined),
            P(joined),
            P(joined, None),
            P(joined, None),
            tiles,
            tiles,
            P(joined),
            P("front", None, None, None, None),
        ),
        out_specs=P("front", None, "row", "col"),
        check_vma=False,
    )
```

time: 363 us -> 347 us (0.956)
  Pallas kernels: 65.4 us -> 46.5 us
  waiting for transfers between devices: 223 us -> 230 us
    pallas_call x6, Pallas kernels: 65.4 us -> 46.5 us  [the longest x2 14.2 us: pack(): pl.pallas_call(functools.partial(pack_kernel, second), in_specs=[SCALAR]...]
    all_to_all x2, waiting for transfers between devices: 171 us -> 180 us  [sent(): lax.all_to_all(slots, joined, split_axis=0, concat_axis=0, tiled=True)]
  transfers between devices with their start and end apart: 26 -> 26, of which waited for: 11 -> 11; matrix products, arithmetic and copies ran while one was open for 1% -> 1% of each run, Pallas kernels for 6% -> 4%
where the time goes in v3:
time: 347 us; the launch traced here: 344 us
  waiting for transfers between devices  230 us (66%)
  starting transfers between devices  58.9 us (17%)
  Pallas kernels  46.5 us (13%)
  local copies, waits for them, and re-layouts  6.81 us (2%)
    all_to_all x2, waiting for transfers between devices, sent(): lax.all_to_all(slots, joined, split_axis=0, concat_axis=0, tiled=True)  180 us
    ppermute x12, starting transfers between devices, exchange(): others.append(lax.ppermute(own, axis, [p for p in pairs if p[1] != 0]))  31.3 us
    ppermute x12, waiting for transfers between devices, spread(): got = [lax.ppermute(pieces[d], axis, [(0, d)]) for d in (2, 1, 3)]  29 us
    ppermute x12, waiting for transfers between devices, exchange(): others.append(lax.ppermute(own, axis, [p for p in pairs if p[1] != 0]))  21.1 us
    all_to_all x2, starting transfers between devices, sent(): lax.all_to_all(slots, joined, split_axis=0, concat_axis=0, tiled=True)  17 us
    pallas_call x2, Pallas kernels, pack(): pl.pallas_call(functools.partial(pack_kernel, second), in_specs=[SCALAR]...  14.2 us
    pallas_call x1, Pallas kernels, trail(): pl.pallas_call(trail_kernel, in_specs=[SCALAR] + [HELD] * (1 + 2 * RING),...  11.1 us
    ppermute x12, starting transfers between devices, spread(): got = [lax.ppermute(pieces[d], axis, [(0, d)]) for d in (2, 1, 3)]  10.6 us
  transfers between devices with their start and end apart: 26, of which 11 were waited for; matrix products, arithmetic and copies ran while one was open for 1% of the time, Pallas kernels for 4%

profile of v3, /device:TPU:34, one launch (start us, length us, event | category | flops | bytes accessed | tf_op | source)
XLA Modules:
  0.0 344.3 jit_solution(12221282606831668434)
XLA Ops:
  0.0 5.2 %shard_map.118 = bf16[32,528,256]{2,1,0:T(8,128)(2,1)} custom-call(s32[28]{0:T(128)} %destination.3, s32[28]{0:T(128)} %place.3, s32[28]{0:T(128)} %ranks.3, bf16[28,256,256]{2,1,0:T(8,128)(2,1)} %left.3, bf16[28,256,256]{2,1,0:T(8,128)(2,1)} %right.3, s32[28,256]{1,0:T(8,128)} %rows.3, s32[28,256]{1,0:T(8,128)} %cols.3), custom_call_target="tpu_custom_call" | custom-call | flops 1879048192 | bytes 16777216 | tf_op jit(solution)/shard_map/pallas_call | solution.py:191
  5.2 8.0 %all-to-all-start = ((bf16[32,528,256]{2,1,0:T(8,128)(2,1)}), bf16[32,528,256]{2,1,0:T(8,128)(2,1)}, u32[]{:S(2)}, u32[]{:S(2)}) async-start(bf16[32,528,256]{2,1,0:T(8,128)(2,1)} %shard_map.118), calls=%async_computation | async-start | bytes 17301504 | tf_op jit(solution)/shard_map/all_to_all | solution.py:623
  13.2 9.1 %shard_map.120 = bf16[32,512,256]{2,1,0:T(8,128)(2,1)} custom-call(s32[28]{0:T(128)} %destination.3, s32[28]{0:T(128)} %place.3, s32[28]{0:T(128)} %ranks.3, bf16[28,256,256]{2,1,0:T(8,128)(2,1)} %left.3, bf16[28,256,256]{2,1,0:T(8,128)(2,1)} %right.3, s32[28,256]{1,0:T(8,128)} %rows.3, s32[28,256]{1,0:T(8,128)} %cols.3), custom_call_target="tpu_custom_call" | custom-call | flops 1879048192 | bytes 16777216 | tf_op jit(solution)/shard_map/pallas_call | solution.py:191
  22.3 91.7 %all-to-all-done.slots = bf16[32,528,256]{2,1,0:T(8,128)(2,1)} async-done(((bf16[32,528,256]{2,1,0:T(8,128)(2,1)}), bf16[32,528,256]{2,1,0:T(8,128)(2,1)}, u32[]{:S(2)}, u32[]{:S(2)}) %all-to-all-start) | async-done | bytes 8650784 | tf_op jit(solution)/shard_map/all_to_all | solution.py:623
  114.0 9.0 %all-to-all-start.1 = ((bf16[32,512,256]{2,1,0:T(8,128)(2,1)}), bf16[32,512,256]{2,1,0:T(8,128)(2,1)}, u32[]{:S(2)}, u32[]{:S(2)}) async-start(bf16[32,512,256]{2,1,0:T(8,128)(2,1)} %shard_map.120), calls=%async_computation.1 | async-start | bytes 16777216 | tf_op jit(solution)/shard_map/all_to_all | solution.py:623
  124.1 5.9 %shard_map.119.before = f32[2,768,768]{2,1,0:T(8,128)S(1)} custom-call(s32[32]{0:T(128)S(1)} %get-tuple-element.41.places, s32[4]{0:T(128)S(1)} %copy-done.6, f32[2,768,768]{2,1,0:T(8,128)} %bitcast.11, bf16[4,256,256]{2,1,0:T(8,128)(2,1)S(1)} %copy-done.4, bf16[4,256,256]{2,1,0:T(8,128)(2,1)S(1)} %copy-done.5, bf16[32,528,256]{2,1,0:T(8,128)(2,1)} %all-to-all-done.slots), custom_call_target="tpu_custom_call" | custom-call | flops 2147483648 | bytes 20971520 | tf_op jit(solution)/shard_map/pallas_call | solution.py:373
  132.2 87.9 %all-to-all-done.1.slots = bf16[32,512,256]{2,1,0:T(8,128)(2,1)} async-done(((bf16[32,512,256]{2,1,0:T(8,128)(2,1)}), bf16[32,512,256]{2,1,0:T(8,128)(2,1)}, u32[]{:S(2)}, u32[]{:S(2)}) %all-to-all-start.1) | async-done | bytes 8388640 | tf_op jit(solution)/shard_map/all_to_all | solution.py:623
  220.1 9.8 %shard_map.121 = (f32[2,768,768]{2,1,0:T(8,128)S(1)}, s16[208,512]{1,0:T(8,128)(2,1)S(1)}, s16[208,512]{1,0:T(8,128)(2,1)S(1)}, s16[208,512]{1,0:T(8,128)(2,1)S(...) custom-call(s32[32]{0:T(128)S(1)} %get-tuple-element.42.places, ...), custom_call_target="tpu_custom_call" | custom-call | flops 2147483648 | bytes 20971520 | tf_op jit(solution)/shard_map/pallas_call | solution.py:401
  230.0 2.2 copy-done.1
  237.5 10.4 %collective-permute-done.1 = s16[208,512]{1,0:T(8,128)(2,1)S(1)} collective-permute-done((s16[208,512]{1,0:T(8,128)(2,1)S(1)}, s16[208,512]{1,0:T(8,128)(2,1)S(1)}, u32[]{:S(2)}, u32[]{:S(2)}) %collective-permute-start.1) | collective-permute-done | bytes 213024 | tf_op jit(solution)/shard_map/ppermute | solution.py:578
  247.9 2.9 collective-permute-start.3
  251.1 2.2 collective-permute-start.10
  254.6 5.2 %collective-permute-start.9 = (s16[144,768]{1,0:T(8,128)(2,1)S(1)}, s16[144,768]{1,0:T(8,128)(2,1)S(1)}, u32[]{:S(2)}, u32[]{:S(2)}) collective-permute-start(s16[144,768]{1,0:T(8,128)(2,1)S(1)} %select_select_fusion.2.refs_4_), channel_id=1, source_target_pairs={{0,8},{4,12},{12,4},{1,9},{5,13},{13,5},{2,10},{6,14},{14,6},{3,11... | collective-permute-start | bytes 663560 | tf_op jit(solution)/shard_map/ppermute | solution.py:591
  259.8 5.5 %collective-permute-start.4 = (s16[208,512]{1,0:T(8,128)(2,1)S(1)}, s16[208,512]{1,0:T(8,128)(2,1)S(1)}, u32[]{:S(2)}, u32[]{:S(2)}) collective-permute-start(s16[208,512]{1,0:T(8,128)(2,1)S(1)} %select_select_fusion.3.refs_0_), channel_id=1, source_target_pairs={{0,1},{1,2},{2,3},{4,5},{5,6},{6,7},{8,9},{9,10},{10,11},{12,13},{... | collective-permute-start | bytes 638984 | tf_op jit(solution)/shard_map/ppermute | solution.py:591
  266.8 3.5 %collective-permute-done.4.refs_2_ = s16[208,512]{1,0:T(8,128)(2,1)S(1)} collective-permute-done((s16[208,512]{1,0:T(8,128)(2,1)S(1)}, s16[208,512]{1,0:T(8,128)(2,1)S(1)}, u32[]{:S(2)}, u32[]{:S(2)}) %collective-permute-start.4) | collective-permute-done | bytes 213024 | tf_op jit(solution)/shard_map/ppermute | solution.py:591
  270.2 4.4 %collective-permute-done.5.refs_3_ = s16[208,512]{1,0:T(8,128)(2,1)S(1)} collective-permute-done((s16[208,512]{1,0:T(8,128)(2,1)S(1)}, s16[208,512]{1,0:T(8,128)(2,1)S(1)}, u32[]{:S(2)}, u32[]{:S(2)}) %collective-permute-start.5) | collective-permute-done | bytes 213024 | tf_op jit(solution)/shard_map/ppermute | solution.py:591
  274.7 2.3 copy-done.2
  277.0 5.5 %shard_map.122 = (f32[2,768,768]{2,1,0:T(8,128)S(1)}, s16[208,1024]{1,0:T(8,128)(2,1)S(1)}, s16[208,1024]{1,0:T(8,128)(2,1)S(1)}, s16[208,1024]{1,0:T(8,128)(2,1...) custom-call(s32[2]{0:T(128)S(1)} %pad_add_fusion.role, ...), custom_call_target="tpu_custom_call" | custom-call | tf_op jit(solution)/shard_map/pallas_call | solution.py:523
  287.9 15.9 %collective-permute-done.19 = s16[272,768]{1,0:T(8,128)(2,1)S(1)} collective-permute-done((s16[272,768]{1,0:T(8,128)(2,1)S(1)}, s16[272,768]{1,0:T(8,128)(2,1)S(1)}, u32[]{:S(2)}, u32[]{:S(2)}) %collective-permute-start.19) | collective-permute-done | bytes 417824 | tf_op jit(solution)/shard_map/ppermute | solution.py:578
  306.0 2.7 collective-permute-done.13
  314.1 4.3 %collective-permute-start.22 = (s16[272,768]{1,0:T(8,128)(2,1)S(1)}, s16[272,768]{1,0:T(8,128)(2,1)S(1)}, u32[]{:S(2)}, u32[]{:S(2)}) collective-permute-start(s16[272,768]{1,0:T(8,128)(2,1)S(1)} %select_select_fusion.1.refs_4_), channel_id=1, source_target_pairs={{0,4},{4,8},{8,12},{1,5},{5,9},{9,13},{2,6},{6,10},{10,14},{3,7},{... | collective-permute-start | bytes 1253384 | tf_op jit(solution)/shard_map/ppermute | solution.py:591
  320.6 7.5 %collective-permute-done.22.refs_6_ = s16[272,768]{1,0:T(8,128)(2,1)S(1)} collective-permute-done((s16[272,768]{1,0:T(8,128)(2,1)S(1)}, s16[272,768]{1,0:T(8,128)(2,1)S(1)}, u32[]{:S(2)}, u32[]{:S(2)}) %collective-permute-start.22) | collective-permute-done | bytes 417824 | tf_op jit(solution)/shard_map/ppermute | solution.py:591
  328.1 4.0 %collective-permute-done.23.refs_7_ = s16[272,768]{1,0:T(8,128)(2,1)S(1)} collective-permute-done((s16[272,768]{1,0:T(8,128)(2,1)S(1)}, s16[272,768]{1,0:T(8,128)(2,1)S(1)}, u32[]{:S(2)}, u32[]{:S(2)}) %collective-permute-start.23) | collective-permute-done | bytes 417824 | tf_op jit(solution)/shard_map/ppermute | solution.py:591
  333.0 11.1 %shard_map.123 = f32[2,768,768]{2,1,0:T(8,128)} custom-call(s32[2]{0:T(128)S(1)} %pad_add_fusion.role, f32[2,768,768]{2,1,0:T(8,128)S(1)} %get-tuple-element.32.block, s16[208,1024]{1,0:T(8,128)(2,1)S(1)} %select_select_fusion.refs_0_, s16[208,1024]{1,0:T(8,128)(2,1)S(1)} %collective-permute-done.15.refs_1_, ...), custom_call_target="tpu_custom_call" | custom-call | tf_op jit(solution)/shard_map/pallas_call | solution.py:565
  (56 shorter events, 27.4 us)
Async XLA Ops:
  5.2 108.8 %all-to-all-start = ((bf16[32,528,256]{2,1,0:T(8,128)(2,1)}), bf16[32,528,256]{2,1,0:T(8,128)(2,1)}, u32[]{:S(2)}, u32[]{:S(2)}) async-start(bf16[32,528,256]{2,1,0:T(8,128)(2,1)} %shard_map.118), calls=%async_computation | async-start | bytes 17301504 | tf_op jit(solution)/shard_map/all_to_all | solution.py:623
  114.0 106.1 %all-to-all-start.1 = ((bf16[32,512,256]{2,1,0:T(8,128)(2,1)}), bf16[32,512,256]{2,1,0:T(8,128)(2,1)}, u32[]{:S(2)}, u32[]{:S(2)}) async-start(bf16[32,512,256]{2,1,0:T(8,128)(2,1)} %shard_map.120), calls=%async_computation.1 | async-start | bytes 16777216 | tf_op jit(solution)/shard_map/all_to_all | solution.py:623
  232.8 15.0 %collective-permute-start.1 = (s16[208,512]{1,0:T(8,128)(2,1)S(1)}, s16[208,512]{1,0:T(8,128)(2,1)S(1)}, u32[]{:S(2)}, u32[]{:S(2)}) collective-permute-start(s16[208,512]{1,0:T(8,128)(2,1)S(1)} %get-tuple-element.26), channel_id=1, source_target_pairs={{0,1},{4,5},{8,9},{12,13},{16,17},{20,21},{24,25},{28,29},{32,33},... | collective-permute-start | bytes 638984 | tf_op jit(solution)/shard_map/ppermute | solution.py:578
  234.1 13.7 %collective-permute-start.2 = (s16[208,512]{1,0:T(8,128)(2,1)S(1)}, s16[208,512]{1,0:T(8,128)(2,1)S(1)}, u32[]{:S(2)}, u32[]{:S(2)}) collective-permute-start(s16[208,512]{1,0:T(8,128)(2,1)S(1)} %get-tuple-element.27), channel_id=1, source_target_pairs={{0,3},{4,7},{8,11},{12,15},{16,19},{20,23},{24,27},{28,31},{32,35}... | collective-permute-start | bytes 638984 | tf_op jit(solution)/shard_map/ppermute | solution.py:578
  234.8 16.1 %collective-permute-start.6 = (s16[144,768]{1,0:T(8,128)(2,1)S(1)}, s16[144,768]{1,0:T(8,128)(2,1)S(1)}, u32[]{:S(2)}, u32[]{:S(2)}) collective-permute-start(s16[144,768]{1,0:T(8,128)(2,1)S(1)} %get-tuple-element.29), channel_id=1, source_target_pairs={{0,8},{1,9},{2,10},{3,11},{16,24},{17,25},{18,26},{19,27},{32,40},... | collective-permute-start | bytes 663560 | tf_op jit(solution)/shard_map/ppermute | solution.py:578
  235.5 15.4 %collective-permute-start.7 = (s16[144,768]{1,0:T(8,128)(2,1)S(1)}, s16[144,768]{1,0:T(8,128)(2,1)S(1)}, u32[]{:S(2)}, u32[]{:S(2)}) collective-permute-start(s16[144,768]{1,0:T(8,128)(2,1)S(1)} %get-tuple-element.30), channel_id=1, source_target_pairs={{0,4},{1,5},{2,6},{3,7},{16,20},{17,21},{18,22},{19,23},{32,36},{3... | collective-permute-start | bytes 663560 | tf_op jit(solution)/shard_map/ppermute | solution.py:578
  236.8 14.1 %collective-permute-start.8 = (s16[144,768]{1,0:T(8,128)(2,1)S(1)}, s16[144,768]{1,0:T(8,128)(2,1)S(1)}, u32[]{:S(2)}, u32[]{:S(2)}) collective-permute-start(s16[144,768]{1,0:T(8,128)(2,1)S(1)} %get-tuple-element.31), channel_id=1, source_target_pairs={{0,12},{1,13},{2,14},{3,15},{16,28},{17,29},{18,30},{19,31},{32,44... | collective-permute-start | bytes 663560 | tf_op jit(solution)/shard_map/ppermute | solution.py:578
  247.9 17.3 %collective-permute-start.3 = (s16[208,512]{1,0:T(8,128)(2,1)S(1)}, s16[208,512]{1,0:T(8,128)(2,1)S(1)}, u32[]{:S(2)}, u32[]{:S(2)}) collective-permute-start(s16[208,512]{1,0:T(8,128)(2,1)S(1)} %select_select_fusion.3.refs_0_), channel_id=1, source_target_pairs={{0,2},{1,3},{3,1},{4,6},{5,7},{7,5},{8,10},{9,11},{11,9},{12,14},{... | collective-permute-start | bytes 638984 | tf_op jit(solution)/shard_map/ppermute | solution.py:591
  251.1 23.6 %collective-permute-start.10 = (s16[144,768]{1,0:T(8,128)(2,1)S(1)}, s16[144,768]{1,0:T(8,128)(2,1)S(1)}, u32[]{:S(2)}, u32[]{:S(2)}) collective-permute-start(s16[144,768]{1,0:T(8,128)(2,1)S(1)} %select_select_fusion.2.refs_4_), channel_id=1, source_target_pairs={{0,4},{4,8},{8,12},{1,5},{5,9},{9,13},{2,6},{6,10},{10,14},{3,7},{... | collective-permute-start | bytes 663560 | tf_op jit(solution)/shard_map/ppermute | solution.py:591
  253.3 21.4 %collective-permute-start.11 = (s16[144,768]{1,0:T(8,128)(2,1)S(1)}, s16[144,768]{1,0:T(8,128)(2,1)S(1)}, u32[]{:S(2)}, u32[]{:S(2)}) collective-permute-start(s16[144,768]{1,0:T(8,128)(2,1)S(1)} %select_select_fusion.2.refs_4_), channel_id=1, source_target_pairs={{0,12},{8,4},{12,8},{1,13},{9,5},{13,9},{2,14},{10,6},{14,10},{3,1... | collective-permute-start | bytes 663560 | tf_op jit(solution)/shard_map/ppermute | solution.py:591
  254.6 20.1 %collective-permute-start.9 = (s16[144,768]{1,0:T(8,128)(2,1)S(1)}, s16[144,768]{1,0:T(8,128)(2,1)S(1)}, u32[]{:S(2)}, u32[]{:S(2)}) collective-permute-start(s16[144,768]{1,0:T(8,128)(2,1)S(1)} %select_select_fusion.2.refs_4_), channel_id=1, source_target_pairs={{0,8},{4,12},{12,4},{1,9},{5,13},{13,5},{2,10},{6,14},{14,6},{3,11... | collective-permute-start | bytes 663560 | tf_op jit(solution)/shard_map/ppermute | solution.py:591
  259.8 10.5 %collective-permute-start.4 = (s16[208,512]{1,0:T(8,128)(2,1)S(1)}, s16[208,512]{1,0:T(8,128)(2,1)S(1)}, u32[]{:S(2)}, u32[]{:S(2)}) collective-permute-start(s16[208,512]{1,0:T(8,128)(2,1)S(1)} %select_select_fusion.3.refs_0_), channel_id=1, source_target_pairs={{0,1},{1,2},{2,3},{4,5},{5,6},{6,7},{8,9},{9,10},{10,11},{12,13},{... | collective-permute-start | bytes 638984 | tf_op jit(solution)/shard_map/ppermute | solution.py:591
  265.3 9.4 %collective-permute-start.5 = (s16[208,512]{1,0:T(8,128)(2,1)S(1)}, s16[208,512]{1,0:T(8,128)(2,1)S(1)}, u32[]{:S(2)}, u32[]{:S(2)}) collective-permute-start(s16[208,512]{1,0:T(8,128)(2,1)S(1)} %select_select_fusion.3.refs_0_), channel_id=1, source_target_pairs={{0,3},{2,1},{3,2},{4,7},{6,5},{7,6},{8,11},{10,9},{11,10},{12,15},... | collective-permute-start | bytes 638984 | tf_op jit(solution)/shard_map/ppermute | solution.py:591
  283.2 20.6 %collective-permute-start.19 = (s16[272,768]{1,0:T(8,128)(2,1)S(1)}, s16[272,768]{1,0:T(8,128)(2,1)S(1)}, u32[]{:S(2)}, u32[]{:S(2)}) collective-permute-start(s16[272,768]{1,0:T(8,128)(2,1)S(1)} %get-tuple-element.39), channel_id=1, source_target_pairs={{0,4},{1,5},{2,6},{3,7},{16,20},{17,21},{18,22},{19,23},{32,36},{3... | collective-permute-start | bytes 1253384 | tf_op jit(solution)/shard_map/ppermute | solution.py:578
  284.5 19.3 %collective-permute-start.20 = (s16[272,768]{1,0:T(8,128)(2,1)S(1)}, s16[272,768]{1,0:T(8,128)(2,1)S(1)}, u32[]{:S(2)}, u32[]{:S(2)}) collective-permute-start(s16[272,768]{1,0:T(8,128)(2,1)S(1)} %get-tuple-element.40), channel_id=1, source_target_pairs={{0,12},{1,13},{2,14},{3,15},{16,28},{17,29},{18,30},{19,31},{32,44... | collective-permute-start | bytes 1253384 | tf_op jit(solution)/shard_map/ppermute | solution.py:578
  285.2 20.8 %collective-permute-start.12 = (s16[208,1024]{1,0:T(8,128)(2,1)S(1)}, s16[208,1024]{1,0:T(8,128)(2,1)S(1)}, u32[]{:S(2)}, u32[]{:S(2)}) collective-permute-start(s16[208,1024]{1,0:T(8,128)(2,1)S(1)} %get-tuple-element.34), channel_id=1, source_target_pairs={{0,2},{4,6},{8,10},{12,14},{16,18},{20,22},{24,26},{28,30},{32,34}... | collective-permute-start | bytes 1277960 | tf_op jit(solution)/shard_map/ppermute | solution.py:578
  285.9 22.8 %collective-permute-start.13 = (s16[208,1024]{1,0:T(8,128)(2,1)S(1)}, s16[208,1024]{1,0:T(8,128)(2,1)S(1)}, u32[]{:S(2)}, u32[]{:S(2)}) collective-permute-start(s16[208,1024]{1,0:T(8,128)(2,1)S(1)} %get-tuple-element.35), channel_id=1, source_target_pairs={{0,1},{4,5},{8,9},{12,13},{16,17},{20,21},{24,25},{28,29},{32,33},... | collective-permute-start | bytes 1277960 | tf_op jit(solution)/shard_map/ppermute | solution.py:578
  287.2 21.5 %collective-permute-start.14 = (s16[208,1024]{1,0:T(8,128)(2,1)S(1)}, s16[208,1024]{1,0:T(8,128)(2,1)S(1)}, u32[]{:S(2)}, u32[]{:S(2)}) collective-permute-start(s16[208,1024]{1,0:T(8,128)(2,1)S(1)} %get-tuple-element.36), channel_id=1, source_target_pairs={{0,3},{4,7},{8,11},{12,15},{16,19},{20,23},{24,27},{28,31},{32,35}... | collective-permute-start | bytes 1277960 | tf_op jit(solution)/shard_map/ppermute | solution.py:578
  304.1 15.2 %collective-permute-start.21 = (s16[272,768]{1,0:T(8,128)(2,1)S(1)}, s16[272,768]{1,0:T(8,128)(2,1)S(1)}, u32[]{:S(2)}, u32[]{:S(2)}) collective-permute-start(s16[272,768]{1,0:T(8,128)(2,1)S(1)} %select_select_fusion.1.refs_4_), channel_id=1, source_target_pairs={{0,8},{4,12},{12,4},{1,9},{5,13},{13,5},{2,10},{6,14},{14,6},{3,11... | collective-permute-start | bytes 1253384 | tf_op jit(solution)/shard_map/ppermute | solution.py:591
  309.0 23.2 %collective-permute-start.15 = (s16[208,1024]{1,0:T(8,128)(2,1)S(1)}, s16[208,1024]{1,0:T(8,128)(2,1)S(1)}, u32[]{:S(2)}, u32[]{:S(2)}) collective-permute-start(s16[208,1024]{1,0:T(8,128)(2,1)S(1)} %select_select_fusion.refs_0_), channel_id=1, source_target_pairs={{0,2},{1,3},{3,1},{4,6},{5,7},{7,5},{8,10},{9,11},{11,9},{12,14},{... | collective-permute-start | bytes 1277960 | tf_op jit(solution)/shard_map/ppermute | solution.py:591
  310.9 21.2 %collective-permute-start.16 = (s16[208,1024]{1,0:T(8,128)(2,1)S(1)}, s16[208,1024]{1,0:T(8,128)(2,1)S(1)}, u32[]{:S(2)}, u32[]{:S(2)}) collective-permute-start(s16[208,1024]{1,0:T(8,128)(2,1)S(1)} %select_select_fusion.refs_0_), channel_id=1, source_target_pairs={{0,1},{1,2},{2,3},{4,5},{5,6},{6,7},{8,9},{9,10},{10,11},{12,13},{... | collective-permute-start | bytes 1277960 | tf_op jit(solution)/shard_map/ppermute | solution.py:591
  312.8 20.2 %collective-permute-start.17 = (s16[208,1024]{1,0:T(8,128)(2,1)S(1)}, s16[208,1024]{1,0:T(8,128)(2,1)S(1)}, u32[]{:S(2)}, u32[]{:S(2)}) collective-permute-start(s16[208,1024]{1,0:T(8,128)(2,1)S(1)} %select_select_fusion.refs_0_), channel_id=1, source_target_pairs={{0,3},{2,1},{3,2},{4,7},{6,5},{7,6},{8,11},{10,9},{11,10},{12,15},... | collective-permute-start | bytes 1277960 | tf_op jit(solution)/shard_map/ppermute | solution.py:591
  314.1 14.0 %collective-permute-start.22 = (s16[272,768]{1,0:T(8,128)(2,1)S(1)}, s16[272,768]{1,0:T(8,128)(2,1)S(1)}, u32[]{:S(2)}, u32[]{:S(2)}) collective-permute-start(s16[272,768]{1,0:T(8,128)(2,1)S(1)} %select_select_fusion.1.refs_4_), channel_id=1, source_target_pairs={{0,4},{4,8},{8,12},{1,5},{5,9},{9,13},{2,6},{6,10},{10,14},{3,7},{... | collective-permute-start | bytes 1253384 | tf_op jit(solution)/shard_map/ppermute | solution.py:591
  319.3 12.9 %collective-permute-start.23 = (s16[272,768]{1,0:T(8,128)(2,1)S(1)}, s16[272,768]{1,0:T(8,128)(2,1)S(1)}, u32[]{:S(2)}, u32[]{:S(2)}) collective-permute-start(s16[272,768]{1,0:T(8,128)(2,1)S(1)} %select_select_fusion.1.refs_4_), channel_id=1, source_target_pairs={{0,12},{8,4},{12,8},{1,13},{9,5},{13,9},{2,14},{10,6},{14,10},{3,1... | collective-permute-start | bytes 1253384 | tf_op jit(solution)/shard_map/ppermute | solution.py:591
  (9 other events, 417.5 us)

commit v4 on v3

--- a/solution.py
+++ b/solution.py
@@ -14,7 +14,9 @@
 SIDE = TS * TILE
 SENT = 28
 GROUP = 32
-RING = 4
+HALVES = 2
+ARRIVALS = 4
+CHUNK = 64
 CODE_ROWS = 16
 NOTE_ROWS = 16
 LOG_STEP = math.log(2.0) / 32.0
@@ -43,11 +45,6 @@
     whole, code_rows = encode(values)
     ref[:rows, :] = whole
     ref[rows:, :] = code_rows
-
-
-def decode(piece_rows, code_rows):
-    code = code_rows[:1].astype(jnp.int32).astype(F32)
-    return piece_rows.astype(jnp.int32).astype(F32) * jnp.exp(code * LOG_STEP)
 
 
 def cut(x):
@@ -314,13 +311,13 @@
 
 
 def second_kernel(places, role, before, slots, inverse, out, *refs):
-    along_row, along_col = refs[:RING], refs[RING : 2 * RING]
+    along_row, along_col = refs[:HALVES], refs[HALVES : 2 * HALVES]
 
     def prepare():
         out[...] = before[...]
 
-    add_slots(out, places, slots, refs[2 * RING :], prepare)
-    long, short = SIDE // RING, 2 * TILE // RING
+    add_slots(out, places, slots, refs[2 * HALVES :], prepare)
+    long = SIDE // HALVES
 
     @pl.when((role[0] == 0) & (role[1] == 0))
     def _():
@@ -341,10 +338,9 @@
             for i, j in ((0, 1), (0, 2), (1, 2))
         ]
         upper = [jnp.concatenate([x[half] for x in upper], 1) for half in (0, 1)]
-        for piece in range(RING):
-            store_piece(along_row[piece], lower[piece * long : (piece + 1) * long])
-            half, start = divmod(piece * short, TILE)
-            store_piece(along_col[piece], upper[half][start : start + short])
+        for half in range(HALVES):
+            store_piece(along_row[half], lower[half * long : (half + 1) * long])
+            store_piece(along_col[half], upper[half])
 
     @pl.when((role[0] > 0) & (role[1] == 0))
     def _():
@@ -353,15 +349,14 @@
             for i in range(TS):
                 at = tile_at(i, p)
                 put(out, *at, complex_dot(cuts(get(out, *at)), pivot))
-        for piece in range(RING):
-            rows = slice(piece * long, (piece + 1) * long)
-            store_piece(along_row[piece], jnp.concatenate(get(out, rows, slice(0, TILE)), 1))
+        for half in range(HALVES):
+            rows = slice(half * long, (half + 1) * long)
+            store_piece(along_row[half], jnp.concatenate(get(out, rows, slice(0, TILE)), 1))
 
     @pl.when((role[0] == 0) & (role[1] > 0))
     def _():
-        for piece in range(RING):
-            half, start = divmod(piece * short, TILE)
-            store_piece(along_col[piece], out[half, start : start + short, :])
+        for half in range(HALVES):
+            store_piece(along_col[half], out[half, :TILE, :])
 
 
 ADD_COST = pl.CostEstimate(
@@ -382,11 +377,11 @@
 
 
 def row_shape(panels):
-    return (SIDE // RING + CODE_ROWS, 2 * TILE * panels)
+    return (SIDE // HALVES + CODE_ROWS, 2 * TILE * panels)
 
 
 def col_shape(panels):
-    return (2 * TILE * panels // RING + CODE_ROWS, SIDE)
+    return (2 * TILE * panels // HALVES + CODE_ROWS, SIDE)
 
 
 def coded(shape):
@@ -394,14 +389,14 @@
 
 
 def pieces_of(panels):
-    return [coded(row_shape(panels))] * RING + [coded(col_shape(panels))] * RING
+    return [coded(row_shape(panels))] * HALVES + [coded(col_shape(panels))] * HALVES
 
 
 def add_second(places, role, before, slots, inverse):
     return pl.pallas_call(
         second_kernel,
         in_specs=[SCALAR, SCALAR, HELD, IN_HBM, HELD],
-        out_specs=[HELD] * (1 + 2 * RING),
+        out_specs=[HELD] * (1 + 2 * HALVES),
         out_shape=[jax.ShapeDtypeStruct(before.shape, F32)] + pieces_of(1),
         scratch_shapes=add_scratch(),
         compiler_params=pltpu.CompilerParams(vmem_limit_bytes=MORE_VMEM_BYTES),
@@ -410,12 +405,25 @@
 
 
 def unpack(refs, place, high, low):
-    rows = refs[0].shape[0] - CODE_ROWS
-    for ref, shift in zip(refs, (0, 2, RING - 1, 1)):
-        at = ((place + shift) & (RING - 1)) * rows
-        h, l = cut(decode(ref[:rows, :], ref[rows:, :]))
-        high[pl.ds(pl.multiple_of(at, 16), rows), :] = h
-        low[pl.ds(pl.multiple_of(at, 16), rows), :] = l
+    one, three, plus, minus = refs
+    half = one.shape[0] - CODE_ROWS
+    scales = lambda ref: jnp.exp(ref[half:, :][:1].astype(jnp.int32).astype(F32) * LOG_STEP)
+
+    for at, pair in ((1, (one, plus)), (2, (plus, minus)), (3, (minus, three))):
+
+        @pl.when(place == at)
+        def _(pair=pair):
+            for which, ref in enumerate(pair):
+                scale = scales(ref)
+
+                def chunk(i, carry, ref=ref, scale=scale, which=which):
+                    rows = pl.ds(pl.multiple_of(i * CHUNK, CHUNK), CHUNK)
+                    into = pl.ds(pl.multiple_of(which * half + i * CHUNK, CHUNK), CHUNK)
+                    values = ref[rows, :].astype(jnp.int32).astype(F32) * scale
+                    high[into, :], low[into, :] = cut(values)
+                    return carry
+
+                lax.fori_loop(0, half // CHUNK, chunk, 0)
 
 
 def trailing(block, out, rows, left, right):
@@ -444,13 +452,10 @@
 
 
 def panel_kernel(role, block, *refs):
-    from_row, from_col = refs[:RING], refs[RING : 2 * RING]
-    out, along_row, along_col = (
-        refs[2 * RING],
-        refs[2 * RING + 1 : 3 * RING + 1],
-        refs[3 * RING + 1 : 4 * RING + 1],
-    )
-    row_high, row_low, col_high, col_low = refs[4 * RING + 1 :]
+    from_row, from_col = refs[:ARRIVALS], refs[ARRIVALS : 2 * ARRIVALS]
+    out, *refs = refs[2 * ARRIVALS :]
+    along_row, along_col = refs[:HALVES], refs[HALVES : 2 * HALVES]
+    row_high, row_low, col_high, col_low = refs[2 * HALVES :]
     parts = [slice(t * TILE, (t + 1) * TILE) for t in range(TS)]
 
     @pl.when(role[1] > 0)
@@ -482,11 +487,11 @@
             return carry
 
         lax.fori_loop(0, TS, chunk, 0)
-        part = SIDE // RING
-        for piece in range(RING):
-            rows = slice(piece * part, (piece + 1) * part)
+        long = SIDE // HALVES
+        for half in range(HALVES):
+            rows = slice(half * long, (half + 1) * long)
             wide = [x for cols in parts[1:] for x in get(out, rows, cols)]
-            store_piece(along_row[piece], jnp.concatenate(wide, 1))
+            store_piece(along_row[half], jnp.concatenate(wide, 1))
 
     @pl.when((role[0] == 0) & (role[1] > 0))
     def _():
@@ -505,9 +510,9 @@
             return carry
 
         lax.fori_loop(0, TS, chunk, 0)
-        for piece in range(RING):
-            at, half = divmod(piece, 2)
-            store_piece(along_col[piece], out[half, parts[at + 1], :])
+        for half in range(HALVES):
+            both = get(out, parts[half + 1], slice(0, SIDE))
+            store_piece(along_col[half], jnp.concatenate(both, 0))
 
     @pl.when((role[0] > 0) & (role[1] > 0))
     def _():
@@ -522,8 +527,8 @@
 def panel(role, block, from_row, from_col):
     return pl.pallas_call(
         panel_kernel,
-        in_specs=[SCALAR] + [HELD] * (1 + 2 * RING),
-        out_specs=[HELD] * (1 + 2 * RING),
+        in_specs=[SCALAR] + [HELD] * (1 + 2 * ARRIVALS),
+        out_specs=[HELD] * (1 + 2 * HALVES),
         out_shape=[jax.ShapeDtypeStruct(block.shape, F32)] + pieces_of(2),
         scratch_shapes=piece_scratch(1),
         compiler_params=pltpu.CompilerParams(vmem_limit_bytes=VMEM_BYTES),
@@ -531,8 +536,8 @@
 
 
 def trail_kernel(role, block, *refs):
-    from_row, from_col = refs[:RING], refs[RING : 2 * RING]
-    out, held, row_high, row_low, col_high, col_low, sem, sems = refs[2 * RING :]
+    from_row, from_col = refs[:ARRIVALS], refs[ARRIVALS : 2 * ARRIVALS]
+    out, held, row_high, row_low, col_high, col_low, sem, sems = refs[2 * ARRIVALS :]
     inner = (role[0] > 0) & (role[1] > 0)
 
     @pl.when(jnp.logical_not(inner))
@@ -564,7 +569,7 @@
 def trail(role, block, from_row, from_col):
     return pl.pallas_call(
         trail_kernel,
-        in_specs=[SCALAR] + [HELD] * (1 + 2 * RING),
+        in_specs=[SCALAR] + [HELD] * (1 + 2 * ARRIVALS),
         out_specs=IN_HBM,
         out_shape=jax.ShapeDtypeStruct(block.shape, F32),
         scratch_shapes=[pltpu.VMEM(block.shape, F32)]
@@ -574,22 +579,13 @@
     )(role, block, *from_row, *from_col)
 
 
-def spread(pieces, axis):
-    got = [lax.ppermute(pieces[d], axis, [(0, d)]) for d in (2, 1, 3)]
-    here = lax.axis_index(axis)
-    return jnp.where(
-        here == 0,
-        pieces[0],
-        jnp.where(here == 2, got[0], jnp.where(here == 1, got[1], got[2])),
-    )
-
-
-def exchange(own, axis):
-    others = []
-    for shift in (2, 1, 3):
-        pairs = [(i, (i + shift) % RING) for i in range(RING)]
-        others.append(lax.ppermute(own, axis, [p for p in pairs if p[1] != 0]))
-    return [own] + others
+def broadcast(halves, axis):
+    first = lax.axis_index(axis) == 0
+    one = lax.ppermute(halves[0], axis, [(0, 1)])
+    three = lax.ppermute(halves[1], axis, [(0, 3)])
+    plus = lax.ppermute(jnp.where(first, halves[1], one), axis, [(0, 1), (1, 2)])
+    minus = lax.ppermute(jnp.where(first, halves[0], three), axis, [(0, 3), (3, 2)])
+    return one, three, plus, minus
 
 
 def body(
@@ -628,11 +624,9 @@
 
     block = add_first(places[:, 0], own_place, parent_front[0], own_left, own_right, second_slots)
     block, *pieces = add_second(places[:, 1], role, block, first_slots, pivot_inverse[0])
-    from_row, from_col = spread(pieces[:RING], "col"), spread(pieces[RING:], "row")
-    from_row, from_col = exchange(from_row, "col"), exchange(from_col, "row")
+    from_row, from_col = broadcast(pieces[:HALVES], "col"), broadcast(pieces[HALVES:], "row")
     block, *pieces = panel(role, block, from_row, from_col)
-    from_row, from_col = spread(pieces[:RING], "col"), spread(pieces[RING:], "row")
-    from_row, from_col = exchange(from_row, "col"), exchange(from_col, "row")
+    from_row, from_col = broadcast(pieces[:HALVES], "col"), broadcast(pieces[HALVES:], "row")
     return trail(role, block, from_row, from_col)[None]
 
 

time: 347 us -> 337 us (0.971)
  starting transfers between devices: 58.9 us -> 35.1 us
  waiting for transfers between devices: 230 us -> 246 us
    ppermute x24 -> x16, starting transfers between devices: 41.9 us -> 18.9 us  [the longest x4 7.86 us: broadcast(): lax.ppermute(jnp.where(first, halves[1], one), axis, [(0, 1), (1, 2)])]
    ppermute x24 -> x16, waiting for transfers between devices: 50.1 us -> 66.1 us  [the longest x4 36.4 us: broadcast(): lax.ppermute(jnp.where(first, halves[1], one), axis, [(0, 1), (1, 2)])]
  transfers between devices with their start and end apart: 26 -> 18, of which waited for: 11 -> 8; matrix products, arithmetic and copies ran while one was open for 1% -> 1% of each run, Pallas kernels for 4% -> 4%
where the time goes in v4:
time: 337 us; the launch traced here: 335 us
  waiting for transfers between devices  246 us (73%)
  Pallas kernels  47 us (14%)
  starting transfers between devices  35.1 us (10%)
  local copies, waits for them, and re-layouts  4.49 us (1%)
    all_to_all x2, waiting for transfers between devices, sent(): lax.all_to_all(slots, joined, split_axis=0, concat_axis=0, tiled=True)  180 us
    ppermute x4, waiting for transfers between devices, broadcast(): lax.ppermute(jnp.where(first, halves[1], one), axis, [(0, 1), (1, 2)])  36.4 us
    ppermute x4, waiting for transfers between devices, broadcast(): one = lax.ppermute(halves[0], axis, [(0, 1)])  29.6 us
    all_to_all x2, starting transfers between devices, sent(): lax.all_to_all(slots, joined, split_axis=0, concat_axis=0, tiled=True)  16.3 us
    pallas_call x2, Pallas kernels, pack(): pl.pallas_call(functools.partial(pack_kernel, second), in_specs=[SCALAR]...  14.3 us
    pallas_call x1, Pallas kernels, trail(): pl.pallas_call(trail_kernel, in_specs=[SCALAR] + [HELD] * (1 + 2 * ARRIVA...  11.2 us
    pallas_call x1, Pallas kernels, add_second(): pl.pallas_call(second_kernel, in_specs=[SCALAR, SCALAR, HELD, IN_HBM, HEL...  9.82 us
    ppermute x4, starting transfers between devices, broadcast(): lax.ppermute(jnp.where(first, halves[1], one), axis, [(0, 1), (1, 2)])  7.86 us
  transfers between devices with their start and end apart: 18, of which 8 were waited for; matrix products, arithmetic and copies ran while one was open for 1% of the time, Pallas kernels for 4%

profile of v4, /device:TPU:34, one launch (start us, length us, event | category | flops | bytes accessed | tf_op | source)
XLA Modules:
  0.0 335.4 jit_solution(3414285978011078040)
XLA Ops:
  0.0 5.5 %shard_map.118 = bf16[32,528,256]{2,1,0:T(8,128)(2,1)} custom-call(s32[28]{0:T(128)} %destination.3, s32[28]{0:T(128)} %place.3, s32[28]{0:T(128)} %ranks.3, bf16[28,256,256]{2,1,0:T(8,128)(2,1)} %left.3, bf16[28,256,256]{2,1,0:T(8,128)(2,1)} %right.3, s32[28,256]{1,0:T(8,128)} %rows.3, s32[28,256]{1,0:T(8,128)} %cols.3), custom_call_target="tpu_custom_call" | custom-call | flops 1879048192 | bytes 16777216 | tf_op jit(solution)/shard_map/pallas_call | solution.py:188
  5.5 7.2 %all-to-all-start = ((bf16[32,528,256]{2,1,0:T(8,128)(2,1)}), bf16[32,528,256]{2,1,0:T(8,128)(2,1)}, u32[]{:S(2)}, u32[]{:S(2)}) async-start(bf16[32,528,256]{2,1,0:T(8,128)(2,1)} %shard_map.118), calls=%async_computation | async-start | bytes 17301504 | tf_op jit(solution)/shard_map/all_to_all | solution.py:619
  12.7 8.8 %shard_map.120 = bf16[32,512,256]{2,1,0:T(8,128)(2,1)} custom-call(s32[28]{0:T(128)} %destination.3, s32[28]{0:T(128)} %place.3, s32[28]{0:T(128)} %ranks.3, bf16[28,256,256]{2,1,0:T(8,128)(2,1)} %left.3, bf16[28,256,256]{2,1,0:T(8,128)(2,1)} %right.3, s32[28,256]{1,0:T(8,128)} %rows.3, s32[28,256]{1,0:T(8,128)} %cols.3), custom_call_target="tpu_custom_call" | custom-call | flops 1879048192 | bytes 16777216 | tf_op jit(solution)/shard_map/pallas_call | solution.py:188
  21.6 92.0 %all-to-all-done.slots = bf16[32,528,256]{2,1,0:T(8,128)(2,1)} async-done(((bf16[32,528,256]{2,1,0:T(8,128)(2,1)}), bf16[32,528,256]{2,1,0:T(8,128)(2,1)}, u32[]{:S(2)}, u32[]{:S(2)}) %all-to-all-start) | async-done | bytes 8650784 | tf_op jit(solution)/shard_map/all_to_all | solution.py:619
  113.5 9.0 %all-to-all-start.1 = ((bf16[32,512,256]{2,1,0:T(8,128)(2,1)}), bf16[32,512,256]{2,1,0:T(8,128)(2,1)}, u32[]{:S(2)}, u32[]{:S(2)}) async-start(bf16[32,512,256]{2,1,0:T(8,128)(2,1)} %shard_map.120), calls=%async_computation.1 | async-start | bytes 16777216 | tf_op jit(solution)/shard_map/all_to_all | solution.py:619
  123.6 6.1 %shard_map.119.before = f32[2,768,768]{2,1,0:T(8,128)S(1)} custom-call(s32[32]{0:T(128)S(1)} %get-tuple-element.25.places, s32[4]{0:T(128)S(1)} %copy-done.6, f32[2,768,768]{2,1,0:T(8,128)} %bitcast.11, bf16[4,256,256]{2,1,0:T(8,128)(2,1)S(1)} %copy-done.4, bf16[4,256,256]{2,1,0:T(8,128)(2,1)S(1)} %copy-done.5, bf16[32,528,256]{2,1,0:T(8,128)(2,1)} %all-to-all-done.slots), custom_call_target="tpu_custom_call" | custom-call | flops 2147483648 | bytes 20971520 | tf_op jit(solution)/shard_map/pallas_call | solution.py:368
  129.8 2.2 copy-done
  132.0 87.7 %all-to-all-done.1.slots = bf16[32,512,256]{2,1,0:T(8,128)(2,1)} async-done(((bf16[32,512,256]{2,1,0:T(8,128)(2,1)}), bf16[32,512,256]{2,1,0:T(8,128)(2,1)}, u32[]{:S(2)}, u32[]{:S(2)}) %all-to-all-start.1) | async-done | bytes 8388640 | tf_op jit(solution)/shard_map/all_to_all | solution.py:619
  219.7 9.8 %shard_map.121 = (f32[2,768,768]{2,1,0:T(8,128)S(1)}, s16[400,512]{1,0:T(8,128)(2,1)S(1)}, s16[400,512]{1,0:T(8,128)(2,1)S(1)}, s16[272,768]{1,0:T(8,128)(2,1)S(1)}, s16[272,768]{1,0:T(8,128)(2,1)S(1)}) custom-call(s32[32]{0:T(128)S(1)} %get-tuple-element.26.places, s32[2]{0:T(128)S(1)} %pad_add_fusion.role, f32[2,768,768]{2,1,0:T(8,128)} %copy-done, ...), custom_call_target="tpu_custom_call" | custom-call | flops 2147483648 | bytes 20971520 | tf_op jit(solution)/shard_map/pallas_call | solution.py:396
  229.5 2.2 copy-done.1
  233.1 1.6 collective-permute-start.4
  234.7 1.3 collective-permute-start
  237.6 10.7 %collective-permute-done.4.refs_4_ = s16[272,768]{1,0:T(8,128)(2,1)S(1)} collective-permute-done((s16[272,768]{1,0:T(8,128)(2,1)S(1)}, s16[272,768]{1,0:T(8,128)(2,1)S(1)}, u32[]{:S(2)}, u32[]{:S(2)}) %collective-permute-start.4) | collective-permute-done | bytes 417824 | tf_op jit(solution)/shard_map/ppermute | solution.py:584
  248.5 1.9 collective-permute-start.6
  250.4 1.5 collective-permute-done.refs_0_
  252.0 2.1 collective-permute-start.2
  254.2 14.5 %collective-permute-done.2.refs_2_ = s16[400,512]{1,0:T(8,128)(2,1)S(1)} collective-permute-done((s16[400,512]{1,0:T(8,128)(2,1)S(1)}, s16[400,512]{1,0:T(8,128)(2,1)S(1)}, u32[]{:S(2)}, u32[]{:S(2)}) %collective-permute-start.2) | collective-permute-done | bytes 409632 | tf_op jit(solution)/shard_map/ppermute | solution.py:586
  268.6 5.7 %shard_map.122 = (f32[2,768,768]{2,1,0:T(8,128)S(1)}, s16[400,1024]{1,0:T(8,128)(2,1)S(1)}, s16[400,1024]{1,0:T(8,128)(2,1)S(1)}, s16[528,768]{1,0:T(8,128)(2,1)S(1)}, s16[528,768]{1,0:T(8,128)(2,1)S(1)}) custom-call(s32[2]{0:T(128)S(1)} %pad_add_fusion.role, f32[2,768,768]{2,1,0:T(8,128)S(1)} %copy-done.2, ...), custom_call_target="tpu_custom_call" | custom-call | tf_op jit(solution)/shard_map/pallas_call | solution.py:528
  275.8 1.3 collective-permute-start.8
  280.4 17.2 %collective-permute-done.8.refs_0_ = s16[400,1024]{1,0:T(8,128)(2,1)S(1)} collective-permute-done((s16[400,1024]{1,0:T(8,128)(2,1)S(1)}, s16[400,1024]{1,0:T(8,128)(2,1)S(1)}, u32[]{:S(2)}, u32[]{:S(2)}) %collective-permute-start.8) | collective-permute-done | bytes 819232 | tf_op jit(solution)/shard_map/ppermute | solution.py:584
  297.9 1.9 collective-permute-start.10
  300.1 1.9 collective-permute-start.14
  302.1 21.9 %collective-permute-done.14.refs_6_ = s16[528,768]{1,0:T(8,128)(2,1)S(1)} collective-permute-done((s16[528,768]{1,0:T(8,128)(2,1)S(1)}, s16[528,768]{1,0:T(8,128)(2,1)S(1)}, u32[]{:S(2)}, u32[]{:S(2)}) %collective-permute-start.14) | collective-permute-done | bytes 811040 | tf_op jit(solution)/shard_map/ppermute | solution.py:586
  324.0 11.2 %shard_map.123 = f32[2,768,768]{2,1,0:T(8,128)} custom-call(s32[2]{0:T(128)S(1)} %pad_add_fusion.role, f32[2,768,768]{2,1,0:T(8,128)S(1)} %get-tuple-element.20.block, s16[400,1024]{1,0:T(8,128)(2,1)S(1)} %collective-permute-done.8.refs_0_, s16[400,1024]{1,0:T(8,128)(2,1)S(1)} %collective-permute-done.9.refs_1_, ...), custom_call_target="tpu_custom_call" | custom-call | tf_op jit(solution)/shard_map/pallas_call | solution.py:570
  (44 shorter events, 9.6 us)
Async XLA Ops:
  5.5 108.1 %all-to-all-start = ((bf16[32,528,256]{2,1,0:T(8,128)(2,1)}), bf16[32,528,256]{2,1,0:T(8,128)(2,1)}, u32[]{:S(2)}, u32[]{:S(2)}) async-start(bf16[32,528,256]{2,1,0:T(8,128)(2,1)} %shard_map.118), calls=%async_computation | async-start | bytes 17301504 | tf_op jit(solution)/shard_map/all_to_all | solution.py:619
  21.5 102.1 %copy-start.4 = (bf16[4,256,256]{2,1,0:T(8,128)(2,1)S(1)}, bf16[4,256,256]{2,1,0:T(8,128)(2,1)}, u32[]{:S(2)}) copy-start(bf16[4,256,256]{2,1,0:T(8,128)(2,1)} %own_left.1) | copy-start | bytes 1572868
  21.5 102.1 %copy-start.5 = (bf16[4,256,256]{2,1,0:T(8,128)(2,1)S(1)}, bf16[4,256,256]{2,1,0:T(8,128)(2,1)}, u32[]{:S(2)}) copy-start(bf16[4,256,256]{2,1,0:T(8,128)(2,1)} %own_right.1) | copy-start | bytes 1572868
  21.6 102.1 %copy-start.6 = (s32[4]{0:T(128)S(1)}, s32[4]{0:T(128)}, u32[]{:S(2)}) copy-start(s32[4]{0:T(128)} %own_places.1) | copy-start | bytes 52
  113.5 106.1 %all-to-all-start.1 = ((bf16[32,512,256]{2,1,0:T(8,128)(2,1)}), bf16[32,512,256]{2,1,0:T(8,128)(2,1)}, u32[]{:S(2)}, u32[]{:S(2)}) async-start(bf16[32,512,256]{2,1,0:T(8,128)(2,1)} %shard_map.120), calls=%async_computation.1 | async-start | bytes 16777216 | tf_op jit(solution)/shard_map/all_to_all | solution.py:619
  123.6 96.0 %copy-start.3 = (f32[1,3,2,256,256]{4,3,2,1,0:T(8,128)S(1)}, f32[1,3,2,256,256]{4,3,2,1,0:T(8,128)}, u32[]{:S(2)}) copy-start(f32[1,3,2,256,256]{4,3,2,1,0:T(8,128)} %param.23) | copy-start | bytes 4718596
  129.8 2.2 copy-start
  231.7 4.3 %collective-permute-start.1 = (s16[400,512]{1,0:T(8,128)(2,1)S(1)}, s16[400,512]{1,0:T(8,128)(2,1)S(1)}, u32[]{:S(2)}, u32[]{:S(2)}) collective-permute-start(s16[400,512]{1,0:T(8,128)(2,1)S(1)} %get-tuple-element.17), channel_id=1, source_target_pairs={{0,3},{4,7},{8,11},{12,15},{16,19},{20,23},{24,27},{28,31},{32,35}... | collective-permute-start | bytes 1228808 | tf_op jit(solution)/shard_map/ppermute | solution.py:585
  232.4 4.4 %collective-permute-start.5 = (s16[272,768]{1,0:T(8,128)(2,1)S(1)}, s16[272,768]{1,0:T(8,128)(2,1)S(1)}, u32[]{:S(2)}, u32[]{:S(2)}) collective-permute-start(s16[272,768]{1,0:T(8,128)(2,1)S(1)} %get-tuple-element.19), channel_id=1, source_target_pairs={{0,12},{1,13},{2,14},{3,15},{16,28},{17,29},{18,30},{19,31},{32,44... | collective-permute-start | bytes 1253384 | tf_op jit(solution)/shard_map/ppermute | solution.py:585
  233.1 35.6 %copy-start.2 = (f32[2,768,768]{2,1,0:T(8,128)S(1)}, f32[2,768,768]{2,1,0:T(8,128)}, u32[]{:S(2)}) copy-start(f32[2,768,768]{2,1,0:T(8,128)} %copy-done.1) | copy-start | bytes 14155780
  233.1 15.2 %collective-permute-start.4 = (s16[272,768]{1,0:T(8,128)(2,1)S(1)}, s16[272,768]{1,0:T(8,128)(2,1)S(1)}, u32[]{:S(2)}, u32[]{:S(2)}) collective-permute-start(s16[272,768]{1,0:T(8,128)(2,1)S(1)} %get-tuple-element.18), channel_id=1, source_target_pairs={{0,4},{1,5},{2,6},{3,7},{16,20},{17,21},{18,22},{19,23},{32,36},{3... | collective-permute-start | bytes 1253384 | tf_op jit(solution)/shard_map/ppermute | solution.py:584
  234.7 17.3 %collective-permute-start = (s16[400,512]{1,0:T(8,128)(2,1)S(1)}, s16[400,512]{1,0:T(8,128)(2,1)S(1)}, u32[]{:S(2)}, u32[]{:S(2)}) collective-permute-start(s16[400,512]{1,0:T(8,128)(2,1)S(1)} %get-tuple-element.16), channel_id=1, source_target_pairs={{0,1},{4,5},{8,9},{12,13},{16,17},{20,21},{24,25},{28,29},{32,33},... | collective-permute-start | bytes 1228808 | tf_op jit(solution)/shard_map/ppermute | solution.py:584
  236.1 18.1 %collective-permute-start.3 = (s16[400,512]{1,0:T(8,128)(2,1)S(1)}, s16[400,512]{1,0:T(8,128)(2,1)S(1)}, u32[]{:S(2)}, u32[]{:S(2)}) collective-permute-start(s16[400,512]{1,0:T(8,128)(2,1)S(1)} %broadcast_select_fusion.6), channel_id=1, source_target_pairs={{0,3},{3,2},{4,7},{7,6},{8,11},{11,10},{12,15},{15,14},{16,19},{19... | collective-permute-start | bytes 1228808 | tf_op jit(solution)/shard_map/ppermute | solution.py:587
  236.9 31.7 %collective-permute-start.7 = (s16[272,768]{1,0:T(8,128)(2,1)S(1)}, s16[272,768]{1,0:T(8,128)(2,1)S(1)}, u32[]{:S(2)}, u32[]{:S(2)}) collective-permute-start(s16[272,768]{1,0:T(8,128)(2,1)S(1)} %broadcast_select_fusion.4), channel_id=1, source_target_pairs={{0,12},{12,8},{1,13},{13,9},{2,14},{14,10},{3,15},{15,11},{16,28},... | collective-permute-start | bytes 1253384 | tf_op jit(solution)/shard_map/ppermute | solution.py:587
  248.5 20.2 %collective-permute-start.6 = (s16[272,768]{1,0:T(8,128)(2,1)S(1)}, s16[272,768]{1,0:T(8,128)(2,1)S(1)}, u32[]{:S(2)}, u32[]{:S(2)}) collective-permute-start(s16[272,768]{1,0:T(8,128)(2,1)S(1)} %broadcast_select_fusion.5), channel_id=1, source_target_pairs={{0,4},{4,8},{1,5},{5,9},{2,6},{6,10},{3,7},{7,11},{16,20},{20,24},... | collective-permute-start | bytes 1253384 | tf_op jit(solution)/shard_map/ppermute | solution.py:586
  252.0 16.6 %collective-permute-start.2 = (s16[400,512]{1,0:T(8,128)(2,1)S(1)}, s16[400,512]{1,0:T(8,128)(2,1)S(1)}, u32[]{:S(2)}, u32[]{:S(2)}) collective-permute-start(s16[400,512]{1,0:T(8,128)(2,1)S(1)} %broadcast_select_fusion.7), channel_id=1, source_target_pairs={{0,1},{1,2},{4,5},{5,6},{8,9},{9,10},{12,13},{13,14},{16,17},{17,1... | collective-permute-start | bytes 1228808 | tf_op jit(solution)/shard_map/ppermute | solution.py:586
  274.3 4.0 %collective-permute-start.13 = (s16[528,768]{1,0:T(8,128)(2,1)S(1)}, s16[528,768]{1,0:T(8,128)(2,1)S(1)}, u32[]{:S(2)}, u32[]{:S(2)}) collective-permute-start(s16[528,768]{1,0:T(8,128)(2,1)S(1)} %get-tuple-element.24), channel_id=1, source_target_pairs={{0,12},{1,13},{2,14},{3,15},{16,28},{17,29},{18,30},{19,31},{32,44... | collective-permute-start | bytes 2433032 | tf_op jit(solution)/shard_map/ppermute | solution.py:585
  275.0 4.3 %collective-permute-start.9 = (s16[400,1024]{1,0:T(8,128)(2,1)S(1)}, s16[400,1024]{1,0:T(8,128)(2,1)S(1)}, u32[]{:S(2)}, u32[]{:S(2)}) collective-permute-start(s16[400,1024]{1,0:T(8,128)(2,1)S(1)} %get-tuple-element.22), channel_id=1, source_target_pairs={{0,3},{4,7},{8,11},{12,15},{16,19},{20,23},{24,27},{28,31},{32,35}... | collective-permute-start | bytes 2457608 | tf_op jit(solution)/shard_map/ppermute | solution.py:585
  275.8 21.8 %collective-permute-start.8 = (s16[400,1024]{1,0:T(8,128)(2,1)S(1)}, s16[400,1024]{1,0:T(8,128)(2,1)S(1)}, u32[]{:S(2)}, u32[]{:S(2)}) collective-permute-start(s16[400,1024]{1,0:T(8,128)(2,1)S(1)} %get-tuple-element.21), channel_id=1, source_target_pairs={{0,1},{4,5},{8,9},{12,13},{16,17},{20,21},{24,25},{28,29},{32,33},... | collective-permute-start | bytes 2457608 | tf_op jit(solution)/shard_map/ppermute | solution.py:584
  277.1 22.9 %collective-permute-start.12 = (s16[528,768]{1,0:T(8,128)(2,1)S(1)}, s16[528,768]{1,0:T(8,128)(2,1)S(1)}, u32[]{:S(2)}, u32[]{:S(2)}) collective-permute-start(s16[528,768]{1,0:T(8,128)(2,1)S(1)} %get-tuple-element.23), channel_id=1, source_target_pairs={{0,4},{1,5},{2,6},{3,7},{16,20},{17,21},{18,22},{19,23},{32,36},{3... | collective-permute-start | bytes 2433032 | tf_op jit(solution)/shard_map/ppermute | solution.py:584
  278.6 23.5 %collective-permute-start.15 = (s16[528,768]{1,0:T(8,128)(2,1)S(1)}, s16[528,768]{1,0:T(8,128)(2,1)S(1)}, u32[]{:S(2)}, u32[]{:S(2)}) collective-permute-start(s16[528,768]{1,0:T(8,128)(2,1)S(1)} %broadcast_select_fusion.2), channel_id=1, source_target_pairs={{0,12},{12,8},{1,13},{13,9},{2,14},{14,10},{3,15},{15,11},{16,28},... | collective-permute-start | bytes 2433032 | tf_op jit(solution)/shard_map/ppermute | solution.py:587
  279.6 44.4 %collective-permute-start.11 = (s16[400,1024]{1,0:T(8,128)(2,1)S(1)}, s16[400,1024]{1,0:T(8,128)(2,1)S(1)}, u32[]{:S(2)}, u32[]{:S(2)}) collective-permute-start(s16[400,1024]{1,0:T(8,128)(2,1)S(1)} %broadcast_select_fusion), channel_id=1, source_target_pairs={{0,3},{3,2},{4,7},{7,6},{8,11},{11,10},{12,15},{15,14},{16,19},{19... | collective-permute-start | bytes 2457608 | tf_op jit(solution)/shard_map/ppermute | solution.py:587
  297.9 26.1 %collective-permute-start.10 = (s16[400,1024]{1,0:T(8,128)(2,1)S(1)}, s16[400,1024]{1,0:T(8,128)(2,1)S(1)}, u32[]{:S(2)}, u32[]{:S(2)}) collective-permute-start(s16[400,1024]{1,0:T(8,128)(2,1)S(1)} %broadcast_select_fusion.1), channel_id=1, source_target_pairs={{0,1},{1,2},{4,5},{5,6},{8,9},{9,10},{12,13},{13,14},{16,17},{17,1... | collective-permute-start | bytes 2457608 | tf_op jit(solution)/shard_map/ppermute | solution.py:586
  300.1 23.9 %collective-permute-start.14 = (s16[528,768]{1,0:T(8,128)(2,1)S(1)}, s16[528,768]{1,0:T(8,128)(2,1)S(1)}, u32[]{:S(2)}, u32[]{:S(2)}) collective-permute-start(s16[528,768]{1,0:T(8,128)(2,1)S(1)} %broadcast_select_fusion.3), channel_id=1, source_target_pairs={{0,4},{4,8},{1,5},{5,9},{2,6},{6,10},{3,7},{7,11},{16,20},{20,24},... | collective-permute-start | bytes 2433032 | tf_op jit(solution)/shard_map/ppermute | solution.py:586
  (1 other events, 2.2 us)

commit v5 on v4

--- a/solution.py
+++ b/solution.py
@@ -17,6 +17,7 @@
 HALVES = 2
 ARRIVALS = 4
 CHUNK = 64
+LONG = SIDE // HALVES
 CODE_ROWS = 16
 NOTE_ROWS = 16
 LOG_STEP = math.log(2.0) / 32.0
@@ -317,7 +318,6 @@
         out[...] = before[...]
 
     add_slots(out, places, slots, refs[2 * HALVES :], prepare)
-    long = SIDE // HALVES
 
     @pl.when((role[0] == 0) & (role[1] == 0))
     def _():
@@ -339,7 +339,7 @@
         ]
         upper = [jnp.concatenate([x[half] for x in upper], 1) for half in (0, 1)]
         for half in range(HALVES):
-            store_piece(along_row[half], lower[half * long : (half + 1) * long])
+            store_piece(along_row[half], lower[half * LONG : (half + 1) * LONG])
             store_piece(along_col[half], upper[half])
 
     @pl.when((role[0] > 0) & (role[1] == 0))
@@ -350,7 +350,7 @@
                 at = tile_at(i, p)
                 put(out, *at, complex_dot(cuts(get(out, *at)), pivot))
         for half in range(HALVES):
-            rows = slice(half * long, (half + 1) * long)
+            rows = slice(half * LONG, (half + 1) * LONG)
             store_piece(along_row[half], jnp.concatenate(get(out, rows, slice(0, TILE)), 1))
 
     @pl.when((role[0] == 0) & (role[1] > 0))
@@ -404,17 +404,19 @@
     )(places, role, before, slots, inverse)
 
 
+def scales(code_rows):
+    return jnp.exp(code_rows[:1].astype(jnp.int32).astype(F32) * LOG_STEP)
+
+
 def unpack(refs, place, high, low):
     one, three, plus, minus = refs
     half = one.shape[0] - CODE_ROWS
-    scales = lambda ref: jnp.exp(ref[half:, :][:1].astype(jnp.int32).astype(F32) * LOG_STEP)
-
     for at, pair in ((1, (one, plus)), (2, (plus, minus)), (3, (minus, three))):
 
         @pl.when(place == at)
         def _(pair=pair):
             for which, ref in enumerate(pair):
-                scale = scales(ref)
+                scale = scales(ref[half:, :])
 
                 def chunk(i, carry, ref=ref, scale=scale, which=which):
                     rows = pl.ds(pl.multiple_of(i * CHUNK, CHUNK), CHUNK)
@@ -453,9 +455,8 @@
 
 def panel_kernel(role, block, *refs):
     from_row, from_col = refs[:ARRIVALS], refs[ARRIVALS : 2 * ARRIVALS]
-    out, *refs = refs[2 * ARRIVALS :]
-    along_row, along_col = refs[:HALVES], refs[HALVES : 2 * HALVES]
-    row_high, row_low, col_high, col_low = refs[2 * HALVES :]
+    out, *halves = refs[2 * ARRIVALS : 2 * ARRIVALS + 1 + HALVES]
+    row_high, row_low, col_high, col_low = refs[2 * ARRIVALS + 1 + HALVES :]
     parts = [slice(t * TILE, (t + 1) * TILE) for t in range(TS)]
 
     @pl.when(role[1] > 0)
@@ -487,11 +488,11 @@
             return carry
 
         lax.fori_loop(0, TS, chunk, 0)
-        long = SIDE // HALVES
-        for half in range(HALVES):
-            rows = slice(half * long, (half + 1) * long)
+        for which, ref in enumerate(halves):
+            half = which ^ (role[0] == ROW_TURNED).astype(jnp.int32)
+            rows = pl.ds(pl.multiple_of(half * LONG, LONG), LONG)
             wide = [x for cols in parts[1:] for x in get(out, rows, cols)]
-            store_piece(along_row[half], jnp.concatenate(wide, 1))
+            store_piece(ref, jnp.concatenate(wide, 1))
 
     @pl.when((role[0] == 0) & (role[1] > 0))
     def _():
@@ -510,9 +511,12 @@
             return carry
 
         lax.fori_loop(0, TS, chunk, 0)
-        for half in range(HALVES):
-            both = get(out, parts[half + 1], slice(0, SIDE))
-            store_piece(along_col[half], jnp.concatenate(both, 0))
+        for which, ref in enumerate(halves):
+            half = which ^ (role[1] == COL_TURNED).astype(jnp.int32)
+            rows = pl.ds(pl.multiple_of((half + 1) * TILE, TILE), TILE)
+            tall = jnp.concatenate(get(out, rows, slice(0, SIDE)), 0)
+            rest = jnp.concatenate([tall[LONG:, cols] for cols in parts], 0)
+            store_piece(ref, jnp.concatenate([tall[:LONG], rest], 1))
 
     @pl.when((role[0] > 0) & (role[1] > 0))
     def _():
@@ -528,16 +532,16 @@
     return pl.pallas_call(
         panel_kernel,
         in_specs=[SCALAR] + [HELD] * (1 + 2 * ARRIVALS),
-        out_specs=[HELD] * (1 + 2 * HALVES),
-        out_shape=[jax.ShapeDtypeStruct(block.shape, F32)] + pieces_of(2),
+        out_specs=[HELD] * (1 + HALVES),
+        out_shape=[jax.ShapeDtypeStruct(block.shape, F32)] + [coded(row_shape(2))] * HALVES,
         scratch_shapes=piece_scratch(1),
         compiler_params=pltpu.CompilerParams(vmem_limit_bytes=VMEM_BYTES),
     )(role, block, *from_row, *from_col)
 
 
-def trail_kernel(role, block, *refs):
-    from_row, from_col = refs[:ARRIVALS], refs[ARRIVALS : 2 * ARRIVALS]
-    out, held, row_high, row_low, col_high, col_low, sem, sems = refs[2 * ARRIVALS :]
+def trail_kernel(role, source, block, *refs):
+    moved = refs[:MOVES]
+    out, held, got, row_high, row_low, col_high, col_low, sem, sems, got_sems = refs[MOVES:]
     inner = (role[0] > 0) & (role[1] > 0)
 
     @pl.when(jnp.logical_not(inner))
@@ -548,8 +552,36 @@
 
     @pl.when(inner)
     def _():
-        unpack(from_row, role[1], row_high, row_low)
-        unpack(from_col, role[0], col_high, col_low)
+        first = (role[0] * 4 + role[1]) * 2 * HALVES
+        for k in range(2 * HALVES):
+            for m in range(MOVES):
+
+                @pl.when(source[first + k] == m)
+                def _(k=k, m=m):
+                    pltpu.make_async_copy(moved[m], got.at[k], got_sems.at[k]).start()
+
+        for k in range(2 * HALVES):
+            pltpu.make_async_copy(moved[0], got.at[k], got_sems.at[k]).wait()
+            scale = scales(got[k, LONG:, :])
+            half = k % HALVES
+
+            def chunk(i, carry, k=k, half=half, scale=scale):
+                rows = pl.ds(pl.multiple_of(i * CHUNK, CHUNK), CHUNK)
+                high, low = cut(got[k, rows, :].astype(jnp.int32).astype(F32) * scale)
+                if k < HALVES:
+                    into = pl.ds(pl.multiple_of(half * LONG + i * CHUNK, CHUNK), CHUNK)
+                    row_high[into, :], row_low[into, :] = high, low
+                else:
+                    start = half * 2 * TILE + i * CHUNK
+                    into = pl.ds(pl.multiple_of(start, CHUNK), CHUNK)
+                    col_high[into, :], col_low[into, :] = high[:, :SIDE], low[:, :SIDE]
+                    start = half * 2 * TILE + LONG + (i & 1) * CHUNK
+                    into = pl.ds(pl.multiple_of(start, CHUNK), CHUNK)
+                    cols = pl.ds(pl.multiple_of((i >> 1) * TILE, TILE), TILE)
+                    col_high[into, cols], col_low[into, cols] = high[:, SIDE:], low[:, SIDE:]
+                return carry
+
+            lax.fori_loop(0, LONG // CHUNK, chunk, 0)
 
         def store(i):
             rows = pl.ds(pl.multiple_of(i * TILE, TILE), TILE)
@@ -566,17 +598,75 @@
             store(i).wait()
 
 
-def trail(role, block, from_row, from_col):
+def trail(role, source, block, moved):
     return pl.pallas_call(
         trail_kernel,
-        in_specs=[SCALAR] + [HELD] * (1 + 2 * ARRIVALS),
+        in_specs=[SCALAR] * 2 + [HELD] * (1 + MOVES),
         out_specs=IN_HBM,
         out_shape=jax.ShapeDtypeStruct(block.shape, F32),
-        scratch_shapes=[pltpu.VMEM(block.shape, F32)]
+        scratch_shapes=[
+            pltpu.VMEM(block.shape, F32),
+            pltpu.VMEM((2 * HALVES,) + row_shape(2), jnp.int16),
+        ]
         + piece_scratch(2)
-        + [pltpu.SemaphoreType.DMA, pltpu.SemaphoreType.DMA((TS,))],
+        + [
+            pltpu.SemaphoreType.DMA,
+            pltpu.SemaphoreType.DMA((TS,)),
+            pltpu.SemaphoreType.DMA((2 * HALVES,)),
+        ],
         compiler_params=pltpu.CompilerParams(vmem_limit_bytes=VMEM_BYTES),
-    )(role, block, *from_row, *from_col)
+    )(role, source, block, *moved)
+
+
+ROW_WAY = {1: 1, 2: 1, 3: 3}
+COL_WAY = {1: 3, 2: 1, 3: 1}
+ROW_TURNED, COL_TURNED = 3, 1
+MOVES = 8
+
+
+def ways(turn):
+    def way(table, line):
+        return 4 - table[line] if turn else table[line]
+
+    return [(r, way(ROW_WAY, r)) for r in ROW_WAY], [(way(COL_WAY, c), c) for c in COL_WAY]
+
+
+def move_all(halves):
+    def move(array, pairs):
+        pairs = [(4 * a + b, 4 * c + d) for (a, b), (c, d) in pairs]
+        return lax.ppermute(array, ("row", "col"), pairs)
+
+    out, on, late = [], [], []
+    for turn in (0, 1):
+        rows, cols = ways(turn)
+        out.append([((r, 0), (r, c)) for r, c in rows] + [((0, c), (r, c)) for r, c in cols])
+        on.append(
+            [((r, c), (r, 2)) for r, c in rows] + [((r, c), (2, c)) for r, c in cols if c != 2]
+        )
+        late.append([((r, c), (2, c)) for r, c in cols if c == 2])
+    first = [move(halves[turn], out[turn]) for turn in (0, 1)]
+    second = [move(halves[1 - turn], out[turn]) for turn in (0, 1)]
+    onward = [move(first[turn], on[turn]) for turn in (0, 1)]
+    return first + second + onward + [move(first[turn], late[turn]) for turn in (0, 1)]
+
+
+def sources():
+    table = [0] * (16 * 2 * HALVES)
+
+    def enter(row, col, slot, half, array):
+        table[(row * 4 + col) * 2 * HALVES + slot * HALVES + half] = array
+
+    for turn in (0, 1):
+        rows, cols = ways(turn)
+        for slot, devices in ((0, rows), (1, cols)):
+            for r, c in devices:
+                half = 0 if (c if slot == 0 else r) == 1 else 1
+                enter(r, c, slot, half, turn)
+                enter(r, c, slot, 1 - half, 2 + turn)
+                middle = (r, 2) if slot == 0 else (2, c)
+                both = slot == 1 and c == 2
+                enter(*middle, slot, half, (6 if both else 4) + turn)
+    return table
 
 
 def broadcast(halves, axis):
@@ -625,9 +715,8 @@
     block = add_first(places[:, 0], own_place, parent_front[0], own_left, own_right, second_slots)
     block, *pieces = add_second(places[:, 1], role, block, first_slots, pivot_inverse[0])
     from_row, from_col = broadcast(pieces[:HALVES], "col"), broadcast(pieces[HALVES:], "row")
-    block, *pieces = panel(role, block, from_row, from_col)
-    from_row, from_col = broadcast(pieces[:HALVES], "col"), broadcast(pieces[HALVES:], "row")
-    return trail(role, block, from_row, from_col)[None]
+    block, *halves = panel(role, block, from_row, from_col)
+    return trail(role, jnp.array(sources(), jnp.int32), block, move_all(halves))[None]
 
 
 def solution(mesh):

time: 337 us -> 332 us (0.985)
  waiting for transfers between devices: 246 us -> 240 us
    ppermute x0 -> x8, waiting for transfers between devices: none -> 33.1 us  [move(): return lax.ppermute(array, ('row', 'col'), pairs)]
    ppermute x4 -> x2, waiting for transfers between devices: 36.4 us -> 16.4 us  [broadcast(): lax.ppermute(jnp.where(first, halves[1], one), axis, [(0, 1), (1, 2)])]
    ppermute x4 -> x2, waiting for transfers between devices: 29.6 us -> 11.8 us  [broadcast(): one = lax.ppermute(halves[0], axis, [(0, 1)])]
    ppermute x0 -> x8, starting transfers between devices: none -> 9.42 us  [move(): return lax.ppermute(array, ('row', 'col'), pairs)]
    ppermute x4 -> x2, starting transfers between devices: 7.86 us -> 4.02 us  [broadcast(): lax.ppermute(jnp.where(first, halves[1], one), axis, [(0, 1), (1, 2)])]
  transfers between devices with their start and end apart: 18 -> 18, of which waited for: 8 -> 9; matrix products, arithmetic and copies ran while one was open for 1% -> 0% of each run, Pallas kernels for 4% -> 5%
where the time goes in v5:
time: 332 us; the launch traced here: 331 us
  waiting for transfers between devices  240 us (72%)
  Pallas kernels  47 us (14%)
  starting transfers between devices  37.1 us (11%)
  local copies, waits for them, and re-layouts  4.5 us (1%)
    all_to_all x2, waiting for transfers between devices, sent(): lax.all_to_all(slots, joined, split_axis=0, concat_axis=0, tiled=True)  179 us
    ppermute x8, waiting for transfers between devices, move(): return lax.ppermute(array, ('row', 'col'), pairs)  33.1 us
    all_to_all x2, starting transfers between devices, sent(): lax.all_to_all(slots, joined, split_axis=0, concat_axis=0, tiled=True)  18.1 us
    ppermute x2, waiting for transfers between devices, broadcast(): lax.ppermute(jnp.where(first, halves[1], one), axis, [(0, 1), (1, 2)])  16.4 us
    pallas_call x2, Pallas kernels, pack(): pl.pallas_call(functools.partial(pack_kernel, second), in_specs=[SCALAR]...  14.3 us
    pallas_call x1, Pallas kernels, trail(): pl.pallas_call(trail_kernel, in_specs=[SCALAR] * 2 + [HELD] * (1 + MOVES)...  11.8 us
    ppermute x2, waiting for transfers between devices, broadcast(): one = lax.ppermute(halves[0], axis, [(0, 1)])  11.8 us
    ppermute x8, starting transfers between devices, move(): return lax.ppermute(array, ('row', 'col'), pairs)  9.42 us
  transfers between devices with their start and end apart: 18, of which 9 were waited for; matrix products, arithmetic and copies ran while one was open for 0% of the time, Pallas kernels for 5%

profile of v5, /device:TPU:34, one launch (start us, length us, event | category | flops | bytes accessed | tf_op | source)
XLA Modules:
  0.0 330.7 jit_solution(6860636674822647370)
XLA Ops:
  0.0 4.6 %shard_map.127 = bf16[32,528,256]{2,1,0:T(8,128)(2,1)} custom-call(s32[28]{0:T(128)} %destination.3, s32[28]{0:T(128)} %place.3, s32[28]{0:T(128)} %ranks.3, bf16[28,256,256]{2,1,0:T(8,128)(2,1)} %left.3, bf16[28,256,256]{2,1,0:T(8,128)(2,1)} %right.3, s32[28,256]{1,0:T(8,128)} %rows.3, s32[28,256]{1,0:T(8,128)} %cols.3), custom_call_target="tpu_custom_call" | custom-call | flops 1879048192 | bytes 16777216 | tf_op jit(solution)/shard_map/pallas_call | solution.py:189
  4.6 9.1 %all-to-all-start = ((bf16[32,528,256]{2,1,0:T(8,128)(2,1)}), bf16[32,528,256]{2,1,0:T(8,128)(2,1)}, u32[]{:S(2)}, u32[]{:S(2)}) async-start(bf16[32,528,256]{2,1,0:T(8,128)(2,1)} %shard_map.127), calls=%async_computation | async-start | bytes 17301504 | tf_op jit(solution)/shard_map/all_to_all | solution.py:709
  13.7 9.7 %shard_map.129 = bf16[32,512,256]{2,1,0:T(8,128)(2,1)} custom-call(s32[28]{0:T(128)} %destination.3, s32[28]{0:T(128)} %place.3, s32[28]{0:T(128)} %ranks.3, bf16[28,256,256]{2,1,0:T(8,128)(2,1)} %left.3, bf16[28,256,256]{2,1,0:T(8,128)(2,1)} %right.3, s32[28,256]{1,0:T(8,128)} %rows.3, s32[28,256]{1,0:T(8,128)} %cols.3), custom_call_target="tpu_custom_call" | custom-call | flops 1879048192 | bytes 16777216 | tf_op jit(solution)/shard_map/pallas_call | solution.py:189
  23.4 91.1 %all-to-all-done.slots = bf16[32,528,256]{2,1,0:T(8,128)(2,1)} async-done(((bf16[32,528,256]{2,1,0:T(8,128)(2,1)}), bf16[32,528,256]{2,1,0:T(8,128)(2,1)}, u32[]{:S(2)}, u32[]{:S(2)}) %all-to-all-start) | async-done | bytes 8650784 | tf_op jit(solution)/shard_map/all_to_all | solution.py:709
  114.6 9.0 %all-to-all-start.1 = ((bf16[32,512,256]{2,1,0:T(8,128)(2,1)}), bf16[32,512,256]{2,1,0:T(8,128)(2,1)}, u32[]{:S(2)}, u32[]{:S(2)}) async-start(bf16[32,512,256]{2,1,0:T(8,128)(2,1)} %shard_map.129), calls=%async_computation.1 | async-start | bytes 16777216 | tf_op jit(solution)/shard_map/all_to_all | solution.py:709
  124.7 5.9 %shard_map.128.before = f32[2,768,768]{2,1,0:T(8,128)S(1)} custom-call(s32[32]{0:T(128)S(1)} %get-tuple-element.21.places, s32[4]{0:T(128)S(1)} %copy-done.6, f32[2,768,768]{2,1,0:T(8,128)} %bitcast.11, bf16[4,256,256]{2,1,0:T(8,128)(2,1)S(1)} %copy-done.4, bf16[4,256,256]{2,1,0:T(8,128)(2,1)S(1)} %copy-done.5, bf16[32,528,256]{2,1,0:T(8,128)(2,1)} %all-to-all-done.slots), custom_call_target="tpu_custom_call" | custom-call | flops 2147483648 | bytes 20971520 | tf_op jit(solution)/shard_map/pallas_call | solution.py:368
  130.6 2.2 copy-done
  132.7 87.9 %all-to-all-done.1.slots = bf16[32,512,256]{2,1,0:T(8,128)(2,1)} async-done(((bf16[32,512,256]{2,1,0:T(8,128)(2,1)}), bf16[32,512,256]{2,1,0:T(8,128)(2,1)}, u32[]{:S(2)}, u32[]{:S(2)}) %all-to-all-start.1) | async-done | bytes 8388640 | tf_op jit(solution)/shard_map/all_to_all | solution.py:709
  220.6 9.3 %shard_map.130 = (f32[2,768,768]{2,1,0:T(8,128)S(1)}, s16[400,512]{1,0:T(8,128)(2,1)S(1)}, s16[400,512]{1,0:T(8,128)(2,1)S(1)}, s16[272,768]{1,0:T(8,128)(2,1)S(1)}, s16[272,768]{1,0:T(8,128)(2,1)S(1)}) custom-call(s32[32]{0:T(128)S(1)} %get-tuple-element.22.places, s32[2]{0:T(128)S(1)} %pad_add_fusion.role, f32[2,768,768]{2,1,0:T(8,128)} %copy-done, ...), custom_call_target="tpu_custom_call" | custom-call | flops 2147483648 | bytes 20971520 | tf_op jit(solution)/shard_map/pallas_call | solution.py:396
  230.0 2.2 copy-done.1
  233.6 1.6 collective-permute-start.4
  235.1 1.3 collective-permute-start
  238.1 11.5 %collective-permute-done.4.refs_4_ = s16[272,768]{1,0:T(8,128)(2,1)S(1)} collective-permute-done((s16[272,768]{1,0:T(8,128)(2,1)S(1)}, s16[272,768]{1,0:T(8,128)(2,1)S(1)}, u32[]{:S(2)}, u32[]{:S(2)}) %collective-permute-start.4) | collective-permute-done | bytes 417824 | tf_op jit(solution)/shard_map/ppermute | solution.py:674
  249.7 1.9 collective-permute-start.6
  252.0 2.1 collective-permute-start.2
  254.1 16.4 %collective-permute-done.2.refs_2_ = s16[400,512]{1,0:T(8,128)(2,1)S(1)} collective-permute-done((s16[400,512]{1,0:T(8,128)(2,1)S(1)}, s16[400,512]{1,0:T(8,128)(2,1)S(1)}, u32[]{:S(2)}, u32[]{:S(2)}) %collective-permute-start.2) | collective-permute-done | bytes 409632 | tf_op jit(solution)/shard_map/ppermute | solution.py:676
  270.5 5.7 %shard_map.131 = (f32[2,768,768]{2,1,0:T(8,128)S(1)}, s16[400,1024]{1,0:T(8,128)(2,1)S(1)}, s16[400,1024]{1,0:T(8,128)(2,1)S(1)}) custom-call(s32[2]{0:T(128)S(1)} %pad_add_fusion.role, f32[2,768,768]{2,1,0:T(8,128)S(1)} %copy-done.2, s16[400,512]{1,0:T(8,128)(2,1)S(1)} %collective-permute-done.refs_0_, s16[400,512]{1,0:T(8,128)(2,1)S(1)} %collective-permute-done.1.refs_1_, ...), custom_call_target="tpu_custom_call" | custom-call | tf_op jit(solution)/shard_map/pallas_call | solution.py:532
  276.2 1.3 collective-permute-start.8
  277.5 1.3 collective-permute-start.9
  281.4 17.8 %collective-permute-done.8.refs_0_ = s16[400,1024]{1,0:T(8,128)(2,1)S(1)} collective-permute-done((s16[400,1024]{1,0:T(8,128)(2,1)S(1)}, s16[400,1024]{1,0:T(8,128)(2,1)S(1)}, u32[]{:S(2)}, u32[]{:S(2)}) %collective-permute-start.8) | collective-permute-done | bytes 819232 | tf_op jit(solution)/shard_map/ppermute | solution.py:637
  299.2 1.5 collective-permute-start.12
  301.5 1.3 collective-permute-start.13
  302.8 12.7 %collective-permute-done.10.refs_2_ = s16[400,1024]{1,0:T(8,128)(2,1)S(1)} collective-permute-done((s16[400,1024]{1,0:T(8,128)(2,1)S(1)}, s16[400,1024]{1,0:T(8,128)(2,1)S(1)}, u32[]{:S(2)}, u32[]{:S(2)}) %collective-permute-start.10) | collective-permute-done | bytes 819232 | tf_op jit(solution)/shard_map/ppermute | solution.py:637
  318.8 11.8 %shard_map.132 = f32[2,768,768]{2,1,0:T(8,128)} custom-call(s32[2]{0:T(128)S(1)} %pad_add_fusion.role, s32[64]{0:T(128)S(1)} %copy-done.7, f32[2,768,768]{2,1,0:T(8,128)S(1)} %get-tuple-element.18.block, s16[400,1024]{1,0:T(8,128)(2,1)S(1)} %collective-permute-done.8.refs_0_, s16[400,1024]{1,0:T(8,128)(2,1)S(1)} %collective-permute-done.9.refs_1_, ...), custom_call_target="tpu_custom_call" | custom-call | tf_op jit(solution)/shard_map/pallas_call | solution.py:602
  (42 shorter events, 11.0 us)
Async XLA Ops:
  4.6 109.9 %all-to-all-start = ((bf16[32,528,256]{2,1,0:T(8,128)(2,1)}), bf16[32,528,256]{2,1,0:T(8,128)(2,1)}, u32[]{:S(2)}, u32[]{:S(2)}) async-start(bf16[32,528,256]{2,1,0:T(8,128)(2,1)} %shard_map.127), calls=%async_computation | async-start | bytes 17301504 | tf_op jit(solution)/shard_map/all_to_all | solution.py:709
  23.4 101.2 %copy-start.4 = (bf16[4,256,256]{2,1,0:T(8,128)(2,1)S(1)}, bf16[4,256,256]{2,1,0:T(8,128)(2,1)}, u32[]{:S(2)}) copy-start(bf16[4,256,256]{2,1,0:T(8,128)(2,1)} %own_left.1) | copy-start | bytes 1572868
  23.4 101.2 %copy-start.5 = (bf16[4,256,256]{2,1,0:T(8,128)(2,1)S(1)}, bf16[4,256,256]{2,1,0:T(8,128)(2,1)}, u32[]{:S(2)}) copy-start(bf16[4,256,256]{2,1,0:T(8,128)(2,1)} %own_right.1) | copy-start | bytes 1572868
  23.4 101.2 %copy-start.6 = (s32[4]{0:T(128)S(1)}, s32[4]{0:T(128)}, u32[]{:S(2)}) copy-start(s32[4]{0:T(128)} %own_places.1) | copy-start | bytes 52
  114.6 106.1 %all-to-all-start.1 = ((bf16[32,512,256]{2,1,0:T(8,128)(2,1)}), bf16[32,512,256]{2,1,0:T(8,128)(2,1)}, u32[]{:S(2)}, u32[]{:S(2)}) async-start(bf16[32,512,256]{2,1,0:T(8,128)(2,1)} %shard_map.129), calls=%async_computation.1 | async-start | bytes 16777216 | tf_op jit(solution)/shard_map/all_to_all | solution.py:709
  124.6 96.0 %copy-start.3 = (f32[1,3,2,256,256]{4,3,2,1,0:T(8,128)S(1)}, f32[1,3,2,256,256]{4,3,2,1,0:T(8,128)}, u32[]{:S(2)}) copy-start(f32[1,3,2,256,256]{4,3,2,1,0:T(8,128)} %param.24) | copy-start | bytes 4718596
  232.2 4.3 %collective-permute-start.1 = (s16[400,512]{1,0:T(8,128)(2,1)S(1)}, s16[400,512]{1,0:T(8,128)(2,1)S(1)}, u32[]{:S(2)}, u32[]{:S(2)}) collective-permute-start(s16[400,512]{1,0:T(8,128)(2,1)S(1)} %get-tuple-element.15), channel_id=1, source_target_pairs={{0,3},{4,7},{8,11},{12,15},{16,19},{20,23},{24,27},{28,31},{32,35}... | collective-permute-start | bytes 1228808 | tf_op jit(solution)/shard_map/ppermute | solution.py:675
  232.8 4.4 %collective-permute-start.5 = (s16[272,768]{1,0:T(8,128)(2,1)S(1)}, s16[272,768]{1,0:T(8,128)(2,1)S(1)}, u32[]{:S(2)}, u32[]{:S(2)}) collective-permute-start(s16[272,768]{1,0:T(8,128)(2,1)S(1)} %get-tuple-element.17), channel_id=1, source_target_pairs={{0,12},{1,13},{2,14},{3,15},{16,28},{17,29},{18,30},{19,31},{32,44... | collective-permute-start | bytes 1253384 | tf_op jit(solution)/shard_map/ppermute | solution.py:675
  233.5 37.0 %copy-start.2 = (f32[2,768,768]{2,1,0:T(8,128)S(1)}, f32[2,768,768]{2,1,0:T(8,128)}, u32[]{:S(2)}) copy-start(f32[2,768,768]{2,1,0:T(8,128)} %copy-done.1) | copy-start | bytes 14155780
  233.6 16.0 %collective-permute-start.4 = (s16[272,768]{1,0:T(8,128)(2,1)S(1)}, s16[272,768]{1,0:T(8,128)(2,1)S(1)}, u32[]{:S(2)}, u32[]{:S(2)}) collective-permute-start(s16[272,768]{1,0:T(8,128)(2,1)S(1)} %get-tuple-element.16), channel_id=1, source_target_pairs={{0,4},{1,5},{2,6},{3,7},{16,20},{17,21},{18,22},{19,23},{32,36},{3... | collective-permute-start | bytes 1253384 | tf_op jit(solution)/shard_map/ppermute | solution.py:674
  235.1 16.8 %collective-permute-start = (s16[400,512]{1,0:T(8,128)(2,1)S(1)}, s16[400,512]{1,0:T(8,128)(2,1)S(1)}, u32[]{:S(2)}, u32[]{:S(2)}) collective-permute-start(s16[400,512]{1,0:T(8,128)(2,1)S(1)} %get-tuple-element.14), channel_id=1, source_target_pairs={{0,1},{4,5},{8,9},{12,13},{16,17},{20,21},{24,25},{28,29},{32,33},... | collective-permute-start | bytes 1228808 | tf_op jit(solution)/shard_map/ppermute | solution.py:674
  236.5 17.6 %collective-permute-start.3 = (s16[400,512]{1,0:T(8,128)(2,1)S(1)}, s16[400,512]{1,0:T(8,128)(2,1)S(1)}, u32[]{:S(2)}, u32[]{:S(2)}) collective-permute-start(s16[400,512]{1,0:T(8,128)(2,1)S(1)} %broadcast_select_fusion.2), channel_id=1, source_target_pairs={{0,3},{3,2},{4,7},{7,6},{8,11},{11,10},{12,15},{15,14},{16,19},{19... | collective-permute-start | bytes 1228808 | tf_op jit(solution)/shard_map/ppermute | solution.py:677
  237.4 33.2 %collective-permute-start.7 = (s16[272,768]{1,0:T(8,128)(2,1)S(1)}, s16[272,768]{1,0:T(8,128)(2,1)S(1)}, u32[]{:S(2)}, u32[]{:S(2)}) collective-permute-start(s16[272,768]{1,0:T(8,128)(2,1)S(1)} %broadcast_select_fusion), channel_id=1, source_target_pairs={{0,12},{12,8},{1,13},{13,9},{2,14},{14,10},{3,15},{15,11},{16,28},... | collective-permute-start | bytes 1253384 | tf_op jit(solution)/shard_map/ppermute | solution.py:677
  249.7 69.0 %copy-start.7 = (s32[64]{0:T(128)S(1)}, s32[64]{0:T(128)}, u32[]{:S(2)}) copy-start(s32[64]{0:T(128)} %constant.11.clone.source) | copy-start | bytes 772
  249.7 20.8 %collective-permute-start.6 = (s16[272,768]{1,0:T(8,128)(2,1)S(1)}, s16[272,768]{1,0:T(8,128)(2,1)S(1)}, u32[]{:S(2)}, u32[]{:S(2)}) collective-permute-start(s16[272,768]{1,0:T(8,128)(2,1)S(1)} %broadcast_select_fusion.1), channel_id=1, source_target_pairs={{0,4},{4,8},{1,5},{5,9},{2,6},{6,10},{3,7},{7,11},{16,20},{20,24},... | collective-permute-start | bytes 1253384 | tf_op jit(solution)/shard_map/ppermute | solution.py:676
  252.0 18.5 %collective-permute-start.2 = (s16[400,512]{1,0:T(8,128)(2,1)S(1)}, s16[400,512]{1,0:T(8,128)(2,1)S(1)}, u32[]{:S(2)}, u32[]{:S(2)}) collective-permute-start(s16[400,512]{1,0:T(8,128)(2,1)S(1)} %broadcast_select_fusion.3), channel_id=1, source_target_pairs={{0,1},{1,2},{4,5},{5,6},{8,9},{9,10},{12,13},{13,14},{16,17},{17,1... | collective-permute-start | bytes 1228808 | tf_op jit(solution)/shard_map/ppermute | solution.py:676
  276.2 23.0 %collective-permute-start.8 = (s16[400,1024]{1,0:T(8,128)(2,1)S(1)}, s16[400,1024]{1,0:T(8,128)(2,1)S(1)}, u32[]{:S(2)}, u32[]{:S(2)}) collective-permute-start(s16[400,1024]{1,0:T(8,128)(2,1)S(1)} %get-tuple-element.19), channel_id=1, source_target_pairs={{4,5},{8,9},{12,15},{1,13},{2,6},{3,7},{20,21},{24,25},{28,31},{17... | collective-permute-start | bytes 2457608 | tf_op jit(solution)/shard_map/ppermute | solution.py:637
  277.5 24.0 %collective-permute-start.9 = (s16[400,1024]{1,0:T(8,128)(2,1)S(1)}, s16[400,1024]{1,0:T(8,128)(2,1)S(1)}, u32[]{:S(2)}, u32[]{:S(2)}) collective-permute-start(s16[400,1024]{1,0:T(8,128)(2,1)S(1)} %get-tuple-element.20), channel_id=1, source_target_pairs={{4,7},{8,11},{12,13},{1,5},{2,14},{3,15},{20,23},{24,27},{28,29},{... | collective-permute-start | bytes 2457608 | tf_op jit(solution)/shard_map/ppermute | solution.py:637
  278.8 36.8 %collective-permute-start.10 = (s16[400,1024]{1,0:T(8,128)(2,1)S(1)}, s16[400,1024]{1,0:T(8,128)(2,1)S(1)}, u32[]{:S(2)}, u32[]{:S(2)}) collective-permute-start(s16[400,1024]{1,0:T(8,128)(2,1)S(1)} %get-tuple-element.20), channel_id=1, source_target_pairs={{4,5},{8,9},{12,15},{1,13},{2,6},{3,7},{20,21},{24,25},{28,31},{17... | collective-permute-start | bytes 2457608 | tf_op jit(solution)/shard_map/ppermute | solution.py:637
  280.1 37.5 %collective-permute-start.11 = (s16[400,1024]{1,0:T(8,128)(2,1)S(1)}, s16[400,1024]{1,0:T(8,128)(2,1)S(1)}, u32[]{:S(2)}, u32[]{:S(2)}) collective-permute-start(s16[400,1024]{1,0:T(8,128)(2,1)S(1)} %get-tuple-element.19), channel_id=1, source_target_pairs={{4,7},{8,11},{12,13},{1,5},{2,14},{3,15},{20,23},{24,27},{28,29},{... | collective-permute-start | bytes 2457608 | tf_op jit(solution)/shard_map/ppermute | solution.py:637
  299.2 18.3 %collective-permute-start.12 = (s16[400,1024]{1,0:T(8,128)(2,1)S(1)}, s16[400,1024]{1,0:T(8,128)(2,1)S(1)}, u32[]{:S(2)}, u32[]{:S(2)}) collective-permute-start(s16[400,1024]{1,0:T(8,128)(2,1)S(1)} %collective-permute-done.8.refs_0_), channel_id=1, source_target_pairs={{5,6},{9,10},{15,14},{13,9},{7,11},{21,22},{25,26},{31,30},{29,25}... | collective-permute-start | bytes 2457608 | tf_op jit(solution)/shard_map/ppermute | solution.py:637
  300.7 18.0 %collective-permute-start.14 = (s16[400,1024]{1,0:T(8,128)(2,1)S(1)}, s16[400,1024]{1,0:T(8,128)(2,1)S(1)}, u32[]{:S(2)}, u32[]{:S(2)}) collective-permute-start(s16[400,1024]{1,0:T(8,128)(2,1)S(1)} %collective-permute-done.8.refs_0_), channel_id=1, source_target_pairs={{6,10},{22,26},{38,42},{54,58},{70,74},{86,90},{102,106},{118,122}} | collective-permute-start | bytes 2457608 | tf_op jit(solution)/shard_map/ppermute | solution.py:637
  301.5 17.3 %collective-permute-start.13 = (s16[400,1024]{1,0:T(8,128)(2,1)S(1)}, s16[400,1024]{1,0:T(8,128)(2,1)S(1)}, u32[]{:S(2)}, u32[]{:S(2)}) collective-permute-start(s16[400,1024]{1,0:T(8,128)(2,1)S(1)} %collective-permute-done.9.refs_1_), channel_id=1, source_target_pairs={{7,6},{11,10},{13,14},{5,9},{15,11},{23,22},{27,26},{29,30},{21,25... | collective-permute-start | bytes 2457608 | tf_op jit(solution)/shard_map/ppermute | solution.py:637
  315.6 3.2 collective-permute-start.15
  (2 other events, 4.4 us)

commit v6 on v5

--- a/solution.py
+++ b/solution.py
@@ -314,10 +314,10 @@
 def second_kernel(places, role, before, slots, inverse, out, *refs):
     along_row, along_col = refs[:HALVES], refs[HALVES : 2 * HALVES]
 
-    def prepare():
-        out[...] = before[...]
-
-    add_slots(out, places, slots, refs[2 * HALVES :], prepare)
+    sem, *scratch = refs[2 * HALVES :]
+    fetch = pltpu.make_async_copy(before, out, sem)
+    fetch.start()
+    add_slots(out, places, slots, scratch, fetch.wait)
 
     @pl.when((role[0] == 0) & (role[1] == 0))
     def _():
@@ -395,10 +395,10 @@
 def add_second(places, role, before, slots, inverse):
     return pl.pallas_call(
         second_kernel,
-        in_specs=[SCALAR, SCALAR, HELD, IN_HBM, HELD],
+        in_specs=[SCALAR, SCALAR, IN_HBM, IN_HBM, HELD],
         out_specs=[HELD] * (1 + 2 * HALVES),
         out_shape=[jax.ShapeDtypeStruct(before.shape, F32)] + pieces_of(1),
-        scratch_shapes=add_scratch(),
+        scratch_shapes=[pltpu.SemaphoreType.DMA] + add_scratch(),
         compiler_params=pltpu.CompilerParams(vmem_limit_bytes=MORE_VMEM_BYTES),
         cost_estimate=ADD_COST,
     )(places, role, before, slots, inverse)

time: 332 us -> 331 us (level)
  transfers between devices with their start and end apart: 18 -> 18, of which waited for: 9 -> 10; matrix products, arithmetic and copies ran while one was open for 0% -> 0% of each run, Pallas kernels for 5% -> 5%
where the time goes in v6:
time: 331 us; the launch traced here: 328 us
  waiting for transfers between devices  237 us (72%)
  Pallas kernels  46.4 us (14%)
  starting transfers between devices  37.8 us (11%)
  local copies, waits for them, and re-layouts  4.5 us (1%)
    all_to_all x2, waiting for transfers between devices, sent(): lax.all_to_all(slots, joined, split_axis=0, concat_axis=0, tiled=True)  179 us
    ppermute x8, waiting for transfers between devices, move(): return lax.ppermute(array, ('row', 'col'), pairs)  32.2 us
    all_to_all x2, starting transfers between devices, sent(): lax.all_to_all(slots, joined, split_axis=0, concat_axis=0, tiled=True)  17.3 us
    ppermute x2, waiting for transfers between devices, broadcast(): lax.ppermute(jnp.where(first, halves[1], one), axis, [(0, 1), (1, 2)])  14.7 us
    pallas_call x2, Pallas kernels, pack(): pl.pallas_call(functools.partial(pack_kernel, second), in_specs=[SCALAR]...  14.3 us
    pallas_call x1, Pallas kernels, trail(): pl.pallas_call(trail_kernel, in_specs=[SCALAR] * 2 + [HELD] * (1 + MOVES)...  11.8 us
    ppermute x2, waiting for transfers between devices, broadcast(): one = lax.ppermute(halves[0], axis, [(0, 1)])  11.1 us
    ppermute x8, starting transfers between devices, move(): return lax.ppermute(array, ('row', 'col'), pairs)  10.1 us
  transfers between devices with their start and end apart: 18, of which 10 were waited for; matrix products, arithmetic and copies ran while one was open for 0% of the time, Pallas kernels for 5%

profile of v6, /device:TPU:34, one launch (start us, length us, event | category | flops | bytes accessed | tf_op | source)
XLA Modules:
  0.0 327.5 jit_solution(656900697124935108)
XLA Ops:
  0.0 4.9 %shard_map.127 = bf16[32,528,256]{2,1,0:T(8,128)(2,1)} custom-call(s32[28]{0:T(128)} %destination.3, s32[28]{0:T(128)} %place.3, s32[28]{0:T(128)} %ranks.3, bf16[28,256,256]{2,1,0:T(8,128)(2,1)} %left.3, bf16[28,256,256]{2,1,0:T(8,128)(2,1)} %right.3, s32[28,256]{1,0:T(8,128)} %rows.3, s32[28,256]{1,0:T(8,128)} %cols.3), custom_call_target="tpu_custom_call" | custom-call | flops 1879048192 | bytes 16777216 | tf_op jit(solution)/shard_map/pallas_call | solution.py:189
  4.9 8.2 %all-to-all-start = ((bf16[32,528,256]{2,1,0:T(8,128)(2,1)}), bf16[32,528,256]{2,1,0:T(8,128)(2,1)}, u32[]{:S(2)}, u32[]{:S(2)}) async-start(bf16[32,528,256]{2,1,0:T(8,128)(2,1)} %shard_map.127), calls=%async_computation | async-start | bytes 17301504 | tf_op jit(solution)/shard_map/all_to_all | solution.py:709
  13.2 9.3 %shard_map.129 = bf16[32,512,256]{2,1,0:T(8,128)(2,1)} custom-call(s32[28]{0:T(128)} %destination.3, s32[28]{0:T(128)} %place.3, s32[28]{0:T(128)} %ranks.3, bf16[28,256,256]{2,1,0:T(8,128)(2,1)} %left.3, bf16[28,256,256]{2,1,0:T(8,128)(2,1)} %right.3, s32[28,256]{1,0:T(8,128)} %rows.3, s32[28,256]{1,0:T(8,128)} %cols.3), custom_call_target="tpu_custom_call" | custom-call | flops 1879048192 | bytes 16777216 | tf_op jit(solution)/shard_map/pallas_call | solution.py:189
  22.6 91.4 %all-to-all-done.slots = bf16[32,528,256]{2,1,0:T(8,128)(2,1)} async-done(((bf16[32,528,256]{2,1,0:T(8,128)(2,1)}), bf16[32,528,256]{2,1,0:T(8,128)(2,1)}, u32[]{:S(2)}, u32[]{:S(2)}) %all-to-all-start) | async-done | bytes 8650784 | tf_op jit(solution)/shard_map/all_to_all | solution.py:709
  114.0 9.0 %all-to-all-start.1 = ((bf16[32,512,256]{2,1,0:T(8,128)(2,1)}), bf16[32,512,256]{2,1,0:T(8,128)(2,1)}, u32[]{:S(2)}, u32[]{:S(2)}) async-start(bf16[32,512,256]{2,1,0:T(8,128)(2,1)} %shard_map.129), calls=%async_computation.1 | async-start | bytes 16777216 | tf_op jit(solution)/shard_map/all_to_all | solution.py:709
  124.1 6.4 %shard_map.128.before = f32[2,768,768]{2,1,0:T(8,128)S(1)} custom-call(s32[32]{0:T(128)S(1)} %get-tuple-element.21.places, s32[4]{0:T(128)S(1)} %copy-done.6, f32[2,768,768]{2,1,0:T(8,128)} %bitcast.11, bf16[4,256,256]{2,1,0:T(8,128)(2,1)S(1)} %copy-done.4, bf16[4,256,256]{2,1,0:T(8,128)(2,1)S(1)} %copy-done.5, bf16[32,528,256]{2,1,0:T(8,128)(2,1)} %all-to-all-done.slots), custom_call_target="tpu_custom_call" | custom-call | flops 2147483648 | bytes 20971520 | tf_op jit(solution)/shard_map/pallas_call | solution.py:368
  130.5 2.2 copy-done
  132.7 87.4 %all-to-all-done.1.slots = bf16[32,512,256]{2,1,0:T(8,128)(2,1)} async-done(((bf16[32,512,256]{2,1,0:T(8,128)(2,1)}), bf16[32,512,256]{2,1,0:T(8,128)(2,1)}, u32[]{:S(2)}, u32[]{:S(2)}) %all-to-all-start.1) | async-done | bytes 8388640 | tf_op jit(solution)/shard_map/all_to_all | solution.py:709
  220.1 8.1 %shard_map.130 = (f32[2,768,768]{2,1,0:T(8,128)S(1)}, s16[400,512]{1,0:T(8,128)(2,1)S(1)}, s16[400,512]{1,0:T(8,128)(2,1)S(1)}, s16[272,768]{1,0:T(8,128)(2,1)S(1)}, s16[272,768]{1,0:T(8,128)(2,1)S(1)}) custom-call(s32[32]{0:T(128)S(1)} %get-tuple-element.22.places, s32[2]{0:T(128)S(1)} %pad_add_fusion.role, f32[2,768,768]{2,1,0:T(8,128)} %copy-done, ...), custom_call_target="tpu_custom_call" | custom-call | flops 2147483648 | bytes 20971520 | tf_op jit(solution)/shard_map/pallas_call | solution.py:396
  228.2 2.2 copy-done.1
  231.8 1.6 collective-permute-start.4
  236.3 8.8 %collective-permute-done.4.refs_4_ = s16[272,768]{1,0:T(8,128)(2,1)S(1)} collective-permute-done((s16[272,768]{1,0:T(8,128)(2,1)S(1)}, s16[272,768]{1,0:T(8,128)(2,1)S(1)}, u32[]{:S(2)}, u32[]{:S(2)}) %collective-permute-start.4) | collective-permute-done | bytes 417824 | tf_op jit(solution)/shard_map/ppermute | solution.py:674
  245.2 1.9 collective-permute-start.6
  247.1 2.4 collective-permute-done.refs_0_
  249.6 3.0 collective-permute-start.2
  252.6 14.7 %collective-permute-done.2.refs_2_ = s16[400,512]{1,0:T(8,128)(2,1)S(1)} collective-permute-done((s16[400,512]{1,0:T(8,128)(2,1)S(1)}, s16[400,512]{1,0:T(8,128)(2,1)S(1)}, u32[]{:S(2)}, u32[]{:S(2)}) %collective-permute-start.2) | collective-permute-done | bytes 409632 | tf_op jit(solution)/shard_map/ppermute | solution.py:676
  267.3 5.8 %shard_map.131 = (f32[2,768,768]{2,1,0:T(8,128)S(1)}, s16[400,1024]{1,0:T(8,128)(2,1)S(1)}, s16[400,1024]{1,0:T(8,128)(2,1)S(1)}) custom-call(s32[2]{0:T(128)S(1)} %pad_add_fusion.role, f32[2,768,768]{2,1,0:T(8,128)S(1)} %copy-done.2, s16[400,512]{1,0:T(8,128)(2,1)S(1)} %collective-permute-done.refs_0_, s16[400,512]{1,0:T(8,128)(2,1)S(1)} %collective-permute-done.1.refs_1_, ...), custom_call_target="tpu_custom_call" | custom-call | tf_op jit(solution)/shard_map/pallas_call | solution.py:532
  273.1 1.3 collective-permute-start.8
  278.3 17.9 %collective-permute-done.8.refs_0_ = s16[400,1024]{1,0:T(8,128)(2,1)S(1)} collective-permute-done((s16[400,1024]{1,0:T(8,128)(2,1)S(1)}, s16[400,1024]{1,0:T(8,128)(2,1)S(1)}, u32[]{:S(2)}, u32[]{:S(2)}) %collective-permute-start.8) | collective-permute-done | bytes 819232 | tf_op jit(solution)/shard_map/ppermute | solution.py:637
  296.2 1.3 collective-permute-start.12
  298.3 2.2 collective-permute-start.13
  300.5 10.8 %collective-permute-done.10.refs_2_ = s16[400,1024]{1,0:T(8,128)(2,1)S(1)} collective-permute-done((s16[400,1024]{1,0:T(8,128)(2,1)S(1)}, s16[400,1024]{1,0:T(8,128)(2,1)S(1)}, u32[]{:S(2)}, u32[]{:S(2)}) %collective-permute-start.10) | collective-permute-done | bytes 819232 | tf_op jit(solution)/shard_map/ppermute | solution.py:637
  313.5 2.1 collective-permute-done.13.refs_5_
  315.6 11.8 %shard_map.132 = f32[2,768,768]{2,1,0:T(8,128)} custom-call(s32[2]{0:T(128)S(1)} %pad_add_fusion.role, s32[64]{0:T(128)S(1)} %copy-done.7, f32[2,768,768]{2,1,0:T(8,128)S(1)} %get-tuple-element.18.block, s16[400,1024]{1,0:T(8,128)(2,1)S(1)} %collective-permute-done.8.refs_0_, s16[400,1024]{1,0:T(8,128)(2,1)S(1)} %collective-permute-done.9.refs_1_, ...), custom_call_target="tpu_custom_call" | custom-call | tf_op jit(solution)/shard_map/pallas_call | solution.py:602
  (42 shorter events, 12.3 us)
Async XLA Ops:
  4.9 109.1 %all-to-all-start = ((bf16[32,528,256]{2,1,0:T(8,128)(2,1)}), bf16[32,528,256]{2,1,0:T(8,128)(2,1)}, u32[]{:S(2)}, u32[]{:S(2)}) async-start(bf16[32,528,256]{2,1,0:T(8,128)(2,1)} %shard_map.127), calls=%async_computation | async-start | bytes 17301504 | tf_op jit(solution)/shard_map/all_to_all | solution.py:709
  22.5 101.5 %copy-start.4 = (bf16[4,256,256]{2,1,0:T(8,128)(2,1)S(1)}, bf16[4,256,256]{2,1,0:T(8,128)(2,1)}, u32[]{:S(2)}) copy-start(bf16[4,256,256]{2,1,0:T(8,128)(2,1)} %own_left.1) | copy-start | bytes 1572868
  22.5 101.5 %copy-start.5 = (bf16[4,256,256]{2,1,0:T(8,128)(2,1)S(1)}, bf16[4,256,256]{2,1,0:T(8,128)(2,1)}, u32[]{:S(2)}) copy-start(bf16[4,256,256]{2,1,0:T(8,128)(2,1)} %own_right.1) | copy-start | bytes 1572868
  22.5 101.5 %copy-start.6 = (s32[4]{0:T(128)S(1)}, s32[4]{0:T(128)}, u32[]{:S(2)}) copy-start(s32[4]{0:T(128)} %own_places.1) | copy-start | bytes 52
  114.0 106.1 %all-to-all-start.1 = ((bf16[32,512,256]{2,1,0:T(8,128)(2,1)}), bf16[32,512,256]{2,1,0:T(8,128)(2,1)}, u32[]{:S(2)}, u32[]{:S(2)}) async-start(bf16[32,512,256]{2,1,0:T(8,128)(2,1)} %shard_map.129), calls=%async_computation.1 | async-start | bytes 16777216 | tf_op jit(solution)/shard_map/all_to_all | solution.py:709
  124.1 96.0 %copy-start.3 = (f32[1,3,2,256,256]{4,3,2,1,0:T(8,128)S(1)}, f32[1,3,2,256,256]{4,3,2,1,0:T(8,128)}, u32[]{:S(2)}) copy-start(f32[1,3,2,256,256]{4,3,2,1,0:T(8,128)} %param.24) | copy-start | bytes 4718596
  230.4 4.3 %collective-permute-start.1 = (s16[400,512]{1,0:T(8,128)(2,1)S(1)}, s16[400,512]{1,0:T(8,128)(2,1)S(1)}, u32[]{:S(2)}, u32[]{:S(2)}) collective-permute-start(s16[400,512]{1,0:T(8,128)(2,1)S(1)} %get-tuple-element.15), channel_id=1, source_target_pairs={{0,3},{4,7},{8,11},{12,15},{16,19},{20,23},{24,27},{28,31},{32,35}... | collective-permute-start | bytes 1228808 | tf_op jit(solution)/shard_map/ppermute | solution.py:675
  231.1 4.4 %collective-permute-start.5 = (s16[272,768]{1,0:T(8,128)(2,1)S(1)}, s16[272,768]{1,0:T(8,128)(2,1)S(1)}, u32[]{:S(2)}, u32[]{:S(2)}) collective-permute-start(s16[272,768]{1,0:T(8,128)(2,1)S(1)} %get-tuple-element.17), channel_id=1, source_target_pairs={{0,12},{1,13},{2,14},{3,15},{16,28},{17,29},{18,30},{19,31},{32,44... | collective-permute-start | bytes 1253384 | tf_op jit(solution)/shard_map/ppermute | solution.py:675
  231.8 35.5 %copy-start.2 = (f32[2,768,768]{2,1,0:T(8,128)S(1)}, f32[2,768,768]{2,1,0:T(8,128)}, u32[]{:S(2)}) copy-start(f32[2,768,768]{2,1,0:T(8,128)} %copy-done.1) | copy-start | bytes 14155780
  231.8 13.2 %collective-permute-start.4 = (s16[272,768]{1,0:T(8,128)(2,1)S(1)}, s16[272,768]{1,0:T(8,128)(2,1)S(1)}, u32[]{:S(2)}, u32[]{:S(2)}) collective-permute-start(s16[272,768]{1,0:T(8,128)(2,1)S(1)} %get-tuple-element.16), channel_id=1, source_target_pairs={{0,4},{1,5},{2,6},{3,7},{16,20},{17,21},{18,22},{19,23},{32,36},{3... | collective-permute-start | bytes 1253384 | tf_op jit(solution)/shard_map/ppermute | solution.py:674
  233.4 16.1 %collective-permute-start = (s16[400,512]{1,0:T(8,128)(2,1)S(1)}, s16[400,512]{1,0:T(8,128)(2,1)S(1)}, u32[]{:S(2)}, u32[]{:S(2)}) collective-permute-start(s16[400,512]{1,0:T(8,128)(2,1)S(1)} %get-tuple-element.14), channel_id=1, source_target_pairs={{0,1},{4,5},{8,9},{12,13},{16,17},{20,21},{24,25},{28,29},{32,33},... | collective-permute-start | bytes 1228808 | tf_op jit(solution)/shard_map/ppermute | solution.py:674
  234.8 17.8 %collective-permute-start.3 = (s16[400,512]{1,0:T(8,128)(2,1)S(1)}, s16[400,512]{1,0:T(8,128)(2,1)S(1)}, u32[]{:S(2)}, u32[]{:S(2)}) collective-permute-start(s16[400,512]{1,0:T(8,128)(2,1)S(1)} %broadcast_select_fusion.2), channel_id=1, source_target_pairs={{0,3},{3,2},{4,7},{7,6},{8,11},{11,10},{12,15},{15,14},{16,19},{19... | collective-permute-start | bytes 1228808 | tf_op jit(solution)/shard_map/ppermute | solution.py:677
  235.6 31.7 %collective-permute-start.7 = (s16[272,768]{1,0:T(8,128)(2,1)S(1)}, s16[272,768]{1,0:T(8,128)(2,1)S(1)}, u32[]{:S(2)}, u32[]{:S(2)}) collective-permute-start(s16[272,768]{1,0:T(8,128)(2,1)S(1)} %broadcast_select_fusion), channel_id=1, source_target_pairs={{0,12},{12,8},{1,13},{13,9},{2,14},{14,10},{3,15},{15,11},{16,28},... | collective-permute-start | bytes 1253384 | tf_op jit(solution)/shard_map/ppermute | solution.py:677
  245.2 70.4 %copy-start.7 = (s32[64]{0:T(128)S(1)}, s32[64]{0:T(128)}, u32[]{:S(2)}) copy-start(s32[64]{0:T(128)} %constant.11.clone.source) | copy-start | bytes 772
  245.2 22.1 %collective-permute-start.6 = (s16[272,768]{1,0:T(8,128)(2,1)S(1)}, s16[272,768]{1,0:T(8,128)(2,1)S(1)}, u32[]{:S(2)}, u32[]{:S(2)}) collective-permute-start(s16[272,768]{1,0:T(8,128)(2,1)S(1)} %broadcast_select_fusion.1), channel_id=1, source_target_pairs={{0,4},{4,8},{1,5},{5,9},{2,6},{6,10},{3,7},{7,11},{16,20},{20,24},... | collective-permute-start | bytes 1253384 | tf_op jit(solution)/shard_map/ppermute | solution.py:676
  249.6 17.7 %collective-permute-start.2 = (s16[400,512]{1,0:T(8,128)(2,1)S(1)}, s16[400,512]{1,0:T(8,128)(2,1)S(1)}, u32[]{:S(2)}, u32[]{:S(2)}) collective-permute-start(s16[400,512]{1,0:T(8,128)(2,1)S(1)} %broadcast_select_fusion.3), channel_id=1, source_target_pairs={{0,1},{1,2},{4,5},{5,6},{8,9},{9,10},{12,13},{13,14},{16,17},{17,1... | collective-permute-start | bytes 1228808 | tf_op jit(solution)/shard_map/ppermute | solution.py:676
  273.1 23.1 %collective-permute-start.8 = (s16[400,1024]{1,0:T(8,128)(2,1)S(1)}, s16[400,1024]{1,0:T(8,128)(2,1)S(1)}, u32[]{:S(2)}, u32[]{:S(2)}) collective-permute-start(s16[400,1024]{1,0:T(8,128)(2,1)S(1)} %get-tuple-element.19), channel_id=1, source_target_pairs={{4,5},{8,9},{12,15},{1,13},{2,6},{3,7},{20,21},{24,25},{28,31},{17... | collective-permute-start | bytes 2457608 | tf_op jit(solution)/shard_map/ppermute | solution.py:637
  274.4 23.8 %collective-permute-start.9 = (s16[400,1024]{1,0:T(8,128)(2,1)S(1)}, s16[400,1024]{1,0:T(8,128)(2,1)S(1)}, u32[]{:S(2)}, u32[]{:S(2)}) collective-permute-start(s16[400,1024]{1,0:T(8,128)(2,1)S(1)} %get-tuple-element.20), channel_id=1, source_target_pairs={{4,7},{8,11},{12,13},{1,5},{2,14},{3,15},{20,23},{24,27},{28,29},{... | collective-permute-start | bytes 2457608 | tf_op jit(solution)/shard_map/ppermute | solution.py:637
  275.7 35.5 %collective-permute-start.10 = (s16[400,1024]{1,0:T(8,128)(2,1)S(1)}, s16[400,1024]{1,0:T(8,128)(2,1)S(1)}, u32[]{:S(2)}, u32[]{:S(2)}) collective-permute-start(s16[400,1024]{1,0:T(8,128)(2,1)S(1)} %get-tuple-element.20), channel_id=1, source_target_pairs={{4,5},{8,9},{12,15},{1,13},{2,6},{3,7},{20,21},{24,25},{28,31},{17... | collective-permute-start | bytes 2457608 | tf_op jit(solution)/shard_map/ppermute | solution.py:637
  277.0 36.0 %collective-permute-start.11 = (s16[400,1024]{1,0:T(8,128)(2,1)S(1)}, s16[400,1024]{1,0:T(8,128)(2,1)S(1)}, u32[]{:S(2)}, u32[]{:S(2)}) collective-permute-start(s16[400,1024]{1,0:T(8,128)(2,1)S(1)} %get-tuple-element.19), channel_id=1, source_target_pairs={{4,7},{8,11},{12,13},{1,5},{2,14},{3,15},{20,23},{24,27},{28,29},{... | collective-permute-start | bytes 2457608 | tf_op jit(solution)/shard_map/ppermute | solution.py:637
  296.2 17.2 %collective-permute-start.12 = (s16[400,1024]{1,0:T(8,128)(2,1)S(1)}, s16[400,1024]{1,0:T(8,128)(2,1)S(1)}, u32[]{:S(2)}, u32[]{:S(2)}) collective-permute-start(s16[400,1024]{1,0:T(8,128)(2,1)S(1)} %collective-permute-done.8.refs_0_), channel_id=1, source_target_pairs={{5,6},{9,10},{15,14},{13,9},{7,11},{21,22},{25,26},{31,30},{29,25}... | collective-permute-start | bytes 2457608 | tf_op jit(solution)/shard_map/ppermute | solution.py:637
  297.6 18.0 %collective-permute-start.14 = (s16[400,1024]{1,0:T(8,128)(2,1)S(1)}, s16[400,1024]{1,0:T(8,128)(2,1)S(1)}, u32[]{:S(2)}, u32[]{:S(2)}) collective-permute-start(s16[400,1024]{1,0:T(8,128)(2,1)S(1)} %collective-permute-done.8.refs_0_), channel_id=1, source_target_pairs={{6,10},{22,26},{38,42},{54,58},{70,74},{86,90},{102,106},{118,122}} | collective-permute-start | bytes 2457608 | tf_op jit(solution)/shard_map/ppermute | solution.py:637
  298.3 17.3 %collective-permute-start.13 = (s16[400,1024]{1,0:T(8,128)(2,1)S(1)}, s16[400,1024]{1,0:T(8,128)(2,1)S(1)}, u32[]{:S(2)}, u32[]{:S(2)}) collective-permute-start(s16[400,1024]{1,0:T(8,128)(2,1)S(1)} %collective-permute-done.9.refs_1_), channel_id=1, source_target_pairs={{7,6},{11,10},{13,14},{5,9},{15,11},{23,22},{27,26},{29,30},{21,25... | collective-permute-start | bytes 2457608 | tf_op jit(solution)/shard_map/ppermute | solution.py:637
  311.3 4.3 %collective-permute-start.15 = (s16[400,1024]{1,0:T(8,128)(2,1)S(1)}, s16[400,1024]{1,0:T(8,128)(2,1)S(1)}, u32[]{:S(2)}, u32[]{:S(2)}) collective-permute-start(s16[400,1024]{1,0:T(8,128)(2,1)S(1)} %collective-permute-done.9.refs_1_), channel_id=1, source_target_pairs={{14,10},{30,26},{46,42},{62,58},{78,74},{94,90},{110,106},{126,122}} | collective-permute-start | bytes 2457608 | tf_op jit(solution)/shard_map/ppermute | solution.py:637
  (2 other events, 4.4 us)
